TPU v7x, 32 devices: a whole 2x2x4 slice. The times are simulated.
32 devices in a mesh: grp: 4 (over y, core), dev: 8 (over z, x).
Axes of the slice: x: 2, y: 2, z: 4, core: 2. Of those that a mesh axis runs over, the one named last changes fastest.
Arguments:
- charges: bfloat16 [1024, 16, 128], P(('grp', 'dev')), may hold values from -6 to 6
- leaf_basis: bfloat16 [1024, 128, 64], P(('grp', 'dev')), may hold values from -0.5 to 0.5
- near_blocks: bfloat16 [5120, 128, 128], P(('grp', 'dev')), may hold values from -0.375 to 0.375
- near_target: int32 [5120], P(('grp', 'dev')), may hold values from 0 to 1023, as said below
- near_source: int32 [5120], P(('grp', 'dev')), may hold values from 0 to 1023, as said below
- near_count: int32 [32], P(('grp', 'dev')), may hold values from 40 to 160, as said below
- leaf_far: int32 [1024, 16], P(('grp', 'dev')), may hold values from 0 to 1023, as said below
- leaf_far_couple: int32 [1024, 16], P(('grp', 'dev')), may hold values from 0 to 315
- leaf_trans: int32 [1024], P(('grp', 'dev')), may hold values from 0 to 7
- dev_trans: int32 [32], P(('grp', 'dev')), may hold values from 0 to 7
- dev_list: int32 [32, 4], P(('grp', 'dev')), may hold values from 0 to 31, as said below
- dev_couple: int32 [32, 4], P(('grp', 'dev')), may hold values from 0 to 315
- grp_couple: int32 [4, 4], replicated, may hold values from 0 to 315
- trans_leaf: float32 [8, 64, 64], replicated, may hold values from -0.375 to 0.375
- trans_dev: float32 [8, 64, 64], replicated, may hold values from -0.25 to 0.25
- couple_table: float32 [316, 64, 64], replicated, may hold values from -0.375 to 0.375
Outputs:
- potentials: float32 [1024, 16, 128], P(('grp', 'dev'))
Inputs may be any that keep to these rules, and one draw needn't show every extreme that they name: `near_count`: live slots of a device are at least a quarter of its 160; some device has all slots live and some device exactly 40. `near_target`: slot s names a leaf of device s // 160. `near_source`: slot s names a leaf within 16 leaves of device s // 160's range of leaves; on every device both ends of that window are named where they exist. `leaf_far`: leaf b names leaves within 16 leaves of the range of its device; on every device both ends of that window are named where they exist. `dev_list`: box d names boxes of its own subtree, never itself nor the two next to it in cyclic order within the subtree.
All inputs are finite; a program needn't handle non-finite values.
Results may differ from a plain program's by a relative error of at most 0.0024.
Values may be sent and summed in bfloat16 or wider, within the bound.
No kernel may reach another device: no remote copies, remote signals or barrier semaphores. Data moves between devices by JAX's collectives and lax.ppermute only.
A program may use at most 128 MiB of HBM per device.

v0:
```python
import jax
import jax.numpy as jnp
from jax import lax
from jax.sharding import PartitionSpec as P

HIGHEST = lax.Precision.HIGHEST


def padded(block, sides, width):
    for axis, dim in sides:
        count = lax.axis_size(axis)
        forward = [(i, i + 1) for i in range(count - 1)]
        backward = [(target, source) for source, target in forward]
        low = lax.ppermute(
            lax.slice_in_dim(block, block.shape[dim] - width, None, axis=dim), axis, forward
        )
        high = lax.ppermute(lax.slice_in_dim(block, 0, width, axis=dim), axis, backward)
        block = jnp.concatenate([low, block, high], axis=dim)
    return block


def near_slots(source_rows, blocks, targets, picks, live, leaf_start, leaves):
    picked = source_rows[picks]
    product = jnp.einsum("sij,srj->sri", blocks, picked, preferred_element_type=jnp.float32)
    local_target = targets - leaf_start
    onehot = ((local_target[None, :] == jnp.arange(leaves)[:, None]) & live[None, :]).astype(
        jnp.float32
    )
    return jnp.einsum("ts,sri->tri", onehot, product, precision=HIGHEST)


def local(
    charges,
    leaf_basis,
    near_blocks,
    near_target,
    near_source,
    near_count,
    leaf_far,
    leaf_far_couple,
    leaf_trans,
    dev_trans,
    dev_list,
    dev_couple,
    grp_couple,
    trans_leaf,
    trans_dev,
    couple_table,
):
    leaves = charges.shape[0]
    margin = leaves // 2
    slot_total = near_blocks.shape[0]
    per_group = lax.axis_size("dev")
    group_index = lax.axis_index("grp")
    box_index = group_index * per_group + lax.axis_index("dev")
    leaf_start = box_index * leaves
    window = padded(charges, ((("grp", "dev"), 0),), margin)
    leaf_moment = jnp.einsum(
        "lrp,lpk->lrk", charges, leaf_basis, preferred_element_type=jnp.float32
    )
    moment_window = padded(leaf_moment, ((("grp", "dev"), 0),), margin)
    child_maps = trans_leaf[leaf_trans]
    box_moment = jnp.einsum("lrk,lkj->rj", leaf_moment, child_maps, precision=HIGHEST)
    moments, kinds = (
        lax.all_gather(box_moment[None], ("grp", "dev"), axis=0, tiled=True),
        lax.all_gather(dev_trans, ("grp", "dev"), axis=0, tiled=True),
    )
    groups = moments.shape[0] // per_group
    up_all = trans_dev[kinds]
    group_moment = jnp.einsum(
        "gdrk,gdkj->grj",
        moments.reshape(groups, per_group, moments.shape[1], moments.shape[2]),
        up_all.reshape(groups, per_group, up_all.shape[1], up_all.shape[2]),
        precision=HIGHEST,
    )
    peers = lax.dynamic_slice_in_dim(moments, group_index * per_group, per_group, 0)
    groups = group_moment.shape[0]
    away = (jnp.arange(groups) != group_index).astype(jnp.float32)
    group_local = jnp.einsum(
        "h,hrk,hkj->rj",
        away,
        group_moment,
        couple_table[grp_couple[group_index]],
        precision=HIGHEST,
    )
    own_up = trans_dev[dev_trans[0]]
    box_local = jnp.einsum("rj,kj->rk", group_local, own_up, precision=HIGHEST)
    listed = peers[dev_list[0] - group_index * per_group]
    box_local = box_local + jnp.einsum(
        "nrk,nkj->rj", listed, couple_table[dev_couple[0]], precision=HIGHEST
    )
    far_moments = moment_window[leaf_far - leaf_start + margin]
    far_terms = jnp.einsum(
        "lfrk,lfkj->lrj", far_moments, couple_table[leaf_far_couple], precision=HIGHEST
    )
    leaf_local = jnp.einsum("rj,lkj->lrk", box_local, child_maps, precision=HIGHEST) + far_terms
    leaf_local = leaf_local.astype(jnp.bfloat16)
    far_part = jnp.einsum(
        "lrk,lpk->lrp", leaf_local, leaf_basis, preferred_element_type=jnp.float32
    )
    live = jnp.arange(slot_total) < near_count[0]
    near_part = near_slots(
        window,
        near_blocks,
        near_target,
        near_source - leaf_start + margin,
        live,
        leaf_start,
        leaves,
    )
    return near_part + far_part


def solution(mesh):
    return jax.shard_map(
        local,
        mesh=mesh,
        in_specs=(
            P(("grp", "dev"), None, None),
            P(("grp", "dev"), None, None),
            P(("grp", "dev"), None, None),
            P(("grp", "dev")),
            P(("grp", "dev")),
            P(("grp", "dev")),
            P(("grp", "dev"), None),
            P(("grp", "dev"), None),
            P(("grp", "dev")),
            P(("grp", "dev")),
            P(("grp", "dev"), None),
            P(("grp", "dev"), None),
            P(),
            P(),
            P(),
            P(),
        ),
        out_specs=P(("grp", "dev"), None, None),
        check_vma=False,
    )
```

profile of v0, /device:TPU:0, one launch (start us, length us, event | category | flops | bytes accessed | tf_op | source)
XLA Modules:
  0.0 213.8 jit_solution(9041478802082083610)
XLA Ops:
  0.0 0.0 copy-start
  0.0 0.0 copy-start.7
  0.0 1.0 copy-done
  1.0 1.3 fusion.26
  2.3 0.8 fusion.23
  3.1 5.5 %collective-permute-start.2 = (f32[16,16,64]{2,1,0:T(8,128)}, f32[16,16,64]{2,1,0:T(8,128)}, u32[]{:S(2)}, u32[]{:S(2)}) collective-permute-start(f32[16,16,64]{2,1,0:T(8,128)} %get-tuple-element.5), channel_id=1, source_target_pairs={{0,1},{1,2},{2,3},{3,4},{4,5},{5,6},{6,7},{7,8},{8,9},{9,10},{10,1... | collective-permute-start | bytes 196616 | tf_op jit(solution)/shard_map/ppermute | solution.py:14
  8.6 1.3 collective-permute-start.3
  9.8 1.5 fusion.24
  11.4 5.2 %collective-permute-start = (bf16[16,16,128]{2,1,0:T(8,128)(2,1)}, bf16[16,16,128]{2,1,0:T(8,128)(2,1)}, u32[]{:S(2)}, u32[]{:S(2)}) collective-permute-start(bf16[16,16,128]{2,1,0:T(8,128)(2,1)} %get-tuple-element.7), channel_id=1, source_target_pairs={{0,1},{1,2},{2,3},{3,4},{4,5},{5,6},{6,7},{7,8},{8,9},{9,10},{10,1... | collective-permute-start | bytes 196616 | tf_op jit(solution)/shard_map/ppermute | solution.py:14
  16.5 1.3 collective-permute-start.1
  18.5 0.5 compare_convert_fusion
  19.0 0.1 dynamic-update-slice
  19.1 42.9 %all-reduce = s32[32]{0:T(128)S(1)} all-reduce(s32[32]{0:T(128)S(1)} %dynamic-update-slice), channel_id=1, replica_groups=mesh['grp'=4,'dev'=8] {'grp','dev'}, use_global_device_ids=true, to_apply=%add | all-reduce | flops 32 | bytes 256
  62.0 0.7 compare_select_fusion.6
  62.7 1.6 gather_fusion.1
  64.2 0.7 convolution_bitcast_fusion.5
  64.9 67.3 %all-gather = f32[512,64]{1,0:T(8,128)S(1)} all-gather(f32[16,64]{1,0:T(8,128)S(1)} %convolution_bitcast_fusion.5), channel_id=2, replica_groups=mesh['grp'=4,'dev'=8] {'grp','dev'}, dimensions={0}, use_global_device_ids=true | all-gather | bytes 135168 | tf_op jit(solution)/shard_map/all_gather | solution.py:65
  132.2 0.6 pad_clamp_fusion.5
  132.8 0.0 copy-done.7
  132.8 0.7 fusion.21
  133.5 0.0 copy-start.8
  133.5 0.0 copy-start.1
  133.5 12.5 %copy.19 = f32[316,64,64]{2,1,0:T(8,128)} copy(f32[316,64,64]{0,2,1:T(8,128)} %param.31) | data formatting | bytes 10354688 | tf_op args[15]
  146.1 0.0 copy-start.3
  146.1 0.0 copy-start.4
  146.1 0.0 copy-done.8
  146.1 0.6 pad_clamp_fusion.3
  146.7 5.1 %gather_fusion.3 = f32[4,64,64]{2,1,0:T(8,128)} fusion(f32[316,64,64]{2,1,0:T(8,128)} %copy.19, s32[1024]{0:T(1024)S(1)} %pad_clamp_fusion.4), kind=kCustom, calls=%fused_computation.3 | custom fusion | bytes 131088 | tf_op jit(solution)/shard_map/gather | solution.py:83
  151.8 4.5 %gather_fusion.5 = f32[4,64,64]{2,1,0:T(8,128)S(1)} fusion(f32[316,64,64]{2,1,0:T(8,128)} %copy.19, s32[1024]{0:T(1024)S(1)} %pad_clamp_fusion.2), kind=kCustom, calls=%fused_computation.5 | custom fusion | bytes 131088 | tf_op jit(solution)/shard_map/gather | solution.py:90
  156.3 0.0 copy-done.1
  156.3 0.7 gather_fusion.2
  157.1 1.2 fusion.7
  158.3 1.1 convolution_bitcast_fusion.4
  159.5 0.1 fusion.10
  159.7 0.7 gather_fusion.4
  160.3 0.2 fusion.9
  160.6 2.5 %convolution_bitcast_fusion.1 = f32[32,16,64]{2,1,0:T(8,128)S(1)} fusion(f32[32,64,64]{2,1,0:T(8,128)S(1)} %gather_fusion.1, f32[16,64,1]{1,0,2:T(8,128)S(1)} %fusion.9), kind=kOutput, calls=%fused_computation.12 | convolution fusion | flops 25165824 | bytes 659456 | tf_op jit(solution)/shard_map/rj,lkj->lrk/dot_general | solution.py:96
  163.1 0.0 copy-done.3
  163.1 0.1 copy.21
  163.2 0.1 reshape.140
  163.3 0.0 copy-done.4
  163.3 0.1 copy.22
  163.4 0.1 reshape.148
  163.5 0.0 copy-start.5
  163.5 0.0 copy-start.6
  163.5 25.0 %gather_fusion.7 = f32[512,64,64]{2,1,0:T(8,128)} fusion(f32[316,64,64]{2,1,0:T(8,128)} %copy.19, s32[1024]{0:T(1024)S(1)} %pad_clamp_fusion), kind=kCustom, calls=%fused_computation.7 | custom fusion | bytes 16779264 | tf_op jit(solution)/shard_map/gather | solution.py:94
  188.5 0.0 copy-done.5
  188.5 0.0 copy-done.6
  189.2 0.0 collective-permute-done.2
  189.2 0.0 collective-permute-done.3
  189.2 1.0 pad_maximum_fusion
  190.3 3.1 %gather_fusion.6 = f32[512,16,64]{2,1,0:T(8,128)} fusion(f32[64,16,64]{2,1,0:T(8,128)S(1)} %pad_maximum_fusion, s32[1024]{0:T(1024)S(1)} %pad_clamp_fusion.1), kind=kCustom, calls=%fused_computation.6 | custom fusion | bytes 4196352 | tf_op jit(solution)/shard_map/gather | solution.py:92
  193.3 0.0 copy-start.2
  193.3 12.0 %fusion.6 = bf16[32,16,64]{2,1,0:T(8,128)(2,1)S(1)} fusion(f32[32,16,64]{2,1,0:T(8,128)S(1)} %convolution_bitcast_fusion.1, f32[32,16,16,64]{3,2,1,0:T(8,128)} %bitcast.79, f32[32,16,64,64]{3,2,1,0:T(8,128)} %bitcast.78), kind=kOutput, calls=%fused_computation.14 | convolution fusion | flops 402718720 | bytes 10682368 | tf_op jit(solution)/shard_map/lfrk,lfkj->lrj/dot_general | solution.py:93
  205.4 0.3 fusion.27
  205.6 0.0 collective-permute-done
  205.6 0.0 collective-permute-done.1
  205.6 0.0 copy-done.2
  205.7 0.9 pad_maximum_fusion.1
  206.6 0.7 gather_fusion
  207.3 4.7 %fusion.25 = f32[160,16,128]{2,1,0:T(8,128)S(1)} fusion(bf16[160,16,128]{2,1,0:T(8,128)(2,1)S(1)} %gather_fusion, bf16[160,128,128]{2,1,0:T(8,128)(2,1)} %param.18), kind=kOutput, calls=%fused_computation.60 | convolution fusion | flops 83886080 | bytes 7208960 | tf_op jit(solution)/shard_map/sij,srj->sri/dot_general | solution.py:24
  212.0 0.9 fusion.3
  212.9 0.9 copy.25
  (14 shorter events, 0.1 us)
Async XLA Ops:
  0.0 1.0 copy-start
  0.0 132.8 %copy-start.7 = (s32[1,4]{1,0:T(1,128)S(1)}, s32[1,4]{1,0:T(1,128)}, u32[]{:S(2)}) copy-start(s32[1,4]{1,0:T(1,128)} %param.27) | copy-start | bytes 52
  3.1 186.2 %collective-permute-start.2 = (f32[16,16,64]{2,1,0:T(8,128)}, f32[16,16,64]{2,1,0:T(8,128)}, u32[]{:S(2)}, u32[]{:S(2)}) collective-permute-start(f32[16,16,64]{2,1,0:T(8,128)} %get-tuple-element.5), channel_id=1, source_target_pairs={{0,1},{1,2},{2,3},{3,4},{4,5},{5,6},{6,7},{7,8},{8,9},{9,10},{10,1... | collective-permute-start | bytes 196616 | tf_op jit(solution)/shard_map/ppermute | solution.py:14
  8.6 180.7 %collective-permute-start.3 = (f32[16,16,64]{2,1,0:T(8,128)}, f32[16,16,64]{2,1,0:T(8,128)}, u32[]{:S(2)}, u32[]{:S(2)}) collective-permute-start(f32[16,16,64]{2,1,0:T(8,128)} %get-tuple-element.6), channel_id=1, source_target_pairs={{1,0},{2,1},{3,2},{4,3},{5,4},{6,5},{7,6},{8,7},{9,8},{10,9},{11,1... | collective-permute-start | bytes 196616 | tf_op jit(solution)/shard_map/ppermute | solution.py:17
  11.4 194.2 %collective-permute-start = (bf16[16,16,128]{2,1,0:T(8,128)(2,1)}, bf16[16,16,128]{2,1,0:T(8,128)(2,1)}, u32[]{:S(2)}, u32[]{:S(2)}) collective-permute-start(bf16[16,16,128]{2,1,0:T(8,128)(2,1)} %get-tuple-element.7), channel_id=1, source_target_pairs={{0,1},{1,2},{2,3},{3,4},{4,5},{5,6},{6,7},{7,8},{8,9},{9,10},{10,1... | collective-permute-start | bytes 196616 | tf_op jit(solution)/shard_map/ppermute | solution.py:14
  16.5 189.1 %collective-permute-start.1 = (bf16[16,16,128]{2,1,0:T(8,128)(2,1)}, bf16[16,16,128]{2,1,0:T(8,128)(2,1)}, u32[]{:S(2)}, u32[]{:S(2)}) collective-permute-start(bf16[16,16,128]{2,1,0:T(8,128)(2,1)} %get-tuple-element.8), channel_id=1, source_target_pairs={{1,0},{2,1},{3,2},{4,3},{5,4},{6,5},{7,6},{8,7},{9,8},{10,9},{11,1... | collective-permute-start | bytes 196616 | tf_op jit(solution)/shard_map/ppermute | solution.py:17
  133.5 12.6 %copy-start.8 = (s32[1,4]{1,0:T(1,128)S(1)}, s32[1,4]{1,0:T(1,128)}, u32[]{:S(2)}) copy-start(s32[1,4]{1,0:T(1,128)} %param.26) | copy-start | bytes 52
  133.5 22.8 %copy-start.1 = (f32[8,64,64]{2,1,0:T(8,128)S(1)}, f32[8,64,64]{2,1,0:T(8,128)}, u32[]{:S(2)}) copy-start(f32[8,64,64]{2,1,0:T(8,128)} %param.30) | copy-start | bytes 393220
  146.1 17.1 %copy-start.3 = (s32[32,16]{0,1:T(8,128)S(1)}, s32[32,16]{0,1:T(8,128)}, u32[]{:S(2)}) copy-start(s32[32,16]{0,1:T(8,128)} %param.22) | copy-start | bytes 6148
  146.1 17.2 %copy-start.4 = (s32[32,16]{0,1:T(8,128)S(1)}, s32[32,16]{0,1:T(8,128)}, u32[]{:S(2)}) copy-start(s32[32,16]{0,1:T(8,128)} %param.23) | copy-start | bytes 6148
  163.5 25.0 %copy-start.5 = (s32[160]{0:T(256)S(1)}, s32[160]{0:T(256)}, u32[]{:S(2)}) copy-start(s32[160]{0:T(256)} %param.20) | copy-start | bytes 1924
  163.5 25.0 %copy-start.6 = (s32[160]{0:T(256)S(1)}, s32[160]{0:T(256)}, u32[]{:S(2)}) copy-start(s32[160]{0:T(256)} %param.19) | copy-start | bytes 1924
  193.3 12.3 %copy-start.2 = (bf16[32,16,128]{2,1,0:T(8,128)(2,1)S(1)}, bf16[32,16,128]{2,1,0:T(8,128)(2,1)}, u32[]{:S(2)}) copy-start(bf16[32,16,128]{2,1,0:T(8,128)(2,1)} %param.16) | copy-start | bytes 393220
where the time goes:
time: 215 us; the launch traced here: 214 us
  blocking collectives  110 us (51%)
  local copies, waits for them, and re-layouts  58.6 us (27%)
  matrix products  25.1 us (12%)
  starting transfers between devices  13.2 us (6%)
  other arithmetic  5.01 us (2%)
    all_gather x1, blocking collectives, local(): lax.all_gather(box_moment[None], ('grp', 'dev'), axis=0, tiled=True)  67.3 us
    unnamed x1, blocking collectives  42.9 us
    gather x1, local copies, waits for them, and re-layouts, local(): couple_table[leaf_far_couple]  25 us
    unnamed x20, local copies, waits for them, and re-layouts  13.7 us
    dot_general x1, matrix products, local(): jnp.einsum('lfrk,lfkj->lrj', far_moments, couple_table[leaf_far_couple],...  12 us
    ppermute x2, starting transfers between devices, padded(): lax.ppermute(lax.slice_in_dim(block, block.shape[dim] - width, None, axis...  10.6 us
    gather x1, local copies, waits for them, and re-layouts, local(): couple_table[grp_couple[group_index]]  5.15 us
    dot_general x1, matrix products, near_slots(): jnp.einsum('sij,srj->sri', blocks, picked, preferred_element_type=jnp.flo...  4.67 us
  transfers between devices with their start and end apart: 4, of which 0 were waited for; matrix products, arithmetic and copies ran while one was open for 36% of the time, Pallas kernels for 0%

commit v1 on v0

v1 whole, which is shorter than its diff:
```python
import functools

import jax
import jax.numpy as jnp
from jax import lax
from jax.experimental import pallas as pl
from jax.experimental.pallas import tpu as pltpu
from jax.sharding import PartitionSpec as P

HIGHEST = lax.Precision.HIGHEST
F32 = jnp.float32
BF16 = jnp.bfloat16
NT = (((1,), (1,)), ((), ()))
AXES = ("grp", "dev")
VMEM = pl.BlockSpec(memory_space=pltpu.VMEM)
SMEM = pl.BlockSpec(memory_space=pltpu.SMEM)
ANY = pl.BlockSpec(memory_space=pl.ANY)
MIB = 2**20


def halves(x):
    half = x.shape[1] // 2
    return jnp.concatenate([x[:, :half], x[:, half:]], axis=0)


def fold(product):
    r, j = product.shape[0] // 2, product.shape[1] // 2
    return product[:r, :j] + product[r:, j:]


def moment_kernel(
    leaf_trans, dev_trans, charges, basis_t, trans_leaf, trans_dev,
    moments, send_first, send_second, sums, classes,
):
    leaves, r, _ = charges.shape
    k = basis_t.shape[1]
    margin = leaves // 2
    kinds = trans_leaf.shape[0]
    even = lax.rem(lax.axis_index("dev"), 2) == 0
    left = lax.broadcasted_iota(jnp.int32, (r, 2 * k), 1) < k
    classes[...] = jnp.zeros_like(classes)
    for leaf in range(leaves):
        basis = basis_t[leaf]
        twice = lax.dot_general(
            charges[leaf], jnp.concatenate([basis, basis], axis=0), NT,
            preferred_element_type=F32,
        )
        kind = leaf_trans[leaf]
        classes[kind] = classes[kind] + twice
        high = twice.astype(BF16).astype(F32)
        moments[leaf] = jnp.where(left, high, twice - high).astype(BF16)
    own = functools.partial(jnp.dot, precision=HIGHEST, preferred_element_type=F32)
    box = jnp.zeros((r, k), F32)
    for pair in range(kinds // 2):
        lhs = jnp.where(left, classes[2 * pair], classes[2 * pair + 1])
        rhs = jnp.concatenate([trans_leaf[2 * pair], trans_leaf[2 * pair + 1]], axis=0)
        box = box + own(lhs, rhs)
    up = own(box, trans_dev[dev_trans[0]])
    both = jnp.concatenate([box, up], axis=0)
    wide = jnp.concatenate([both, jnp.zeros_like(both)], axis=1)
    sums[...] = wide
    high = wide.astype(BF16)
    send_first[margin] = high
    send_first[margin + 1] = (wide - high.astype(F32)).astype(BF16)

    def fill(first_from, second_from):
        for leaf in range(margin):
            send_first[leaf, :r] = charges[first_from + leaf]
            send_first[leaf, r:] = moments[first_from + leaf]
            send_second[leaf, :r] = charges[second_from + leaf]
            send_second[leaf, r:] = moments[second_from + leaf]

    @pl.when(even)
    def _():
        fill(margin, 0)

    @pl.when(jnp.logical_not(even))
    def _():
        fill(0, margin)


def table_kernel(steps, table, out, buffer, sems):
    half, kinds = buffer.shape[1], buffer.shape[3]
    size = half // steps
    copies = [
        pltpu.make_async_copy(
            table.at[:, pl.ds(i * size, size)], buffer.at[:, pl.ds(i * size, size)], sems.at[i]
        )
        for i in range(steps)
    ]
    for copy in copies:
        copy.start()
    for i, copy in enumerate(copies):
        copy.wait()

        def step(row, carry):
            stacked = jnp.concatenate([buffer[0, row], buffer[1, row]], axis=0)
            for start in range(0, kinds, 128):
                width = min(128, kinds - start)
                out[pl.ds(start * half + row, width, stride=half), :] = stacked[
                    :, start : start + width
                ].T
            return carry

        lax.fori_loop(i * size, (i + 1) * size, step, 0, unroll=4)


def near_kernel(
    chunk, unroll, targets, sources, count, charges, first, second, blocks,
    out, window, buffer, total, sems,
):
    slots = blocks.shape[0]
    leaves, r, _ = charges.shape
    margin = leaves // 2
    live = count[0]
    leaf_start = (lax.axis_index("grp") * lax.axis_size("dev") + lax.axis_index("dev")) * leaves
    even = lax.rem(lax.axis_index("dev"), 2) == 0
    copies = [
        pltpu.make_async_copy(
            blocks.at[pl.ds(i * chunk, chunk)], buffer.at[pl.ds(i * chunk, chunk)], sems.at[i]
        )
        for i in range(slots // chunk)
    ]
    for i, copy in enumerate(copies):

        @pl.when(i * chunk < live)
        def _():
            copy.start()

    low_at = jnp.where(even, margin + leaves, 0)
    high_at = jnp.where(even, 0, margin + leaves)
    window[pl.ds(margin, leaves)] = charges[...]
    window[pl.ds(low_at, margin)] = first[:margin, :r]
    window[pl.ds(high_at, margin)] = second[:, :r]
    total[...] = jnp.zeros_like(total)
    for i, copy in enumerate(copies):

        @pl.when(i * chunk < live)
        def _():
            copy.wait()

            def step(group, carry):
                base = i * chunk + group * unroll
                products = [
                    lax.dot_general(
                        window[sources[base + u] - leaf_start + margin], buffer[base + u], NT,
                        preferred_element_type=F32,
                    )
                    for u in range(unroll)
                ]
                for u in range(unroll):
                    slot = base + u
                    row = jnp.where(slot < live, targets[slot] - leaf_start, leaves)
                    total[row] = total[row] + products[u]
                return carry

            here = jnp.minimum(live - i * chunk, chunk)
            lax.fori_loop(0, (here + unroll - 1) // unroll, step, 0)

    out[...] = total[:leaves]


def far_kernel(
    boxes_count, far, far_couple, dev_list, dev_couple, grp_couple, moments, first, second,
    table, *rest,
):
    boxes = rest[:boxes_count]
    out, listed_out, group_tables, window, spread, gathered = rest[boxes_count:]
    leaves, r, width = moments.shape
    margin = leaves // 2
    nfar = far.shape[0]
    half = width // 4
    group = lax.axis_index("grp")
    per_group = lax.axis_size("dev")
    member = lax.axis_index("dev")
    leaf_start = (group * per_group + member) * leaves
    even = lax.rem(member, 2) == 0
    low_at = jnp.where(even, margin + leaves, 0)
    high_at = jnp.where(even, 0, margin + leaves)
    window[pl.ds(margin, leaves)] = moments[...]
    window[pl.ds(low_at, margin)] = first[:margin, r:]
    window[pl.ds(high_at, margin)] = second[:, r:]
    row = lax.broadcasted_iota(jnp.int32, (width, 4 * width), 0)
    column = lax.broadcasted_iota(jnp.int32, (width, 4 * width), 1)
    copier = (row == (column // width) * half + lax.rem(column, half)).astype(BF16)
    piece = 8
    for start in range(0, 2 * leaves, piece):
        rows = window[start : start + piece].reshape(piece * r, width)
        copied = jnp.dot(rows, copier, preferred_element_type=F32).astype(BF16)
        for section in range(4):
            spread[start : start + piece, section * r : (section + 1) * r] = copied[
                :, section * width : (section + 1) * width
            ].reshape(piece, r, width)
    lane = lax.broadcasted_iota(jnp.int32, (4 * r, width), 1) // half

    def couple(kind):
        return table[pl.ds(pl.multiple_of(kind * half, half), half), :]

    def one(leaf):
        lhs, rhs = [], []
        for quad in range(nfar // 4):
            picked = None
            tables = []
            for q in range(4):
                f = quad * 4 + q
                source = spread[far[f, leaf] - leaf_start + margin]
                picked = source if q == 0 else jnp.where(lane >= q, source, picked)
                tables.append(couple(far_couple[f, leaf]))
            stacked = jnp.concatenate(tables, axis=0)
            high = stacked.astype(BF16)
            low = (stacked - high.astype(F32)).astype(BF16)
            lhs.append(picked)
            rhs.append(jnp.concatenate([high, low], axis=1))
        product = jnp.dot(
            jnp.concatenate(lhs, axis=1), jnp.concatenate(rhs, axis=0),
            preferred_element_type=F32,
        )
        product = product[: 2 * r] + product[2 * r :]
        return fold(product[:, :width] + product[:, width:])

    def step(index, carry):
        results = [one(index * 2 + u) for u in range(2)]
        for u in range(2):
            out[index * 2 + u] = results[u]
        return carry

    lax.fori_loop(0, leaves // 2, step, 0)
    for pair in range(boxes_count):
        for e in range(2):
            gathered[2 * pair + e] = boxes[pair][e, :r]
    lhs, rhs = [], []
    for n in range(dev_list.shape[1]):
        place = jnp.bitwise_xor(dev_list[0, n] - group * per_group, member)
        lhs.append(halves(gathered[place][:, : 2 * half]))
        rhs.append(couple(dev_couple[0, n]))
    listed_out[...] = fold(
        jnp.dot(
            jnp.concatenate(lhs, axis=1), jnp.concatenate(rhs, axis=0),
            precision=HIGHEST, preferred_element_type=F32,
        )
    )
    for other in range(1, grp_couple.shape[0]):
        group_tables[other - 1] = couple(grp_couple[group, jnp.bitwise_xor(group, other)])


def final_kernel(
    others, leaf_trans, dev_trans, near, far, listed, group_tables, basis_t, trans_leaf,
    trans_dev, *rest,
):
    groups = rest[:others]
    out, locals_ = rest[others:]
    own = functools.partial(lax.dot_general, precision=HIGHEST, preferred_element_type=F32)
    group_local = None
    for other in range(others):
        term = fold(
            jnp.dot(
                halves(groups[other][...]), group_tables[other],
                precision=HIGHEST, preferred_element_type=F32,
            )
        )
        group_local = term if other == 0 else group_local + term
    box_local = own(group_local, trans_dev[dev_trans[0]], NT) + listed[...]
    for kind in range(trans_leaf.shape[0]):
        locals_[kind] = own(box_local, trans_leaf[kind], NT)
    for leaf in range(near.shape[0]):
        leaf_local = (locals_[leaf_trans[leaf]] + far[leaf]).astype(BF16)
        out[leaf] = near[leaf] + jnp.dot(
            leaf_local, basis_t[leaf], preferred_element_type=F32
        )


def swap(x, axis, distance):
    return lax.ppermute(x, axis, [(i, i ^ distance) for i in range(lax.axis_size(axis))])


def params(mib):
    return pltpu.CompilerParams(vmem_limit_bytes=mib * MIB)


def local(
    charges,
    leaf_basis,
    near_blocks,
    near_target,
    near_source,
    near_count,
    leaf_far,
    leaf_far_couple,
    leaf_trans,
    dev_trans,
    dev_list,
    dev_couple,
    grp_couple,
    trans_leaf,
    trans_dev,
    couple_table,
):
    leaves, r, panels = charges.shape
    k = leaf_basis.shape[2]
    margin = leaves // 2
    slots = near_blocks.shape[0]
    kinds = couple_table.shape[0]
    half = k // 2
    per_group = lax.axis_size("dev")
    devices = per_group * lax.axis_size("grp")
    basis_t = jnp.swapaxes(leaf_basis, 1, 2)
    shape = jax.ShapeDtypeStruct

    moments, send_first, send_second, sums = pl.pallas_call(
        moment_kernel,
        out_shape=(
            shape((leaves, r, 2 * k), BF16),
            shape((margin + 2, 2 * r, panels), BF16),
            shape((margin, 2 * r, panels), BF16),
            shape((2 * r, 2 * k), F32),
        ),
        in_specs=[SMEM, SMEM, VMEM, VMEM, VMEM, VMEM],
        out_specs=(VMEM, VMEM, VMEM, VMEM),
        scratch_shapes=[pltpu.VMEM((trans_leaf.shape[0], r, 2 * k), F32)],
        compiler_params=params(16),
        name="moments",
    )(leaf_trans, dev_trans, charges, basis_t, trans_leaf, trans_dev)

    first = swap(send_first, "dev", 1)
    second = lax.ppermute(
        send_second,
        AXES,
        [(i, i + 1) for i in range(1, devices - 1, 2)]
        + [(i + 1, i) for i in range(1, devices - 1, 2)],
    )

    steps = 4
    table = pl.pallas_call(
        functools.partial(table_kernel, steps),
        out_shape=shape((kinds * half, 2 * k), F32),
        in_specs=[ANY],
        out_specs=VMEM,
        scratch_shapes=[
            pltpu.VMEM((2, half, k, kinds), F32),
            pltpu.SemaphoreType.DMA((steps,)),
        ],
        compiler_params=params(20),
        cost_estimate=pl.CostEstimate(flops=0, bytes_accessed=12 * MIB, transcendentals=0),
        name="table",
    )(jnp.transpose(couple_table, (1, 2, 0)).reshape(2, half, k, kinds))

    peer = first[margin].astype(F32) + first[margin + 1].astype(F32)
    pair = jnp.stack([sums, peer])
    pairs = [pair] + [swap(pair, "dev", distance) for distance in range(2, per_group, 2)]

    chunk = slots // 8
    near = pl.pallas_call(
        functools.partial(near_kernel, chunk, 4),
        out_shape=shape((leaves, r, panels), F32),
        in_specs=[SMEM, SMEM, SMEM, VMEM, VMEM, VMEM, ANY],
        out_specs=VMEM,
        scratch_shapes=[
            pltpu.VMEM((2 * leaves, r, panels), BF16),
            pltpu.VMEM(near_blocks.shape, BF16),
            pltpu.VMEM((leaves + 1, r, panels), F32),
            pltpu.SemaphoreType.DMA((slots // chunk,)),
        ],
        compiler_params=params(16),
        cost_estimate=pl.CostEstimate(flops=0, bytes_accessed=12 * MIB, transcendentals=0),
        name="near",
    )(near_target, near_source, near_count, charges, first, second, near_blocks)

    group_moment = sum(jnp.sum(part[:, r:, :k], axis=0) for part in pairs)
    groups = [
        swap(group_moment, "grp", distance) for distance in range(1, lax.axis_size("grp"))
    ]

    far, listed, group_tables = pl.pallas_call(
        functools.partial(far_kernel, len(pairs)),
        out_shape=(
            shape((leaves, r, k), F32),
            shape((r, k), F32),
            shape((len(groups), half, 2 * k), F32),
        ),
        in_specs=[SMEM] * 5 + [VMEM] * (4 + len(pairs)),
        out_specs=(VMEM, VMEM, VMEM),
        scratch_shapes=[
            pltpu.VMEM((2 * leaves, r, 2 * k), BF16),
            pltpu.VMEM((2 * leaves, 4 * r, 2 * k), BF16),
            pltpu.VMEM((2 * len(pairs), r, 2 * k), F32),
        ],
        compiler_params=params(16),
        cost_estimate=pl.CostEstimate(flops=0, bytes_accessed=12 * MIB, transcendentals=0),
        name="far",
    )(
        leaf_far.T, leaf_far_couple.T, dev_list, dev_couple, grp_couple,
        moments, first, second, table, *pairs,
    )

    return pl.pallas_call(
        functools.partial(final_kernel, len(groups)),
        out_shape=shape((leaves, r, panels), F32),
        in_specs=[SMEM, SMEM] + [VMEM] * (7 + len(groups)),
        out_specs=VMEM,
        scratch_shapes=[pltpu.VMEM((trans_leaf.shape[0], r, k), F32)],
        compiler_params=params(16),
        name="final",
    )(
        leaf_trans, dev_trans, near, far, listed, group_tables, basis_t, trans_leaf,
        trans_dev, *groups,
    )


def solution(mesh):
    leaf = P(AXES)
    return jax.shard_map(
        local,
        mesh=mesh,
        in_specs=(leaf,) * 12 + (P(),) * 4,
        out_specs=leaf,
        check_vma=False,
    )
```

time: 215 us -> 57.1 us (0.27)
  blocking collectives: 110 us -> 0 us
  local copies, waits for them, and re-layouts: 58.6 us -> 7.35 us
  Pallas kernels: 0 us -> 25.7 us
  matrix products: 25.1 us -> 0 us
  waiting for transfers between devices: 0.01 us -> 8.66 us
  other arithmetic: 5.01 us -> 0.04 us
    all_gather x1 -> x0, blocking collectives: 67.3 us -> none  [local(): lax.all_gather(box_moment[None], ('grp', 'dev'), axis=0, tiled=True)]
    unnamed x1 -> x0, blocking collectives: 42.9 us -> none
    gather x8 -> x0, local copies, waits for them, and re-layouts: 41.4 us -> none  [the longest x1 25 us: local(): couple_table[leaf_far_couple]]
    pallas_call x0 -> x5, Pallas kernels: none -> 25.7 us  [the longest x1 8.52 us: local(): pl.pallas_call(functools.partial(near_kernel, chunk, 4), out_shape=shape(...]
    dot_general x11 -> x0, matrix products: 25.1 us -> none  [the longest x1 12 us: local(): jnp.einsum('lfrk,lfkj->lrj', far_moments, couple_table[leaf_far_couple],...]
    ppermute x4 -> x8, waiting for transfers between devices: 0.01 us -> 8.66 us  [the longest x7 8.66 us: swap(): lax.ppermute(x, axis, [(i, i ^ distance) for i in range(lax.axis_size(axi...]
    unnamed x20 -> x38, local copies, waits for them, and re-layouts: 13.7 us -> 7.35 us
    slice x2 -> x0, local copies, waits for them, and re-layouts: 2.3 us -> none  [padded(): lax.slice_in_dim(block, block.shape[dim] - width, None, axis=dim)]
  transfers between devices with their start and end apart: 4 -> 8, of which waited for: 0 -> 2; matrix products, arithmetic and copies ran while one was open for 36% -> 0% of each run, Pallas kernels for 0% -> 37%
where the time goes in v1:
time: 57.1 us; the launch traced here: 57.2 us
  Pallas kernels  25.7 us (45%)
  starting transfers between devices  13.8 us (24%)
  waiting for transfers between devices  8.66 us (15%)
  local copies, waits for them, and re-layouts  7.35 us (13%)
  between operations  1.61 us (3%)
    ppermute x7, starting transfers between devices, swap(): lax.ppermute(x, axis, [(i, i ^ distance) for i in range(lax.axis_size(axi...  13.1 us
    ppermute x7, waiting for transfers between devices, swap(): lax.ppermute(x, axis, [(i, i ^ distance) for i in range(lax.axis_size(axi...  8.66 us
    pallas_call x1, Pallas kernels, local(): pl.pallas_call(functools.partial(near_kernel, chunk, 4), out_shape=shape(...  8.52 us
    unnamed x38, local copies, waits for them, and re-layouts  7.35 us
    pallas_call x1, Pallas kernels, local(): pl.pallas_call(functools.partial(far_kernel, len(pairs)), out_shape=(shap...  6.36 us
    pallas_call x1, Pallas kernels, local(): pl.pallas_call(functools.partial(table_kernel, steps), out_shape=shape((k...  6.18 us
    pallas_call x1, Pallas kernels, local(): pl.pallas_call(functools.partial(final_kernel, len(groups)), out_shape=sh...  2.6 us
    pallas_call x1, Pallas kernels, local(): pl.pallas_call(moment_kernel, out_shape=(shape((leaves, r, 2 * k), BF16),...  2.04 us
  transfers between devices with their start and end apart: 8, of which 2 were waited for; matrix products, arithmetic and copies ran while one was open for 0% of the time, Pallas kernels for 37%

profile of v1, /device:TPU:0, one launch (start us, length us, event | category | flops | bytes accessed | tf_op | source)
XLA Modules:
  0.0 57.2 jit_solution(11355858896687278520)
XLA Ops:
  0.7 0.0 copy-start.2
  0.7 1.0 %copy-done.2 = bf16[32,128,64]{1,2,0:T(8,128)(2,1)S(1)} copy-done((bf16[32,128,64]{1,2,0:T(8,128)(2,1)S(1)}, bf16[32,128,64]{1,2,0:T(8,128)(2,1)}, u32[]{:S(2)}) %copy-start.2) | copy-done | bytes 524312
  1.7 0.0 copy-start.4
  1.7 0.9 %copy-done.4 = f32[8,64,64]{2,1,0:T(8,128)S(1)} copy-done((f32[8,64,64]{2,1,0:T(8,128)S(1)}, f32[8,64,64]{2,1,0:T(8,128)}, u32[]{:S(2)}) %copy-start.4) | copy-done | bytes 131096
  2.6 0.0 copy-start.6
  2.6 0.9 %copy-done.6 = f32[8,64,64]{2,1,0:T(8,128)S(1)} copy-done((f32[8,64,64]{2,1,0:T(8,128)S(1)}, f32[8,64,64]{2,1,0:T(8,128)}, u32[]{:S(2)}) %copy-start.6) | copy-done | bytes 131096
  3.6 0.0 copy-start.8
  3.6 0.9 %copy-done.8 = bf16[32,16,128]{2,1,0:T(8,128)(2,1)S(1)} copy-done((bf16[32,16,128]{2,1,0:T(8,128)(2,1)S(1)}, bf16[32,16,128]{2,1,0:T(8,128)(2,1)}, u32[]{:S(2)}) %copy-start.8) | copy-done | bytes 131096
  4.5 0.0 copy-start.13
  4.5 0.7 %copy-done.13 = s32[32]{0:T(128)S(1)} copy-done((s32[32]{0:T(128)S(1)}, s32[32]{0:T(128)}, u32[]{:S(2)}) %copy-start.13) | copy-done | bytes 152
  5.2 2.0 %moments.1 = (bf16[32,16,128]{2,1,0:T(8,128)(2,1)S(1)}, bf16[18,32,128]{2,1,0:T(8,128)(2,1)S(1)}, bf16[16,32,128]{2,1,0:T(8,128)(2,1)S(1)}, f32[32,128]{1,0:T(8,128)S(1)}) custom-call(s32[32]{0:T(128)S(1)} %copy-done.13, s32[1]{0:T(128)S(6)} %copy.18.dev_trans, bf16[32,16,128]{2,1,0:T(8,128)(2,1)S(1)} %copy-done.8, bf16[32,64,128]{2,1,0:T(8,128)(2,1)S(1)} %bitcast.8, ...), custom_call_target="tpu_custom_call" | custom-call | tf_op jit(solution)/shard_map/moments/pallas_call | solution.py:309
  7.2 3.0 %collective-permute-start = (bf16[18,32,128]{2,1,0:T(8,128)(2,1)S(1)}, bf16[18,32,128]{2,1,0:T(8,128)(2,1)S(1)}, u32[]{:S(2)}, u32[]{:S(2)}) collective-permute-start(bf16[18,32,128]{2,1,0:T(8,128)(2,1)S(1)} %get-tuple-element.12), channel_id=1, source_target_pairs={{0,1},{1,0},{2,3},{3,2},{4,5},{5,4},{6,7},{7,6},{8,9},{9,8},{10,11... | collective-permute-start | bytes 442376 | tf_op jit(solution)/shard_map/ppermute | solution.py:273
  10.2 3.8 %collective-permute-done.first = bf16[18,32,128]{2,1,0:T(8,128)(2,1)S(1)} collective-permute-done((bf16[18,32,128]{2,1,0:T(8,128)(2,1)S(1)}, bf16[18,32,128]{2,1,0:T(8,128)(2,1)S(1)}, u32[]{:S(2)}, u32[]{:S(2)}) %collective-permute-start) | collective-permute-done | bytes 147488 | tf_op jit(solution)/shard_map/ppermute | solution.py:273
  14.1 3.8 %collective-permute-start.4 = (f32[2,32,128]{2,1,0:T(8,128)S(1)}, f32[2,32,128]{2,1,0:T(8,128)S(1)}, u32[]{:S(2)}, u32[]{:S(2)}) collective-permute-start(f32[2,32,128]{2,1,0:T(8,128)S(1)} %pad_maximum_fusion.rest_0_), channel_id=1, source_target_pairs={{0,6},{1,7},{2,4},{3,5},{4,2},{5,3},{6,0},{7,1},{8,14},{9,15},{10,... | collective-permute-start | bytes 98312 | tf_op jit(solution)/shard_map/ppermute | solution.py:273
  17.9 0.7 %collective-permute-start.1 = (bf16[16,32,128]{2,1,0:T(8,128)(2,1)S(1)}, bf16[16,32,128]{2,1,0:T(8,128)(2,1)S(1)}, u32[]{:S(2)}, u32[]{:S(2)}) collective-permute-start(bf16[16,32,128]{2,1,0:T(8,128)(2,1)S(1)} %get-tuple-element.13), channel_id=1, source_target_pairs={{1,2},{3,4},{5,6},{7,8},{9,10},{11,12},{13,14},{15,16},{17,18},{19... | collective-permute-start | bytes 393224 | tf_op jit(solution)/shard_map/ppermute | solution.py:325
  18.6 4.3 %collective-permute-start.2 = (f32[2,32,128]{2,1,0:T(8,128)S(1)}, f32[2,32,128]{2,1,0:T(8,128)S(1)}, u32[]{:S(2)}, u32[]{:S(2)}) collective-permute-start(f32[2,32,128]{2,1,0:T(8,128)S(1)} %pad_maximum_fusion.rest_0_), channel_id=1, source_target_pairs={{0,2},{1,3},{2,0},{3,1},{4,6},{5,7},{6,4},{7,5},{8,10},{9,11},{10,... | collective-permute-start | bytes 98312 | tf_op jit(solution)/shard_map/ppermute | solution.py:273
  22.9 0.0 collective-permute-start.3
  22.9 0.0 collective-permute-done.4.rest_3_
  23.0 4.8 %collective-permute-done.3.rest_2_ = f32[2,32,128]{2,1,0:T(8,128)S(1)} collective-permute-done((f32[2,32,128]{2,1,0:T(8,128)S(1)}, f32[2,32,128]{2,1,0:T(8,128)S(1)}, u32[]{:S(2)}, u32[]{:S(2)}) %collective-permute-start.3) | collective-permute-done | bytes 32800 | tf_op jit(solution)/shard_map/ppermute | solution.py:273
  27.8 0.0 collective-permute-done.2.rest_1_
  27.8 0.1 collective-permute-start.5
  27.9 1.6 %collective-permute-start.6 = (f32[16,64]{1,0:T(8,128)S(1)}, f32[16,64]{1,0:T(8,128)S(1)}, u32[]{:S(2)}, u32[]{:S(2)}) collective-permute-start(f32[16,64]{1,0:T(8,128)S(1)} %add_add_fusion), channel_id=1, source_target_pairs={{0,16},{8,24},{16,0},{24,8},{1,17},{9,25},{17,1},{25,9},{2,18},{10... | collective-permute-start | bytes 12296 | tf_op jit(solution)/shard_map/ppermute | solution.py:273
  29.5 0.3 collective-permute-start.7
  29.7 0.0 copy-start
  29.7 2.8 %copy-done = f32[316,64,64]{0,2,1:T(8,128)S(1)} copy-done((f32[316,64,64]{0,2,1:T(8,128)S(1)}, f32[316,64,64]{0,2,1:T(8,128)}, u32[]{:S(2)}) %copy-start) | copy-done | bytes 5177368
  32.5 0.0 copy-start.1
  32.5 0.0 copy-start.9
  32.5 0.0 copy-start.15
  32.5 0.0 copy-start.16
  32.5 6.2 %table.1 = f32[10112,128]{1,0:T(8,128)S(1)} custom-call(f32[2,32,64,316]{3,2,1,0:T(8,128)S(1)} %bitcast.7), custom_call_target="tpu_custom_call" | custom-call | bytes 12582912 | tf_op jit(solution)/shard_map/table/pallas_call | solution.py:333
  38.7 0.0 copy-start.10
  38.7 0.0 copy-start.11
  38.7 0.0 copy-start.12
  38.8 0.0 copy-start.17
  38.8 0.0 copy-start.18
  39.5 0.0 copy-start.3
  39.5 0.0 copy-start.5
  39.5 0.0 copy-start.7
  39.5 0.0 copy-start.14
  39.5 0.0 collective-permute-done.1.second
  39.5 0.0 copy-done.1
  39.5 0.0 copy-done.9
  39.5 0.0 copy-done.15
  39.5 0.0 copy-done.16
  39.6 8.5 %near.1 = f32[32,16,128]{2,1,0:T(8,128)S(1)} custom-call(s32[160]{0:T(256)S(1)} %copy-done.15, s32[160]{0:T(256)S(1)} %copy-done.16, s32[1]{0:T(128)S(6)} %copy.17.count, bf16[32,16,128]{2,1,0:T(8,128)(2,1)S(1)} %copy-done.9, bf16[18,32,128]{2,1,0:T(8,128)(2,1)S(1)} %collective-permute-done.first, bf16[16,32,128]{2,1,0:T(8,128)(2,1)S(1)} %collective-permute-done.1.second, ...), custom_call_target="tpu_custom_call" | custom-call | bytes 12582912 | tf_op jit(solution)/shard_map/near/pallas_call | solution.py:352
  48.1 0.0 copy-done.10
  48.1 0.0 copy-done.11
  48.1 0.0 copy-done.12
  48.1 0.0 copy-done.17
  48.1 0.0 copy-done.18
  48.1 6.4 %far.1 = (f32[32,16,64]{2,1,0:T(8,128)S(1)}, f32[16,64]{1,0:T(8,128)S(1)}, f32[3,32,128]{2,1,0:T(8,128)S(1)}) custom-call(s32[16,32]{1,0:T(8,128)S(1)} %bitcast.12, s32[16,32]{1,0:T(8,128)S(1)} %bitcast.13, s32[1,4]{1,0:T(1,128)S(1)} %copy-done.17, s32[1,4]{1,0:T(1,128)S(1)} %copy-done.18, s32[4,4]{1,0:T(4,128)S(1)} %copy-done.12, ...), custom_call_target="tpu_custom_call" | custom-call | bytes 12582912 | tf_op jit(solution)/shard_map/far/pallas_call | solution.py:373
  54.5 0.0 collective-permute-done.5.rest_0_
  54.5 0.0 collective-permute-done.6.rest_1_
  54.5 0.0 collective-permute-done.7.rest_2_
  54.5 0.0 copy-done.3
  54.5 0.0 copy-done.5
  54.5 0.0 copy-done.7
  54.5 0.0 copy-done.14
  54.6 2.6 %final.1 = f32[32,16,128]{2,1,0:T(8,128)} custom-call(s32[32]{0:T(128)S(1)} %copy-done.14, s32[1]{0:T(128)S(6)} %copy.18.dev_trans, f32[32,16,128]{2,1,0:T(8,128)S(1)} %near.1, f32[32,16,64]{2,1,0:T(8,128)S(1)} %get-tuple-element.16.far, f32[16,64]{1,0:T(8,128)S(1)} %get-tuple-element.17.listed, f32[3,32,128]{2,1,0:T(8,128)S(1)} %get-tuple-element.18.group_tables, ...), custom_call_target="tpu_custom_call" | custom-call | tf_op jit(solution)/shard_map/final/pallas_call | solution.py:395
  (7 shorter events, 0.0 us)
Async XLA Ops:
  0.7 1.0 %copy-start.2 = (bf16[32,128,64]{1,2,0:T(8,128)(2,1)S(1)}, bf16[32,128,64]{1,2,0:T(8,128)(2,1)}, u32[]{:S(2)}) copy-start(bf16[32,128,64]{1,2,0:T(8,128)(2,1)} %param.17) | copy-start | bytes 1572868
  1.7 0.9 %copy-start.4 = (f32[8,64,64]{2,1,0:T(8,128)S(1)}, f32[8,64,64]{2,1,0:T(8,128)}, u32[]{:S(2)}) copy-start(f32[8,64,64]{2,1,0:T(8,128)} %trans_leaf.3) | copy-start | bytes 393220
  2.6 0.9 %copy-start.6 = (f32[8,64,64]{2,1,0:T(8,128)S(1)}, f32[8,64,64]{2,1,0:T(8,128)}, u32[]{:S(2)}) copy-start(f32[8,64,64]{2,1,0:T(8,128)} %trans_dev.3) | copy-start | bytes 393220
  3.6 0.9 %copy-start.8 = (bf16[32,16,128]{2,1,0:T(8,128)(2,1)S(1)}, bf16[32,16,128]{2,1,0:T(8,128)(2,1)}, u32[]{:S(2)}) copy-start(bf16[32,16,128]{2,1,0:T(8,128)(2,1)} %charges.3) | copy-start | bytes 393220
  4.5 0.7 %copy-start.13 = (s32[32]{0:T(128)S(1)}, s32[32]{0:T(128)}, u32[]{:S(2)}) copy-start(s32[32]{0:T(128)} %leaf_trans.3) | copy-start | bytes 388
  7.2 6.9 %collective-permute-start = (bf16[18,32,128]{2,1,0:T(8,128)(2,1)S(1)}, bf16[18,32,128]{2,1,0:T(8,128)(2,1)S(1)}, u32[]{:S(2)}, u32[]{:S(2)}) collective-permute-start(bf16[18,32,128]{2,1,0:T(8,128)(2,1)S(1)} %get-tuple-element.12), channel_id=1, source_target_pairs={{0,1},{1,0},{2,3},{3,2},{4,5},{5,4},{6,7},{7,6},{8,9},{9,8},{10,11... | collective-permute-start | bytes 442376 | tf_op jit(solution)/shard_map/ppermute | solution.py:273
  14.1 8.9 %collective-permute-start.4 = (f32[2,32,128]{2,1,0:T(8,128)S(1)}, f32[2,32,128]{2,1,0:T(8,128)S(1)}, u32[]{:S(2)}, u32[]{:S(2)}) collective-permute-start(f32[2,32,128]{2,1,0:T(8,128)S(1)} %pad_maximum_fusion.rest_0_), channel_id=1, source_target_pairs={{0,6},{1,7},{2,4},{3,5},{4,2},{5,3},{6,0},{7,1},{8,14},{9,15},{10,... | collective-permute-start | bytes 98312 | tf_op jit(solution)/shard_map/ppermute | solution.py:273
  17.9 21.6 %collective-permute-start.1 = (bf16[16,32,128]{2,1,0:T(8,128)(2,1)S(1)}, bf16[16,32,128]{2,1,0:T(8,128)(2,1)S(1)}, u32[]{:S(2)}, u32[]{:S(2)}) collective-permute-start(bf16[16,32,128]{2,1,0:T(8,128)(2,1)S(1)} %get-tuple-element.13), channel_id=1, source_target_pairs={{1,2},{3,4},{5,6},{7,8},{9,10},{11,12},{13,14},{15,16},{17,18},{19... | collective-permute-start | bytes 393224 | tf_op jit(solution)/shard_map/ppermute | solution.py:325
  18.6 9.2 %collective-permute-start.2 = (f32[2,32,128]{2,1,0:T(8,128)S(1)}, f32[2,32,128]{2,1,0:T(8,128)S(1)}, u32[]{:S(2)}, u32[]{:S(2)}) collective-permute-start(f32[2,32,128]{2,1,0:T(8,128)S(1)} %pad_maximum_fusion.rest_0_), channel_id=1, source_target_pairs={{0,2},{1,3},{2,0},{3,1},{4,6},{5,7},{6,4},{7,5},{8,10},{9,11},{10,... | collective-permute-start | bytes 98312 | tf_op jit(solution)/shard_map/ppermute | solution.py:273
  22.9 4.8 %collective-permute-start.3 = (f32[2,32,128]{2,1,0:T(8,128)S(1)}, f32[2,32,128]{2,1,0:T(8,128)S(1)}, u32[]{:S(2)}, u32[]{:S(2)}) collective-permute-start(f32[2,32,128]{2,1,0:T(8,128)S(1)} %pad_maximum_fusion.rest_0_), channel_id=1, source_target_pairs={{0,4},{1,5},{2,6},{3,7},{4,0},{5,1},{6,2},{7,3},{8,12},{9,13},{10,... | collective-permute-start | bytes 98312 | tf_op jit(solution)/shard_map/ppermute | solution.py:273
  27.8 26.7 %collective-permute-start.5 = (f32[16,64]{1,0:T(8,128)S(1)}, f32[16,64]{1,0:T(8,128)S(1)}, u32[]{:S(2)}, u32[]{:S(2)}) collective-permute-start(f32[16,64]{1,0:T(8,128)S(1)} %add_add_fusion), channel_id=1, source_target_pairs={{0,8},{8,0},{16,24},{24,16},{1,9},{9,1},{17,25},{25,17},{2,10},{10... | collective-permute-start | bytes 12296 | tf_op jit(solution)/shard_map/ppermute | solution.py:273
  27.9 26.6 %collective-permute-start.6 = (f32[16,64]{1,0:T(8,128)S(1)}, f32[16,64]{1,0:T(8,128)S(1)}, u32[]{:S(2)}, u32[]{:S(2)}) collective-permute-start(f32[16,64]{1,0:T(8,128)S(1)} %add_add_fusion), channel_id=1, source_target_pairs={{0,16},{8,24},{16,0},{24,8},{1,17},{9,25},{17,1},{25,9},{2,18},{10... | collective-permute-start | bytes 12296 | tf_op jit(solution)/shard_map/ppermute | solution.py:273
  29.5 25.1 %collective-permute-start.7 = (f32[16,64]{1,0:T(8,128)S(1)}, f32[16,64]{1,0:T(8,128)S(1)}, u32[]{:S(2)}, u32[]{:S(2)}) collective-permute-start(f32[16,64]{1,0:T(8,128)S(1)} %add_add_fusion), channel_id=1, source_target_pairs={{0,24},{8,16},{16,8},{24,0},{1,25},{9,17},{17,9},{25,1},{2,26},{10... | collective-permute-start | bytes 12296 | tf_op jit(solution)/shard_map/ppermute | solution.py:273
  29.7 2.8 %copy-start = (f32[316,64,64]{0,2,1:T(8,128)S(1)}, f32[316,64,64]{0,2,1:T(8,128)}, u32[]{:S(2)}) copy-start(f32[316,64,64]{0,2,1:T(8,128)} %param.31) | copy-start | bytes 15532036
  32.5 7.0 %copy-start.1 = (bf16[160,128,128]{2,1,0:T(8,128)(2,1)S(1)}, bf16[160,128,128]{2,1,0:T(8,128)(2,1)}, u32[]{:S(2)}) copy-start(bf16[160,128,128]{2,1,0:T(8,128)(2,1)} %blocks.1) | copy-start | bytes 15728644
  32.5 7.0 %copy-start.9 = (bf16[32,16,128]{2,1,0:T(8,128)(2,1)S(1)}, bf16[32,16,128]{2,1,0:T(8,128)(2,1)}, u32[]{:S(2)}) copy-start(bf16[32,16,128]{2,1,0:T(8,128)(2,1)} %charges.3) | copy-start | bytes 393220
  32.5 7.0 %copy-start.15 = (s32[160]{0:T(256)S(1)}, s32[160]{0:T(256)}, u32[]{:S(2)}) copy-start(s32[160]{0:T(256)} %targets.1) | copy-start | bytes 1924
  32.5 7.0 %copy-start.16 = (s32[160]{0:T(256)S(1)}, s32[160]{0:T(256)}, u32[]{:S(2)}) copy-start(s32[160]{0:T(256)} %sources.1) | copy-start | bytes 1924
  38.7 9.4 %copy-start.10 = (s32[32,16]{0,1:T(8,128)S(1)}, s32[32,16]{0,1:T(8,128)}, u32[]{:S(2)}) copy-start(s32[32,16]{0,1:T(8,128)} %param.22) | copy-start | bytes 6148
  38.7 9.4 %copy-start.11 = (s32[32,16]{0,1:T(8,128)S(1)}, s32[32,16]{0,1:T(8,128)}, u32[]{:S(2)}) copy-start(s32[32,16]{0,1:T(8,128)} %param.23) | copy-start | bytes 6148
  38.7 9.4 %copy-start.12 = (s32[4,4]{1,0:T(4,128)S(1)}, s32[4,4]{1,0:T(4,128)}, u32[]{:S(2)}) copy-start(s32[4,4]{1,0:T(4,128)} %grp_couple.1) | copy-start | bytes 196
  38.8 9.4 %copy-start.17 = (s32[1,4]{1,0:T(1,128)S(1)}, s32[1,4]{1,0:T(1,128)}, u32[]{:S(2)}) copy-start(s32[1,4]{1,0:T(1,128)} %dev_list.1) | copy-start | bytes 52
  38.8 9.4 %copy-start.18 = (s32[1,4]{1,0:T(1,128)S(1)}, s32[1,4]{1,0:T(1,128)}, u32[]{:S(2)}) copy-start(s32[1,4]{1,0:T(1,128)} %dev_couple.1) | copy-start | bytes 52
  39.5 15.1 %copy-start.3 = (bf16[32,128,64]{1,2,0:T(8,128)(2,1)S(1)}, bf16[32,128,64]{1,2,0:T(8,128)(2,1)}, u32[]{:S(2)}) copy-start(bf16[32,128,64]{1,2,0:T(8,128)(2,1)} %param.17) | copy-start | bytes 1572868
  39.5 15.1 %copy-start.5 = (f32[8,64,64]{2,1,0:T(8,128)S(1)}, f32[8,64,64]{2,1,0:T(8,128)}, u32[]{:S(2)}) copy-start(f32[8,64,64]{2,1,0:T(8,128)} %trans_leaf.3) | copy-start | bytes 393220
  39.5 15.1 %copy-start.7 = (f32[8,64,64]{2,1,0:T(8,128)S(1)}, f32[8,64,64]{2,1,0:T(8,128)}, u32[]{:S(2)}) copy-start(f32[8,64,64]{2,1,0:T(8,128)} %trans_dev.3) | copy-start | bytes 393220
  39.5 15.1 %copy-start.14 = (s32[32]{0:T(128)S(1)}, s32[32]{0:T(128)}, u32[]{:S(2)}) copy-start(s32[32]{0:T(128)} %leaf_trans.3) | copy-start | bytes 388

commit v2 on v1

v2 whole, which is shorter than its diff:
```python
import functools

import jax
import jax.numpy as jnp
from jax import lax
from jax.experimental import pallas as pl
from jax.experimental.pallas import tpu as pltpu
from jax.sharding import PartitionSpec as P

HIGHEST = lax.Precision.HIGHEST
F32 = jnp.float32
BF16 = jnp.bfloat16
NT = (((1,), (1,)), ((), ()))
AXES = ("grp", "dev")
VMEM = pl.BlockSpec(memory_space=pltpu.VMEM)
SMEM = pl.BlockSpec(memory_space=pltpu.SMEM)
HBM = pl.BlockSpec(memory_space=pltpu.HBM)
MIB = 2**20


def halves(x):
    half = x.shape[1] // 2
    return jnp.concatenate([x[:, :half], x[:, half:]], axis=0)


def fold(product):
    r, j = product.shape[0] // 2, product.shape[1] // 2
    return product[:r, :j] + product[r:, j:]


def moment_kernel(
    leaf_trans_hbm, dev_trans_hbm, charges_hbm, basis_hbm, trans_leaf_hbm, trans_dev_hbm, table_hbm,
    moments, send_first, send_second, sums, charges, basis_t, trans_leaf, trans_dev, table,
    leaf_trans, dev_trans, classes, sems,
):
    moves = [
        (charges_hbm, charges), (basis_hbm, basis_t), (leaf_trans_hbm, leaf_trans),
        (trans_leaf_hbm, trans_leaf), (dev_trans_hbm, dev_trans), (trans_dev_hbm, trans_dev),
        (table_hbm, table),
    ]
    copies = [
        pltpu.make_async_copy(source, target, sems.at[i])
        for i, (source, target) in enumerate(moves)
    ]
    for copy in copies:
        copy.start()
    leaves, r, _ = charges.shape
    k = basis_t.shape[1]
    margin = leaves // 2
    kinds = trans_leaf.shape[0]
    even = lax.rem(lax.axis_index("dev"), 2) == 0
    left = lax.broadcasted_iota(jnp.int32, (r, 2 * k), 1) < k
    classes[...] = jnp.zeros_like(classes)
    for copy in copies[:3]:
        copy.wait()
    for leaf in range(leaves):
        basis = basis_t[leaf]
        twice = lax.dot_general(
            charges[leaf], jnp.concatenate([basis, basis], axis=0), NT,
            preferred_element_type=F32,
        )
        kind = leaf_trans[leaf]
        classes[kind] = classes[kind] + twice
        high = twice.astype(BF16).astype(F32)
        moments[leaf] = jnp.where(left, high, twice - high).astype(BF16)
    for copy in copies[3:6]:
        copy.wait()
    own = functools.partial(jnp.dot, precision=HIGHEST, preferred_element_type=F32)
    box = jnp.zeros((r, k), F32)
    for pair in range(kinds // 2):
        lhs = jnp.where(left, classes[2 * pair], classes[2 * pair + 1])
        rhs = jnp.concatenate([trans_leaf[2 * pair], trans_leaf[2 * pair + 1]], axis=0)
        box = box + own(lhs, rhs)
    up = own(box, trans_dev[dev_trans[0]])
    both = jnp.concatenate([box, up], axis=1)
    sums[...] = both
    high = both.astype(BF16)
    send_first[margin, :r] = high
    send_first[margin, r:] = (both - high.astype(F32)).astype(BF16)

    def fill(first_from, second_from):
        for leaf in range(margin):
            send_first[leaf, :r] = charges[first_from + leaf]
            send_first[leaf, r:] = moments[first_from + leaf]
            send_second[leaf, :r] = charges[second_from + leaf]
            send_second[leaf, r:] = moments[second_from + leaf]

    @pl.when(even)
    def _():
        fill(margin, 0)

    @pl.when(jnp.logical_not(even))
    def _():
        fill(0, margin)

    copies[6].wait()


def table_kernel(chunk, count, table, blocks, out, buffer, sems):
    half, kinds = table.shape[1], table.shape[3]
    live = count[0]
    copies = [
        pltpu.make_async_copy(
            blocks.at[pl.ds(i * chunk, chunk)], buffer.at[pl.ds(i * chunk, chunk)], sems.at[i]
        )
        for i in range(blocks.shape[0] // chunk)
    ]
    for i, copy in enumerate(copies):

        @pl.when(i * chunk < live)
        def _():
            copy.start()

    def step(row, carry):
        stacked = jnp.concatenate([table[0, row], table[1, row]], axis=0)
        for start in range(0, kinds, 128):
            width = min(128, kinds - start)
            out[pl.ds(start * half + row, width, stride=half), :] = stacked[
                :, start : start + width
            ].T
        return carry

    lax.fori_loop(0, half, step, 0, unroll=8)
    for i, copy in enumerate(copies):

        @pl.when(i * chunk < live)
        def _():
            copy.wait()


def halo_places(leaves):
    margin = leaves // 2
    even = lax.rem(lax.axis_index("dev"), 2) == 0
    return jnp.where(even, margin + leaves, 0), jnp.where(even, 0, margin + leaves)


def first_leaf(leaves):
    return (lax.axis_index("grp") * lax.axis_size("dev") + lax.axis_index("dev")) * leaves


def near_kernel(
    chunk, targets, sources, count, charges, first, second, blocks, out, window, total
):
    slots = blocks.shape[0]
    leaves, r, panels = charges.shape
    margin = leaves // 2
    live = count[0]
    leaf_start = first_leaf(leaves)
    first_at, second_at = halo_places(leaves)
    window[pl.ds(margin, leaves)] = charges[...]
    window[pl.ds(first_at, margin)] = first[:margin, :r]
    window[pl.ds(second_at, margin)] = second[:, :r]
    total[...] = jnp.zeros_like(total)

    def picked(slot):
        return window[sources[slot] - leaf_start + margin]

    def step(index, carry):
        base = index * chunk
        products = []
        for u in range(0, chunk, 2):
            both = lax.dot_general(
                jnp.concatenate([picked(base + u), picked(base + u + 1)], axis=0),
                blocks[pl.ds(base + u, 2)].reshape(2 * panels, panels),
                NT, preferred_element_type=F32,
            )
            products += [both[:r, :panels], both[r:, panels:]]
        for u in range(chunk):
            slot = base + u
            row = jnp.where(slot < live, targets[slot] - leaf_start, leaves)
            total[row] = total[row] + products[u]
        return carry

    lax.fori_loop(0, (live + chunk - 1) // chunk, step, 0)
    out[...] = total[:leaves]


def couple(table, kind, half):
    return table[pl.ds(pl.multiple_of(kind * half, half), half), :]


def far_leaves(start, far, far_couple, spread, table, out):
    count, r, k = out.shape
    leaves = spread.shape[0] // 2
    nfar = far.shape[0]
    width, half = 2 * k, k // 2
    origin = first_leaf(leaves) - leaves // 2
    lane = lax.broadcasted_iota(jnp.int32, (4 * r, width), 1) // half
    results = []
    for leaf in range(start, start + count):
        lhs, rhs = [], []
        for quad in range(nfar // 4):
            picked = None
            tables = []
            for q in range(4):
                f = quad * 4 + q
                source = spread[far[f, leaf] - origin]
                picked = source if q == 0 else jnp.where(lane >= q, source, picked)
                tables.append(couple(table, far_couple[f, leaf], half))
            stacked = jnp.concatenate(tables, axis=0)
            high = stacked.astype(BF16)
            low = (stacked - high.astype(F32)).astype(BF16)
            lhs.append(picked)
            rhs.append(jnp.concatenate([high, low], axis=1))
        product = jnp.dot(
            jnp.concatenate(lhs, axis=1), jnp.concatenate(rhs, axis=0),
            preferred_element_type=F32,
        )
        product = product[: 2 * r] + product[2 * r :]
        out[leaf - start] = fold(product[:, :width] + product[:, width:])


def far_low_kernel(
    far, far_couple, moments, first, second, table, out, spread, window
):
    leaves, r, width = moments.shape
    margin = leaves // 2
    half = width // 4
    first_at, second_at = halo_places(leaves)
    window[pl.ds(margin, leaves)] = moments[...]
    window[pl.ds(first_at, margin)] = first[:margin, r:]
    window[pl.ds(second_at, margin)] = second[:, r:]
    row = lax.broadcasted_iota(jnp.int32, (width, 4 * width), 0)
    column = lax.broadcasted_iota(jnp.int32, (width, 4 * width), 1)
    copier = (row == (column // width) * half + lax.rem(column, half)).astype(BF16)
    piece = 8
    for start in range(0, 2 * leaves, piece):
        rows = window[start : start + piece].reshape(piece * r, width)
        copied = jnp.dot(rows, copier, preferred_element_type=F32).astype(BF16)
        for section in range(4):
            spread[start : start + piece, section * r : (section + 1) * r] = copied[
                :, section * width : (section + 1) * width
            ].reshape(piece, r, width)
    far_leaves(0, far, far_couple, spread, table, out)


def far_high_kernel(
    far, far_couple, dev_list, dev_couple, grp_couple, spread, table, boxes,
    out, listed_out, group_tables,
):
    _, r, k = out.shape
    half = k // 2
    group = lax.axis_index("grp")
    member = lax.axis_index("dev")
    far_leaves(out.shape[0], far, far_couple, spread, table, out)
    lhs, rhs = [], []
    for n in range(dev_list.shape[1]):
        place = jnp.bitwise_xor(dev_list[0, n] - group * lax.axis_size("dev"), member)
        lhs.append(halves(boxes[place][:, :k]))
        rhs.append(couple(table, dev_couple[0, n], half))
    listed_out[...] = fold(
        jnp.dot(
            jnp.concatenate(lhs, axis=1), jnp.concatenate(rhs, axis=0),
            precision=HIGHEST, preferred_element_type=F32,
        )
    )
    for other in range(1, grp_couple.shape[0]):
        group_tables[other - 1] = couple(
            table, grp_couple[group, jnp.bitwise_xor(group, other)], half
        )


def final_kernel(
    leaf_trans, dev_trans, near, far_low, far_high, listed, group_tables, groups, basis_t,
    trans_leaf, trans_dev, out, locals_,
):
    leaves = near.shape[0]
    own = functools.partial(lax.dot_general, precision=HIGHEST, preferred_element_type=F32)
    group_local = None
    for other in range(group_tables.shape[0]):
        term = fold(
            jnp.dot(
                halves(groups[other + 1]), group_tables[other],
                precision=HIGHEST, preferred_element_type=F32,
            )
        )
        group_local = term if other == 0 else group_local + term
    box_local = own(group_local, trans_dev[dev_trans[0]], NT) + listed[...]
    for kind in range(trans_leaf.shape[0]):
        locals_[kind] = own(box_local, trans_leaf[kind], NT)
    for leaf in range(leaves):
        far = far_low[leaf] if leaf < leaves // 2 else far_high[leaf - leaves // 2]
        leaf_local = (locals_[leaf_trans[leaf]] + far).astype(BF16)
        out[leaf] = near[leaf] + jnp.dot(
            leaf_local, basis_t[leaf], preferred_element_type=F32
        )


def swap(x, axis, distance):
    return lax.ppermute(x, axis, [(i, i ^ distance) for i in range(lax.axis_size(axis))])


def cost(us):
    return pl.CostEstimate(flops=0, bytes_accessed=us * 3 * MIB, transcendentals=0)


def params(mib):
    return pltpu.CompilerParams(vmem_limit_bytes=mib * MIB)


def local(
    charges,
    leaf_basis,
    near_blocks,
    near_target,
    near_source,
    near_count,
    leaf_far,
    leaf_far_couple,
    leaf_trans,
    dev_trans,
    dev_list,
    dev_couple,
    grp_couple,
    trans_leaf,
    trans_dev,
    couple_table,
):
    leaves, r, panels = charges.shape
    k = leaf_basis.shape[2]
    margin = leaves // 2
    slots = near_blocks.shape[0]
    kinds = couple_table.shape[0]
    half = k // 2
    per_group = lax.axis_size("dev")
    devices = per_group * lax.axis_size("grp")
    basis_t = jnp.swapaxes(leaf_basis, 1, 2)
    shape = jax.ShapeDtypeStruct

    moments, send_first, send_second, sums, own_charges, basis, leaf_maps, dev_maps, raw = (
        pl.pallas_call(
            moment_kernel,
            out_shape=(
                shape((leaves, r, 2 * k), BF16),
                shape((margin + 1, 2 * r, panels), BF16),
                shape((margin, 2 * r, panels), BF16),
                shape((r, 2 * k), F32),
                shape(charges.shape, BF16),
                shape(basis_t.shape, BF16),
                shape(trans_leaf.shape, F32),
                shape(trans_dev.shape, F32),
                shape((2, half, k, kinds), F32),
            ),
            in_specs=[HBM] * 7,
            out_specs=(VMEM,) * 9,
            scratch_shapes=[
                pltpu.SMEM(leaf_trans.shape, jnp.int32),
                pltpu.SMEM(dev_trans.shape, jnp.int32),
                pltpu.VMEM((trans_leaf.shape[0], r, 2 * k), F32),
                pltpu.SemaphoreType.DMA((7,)),
            ],
            compiler_params=params(24),
            name="moments",
        )(
            leaf_trans, dev_trans, charges, basis_t, trans_leaf, trans_dev,
            jnp.transpose(couple_table, (1, 2, 0)).reshape(2, half, k, kinds),
        )
    )

    first = swap(send_first, "dev", 1)
    partners = [(i, i + 1) for i in range(1, devices - 1, 2)] + [(0, devices - 1)]
    second = lax.ppermute(send_second, AXES, partners + [(j, i) for i, j in partners])

    chunk = slots // 5
    table, blocks = pl.pallas_call(
        functools.partial(table_kernel, chunk),
        out_shape=(shape((kinds * half, 2 * k), F32), shape(near_blocks.shape, BF16)),
        in_specs=[SMEM, VMEM, HBM],
        out_specs=(VMEM, VMEM),
        scratch_shapes=[pltpu.SemaphoreType.DMA((slots // chunk,))],
        compiler_params=params(24),
        cost_estimate=cost(3),
        name="table",
    )(near_count, raw, near_blocks)

    peer = first[margin, :r].astype(F32) + first[margin, r:].astype(F32)
    boxes = jnp.stack([sums, peer])
    boxes, table, blocks, first, second = lax.optimization_barrier(
        (boxes, table, blocks, first, second)
    )
    boxes_next = jnp.concatenate([boxes, swap(boxes, "dev", 2)])

    near = pl.pallas_call(
        functools.partial(near_kernel, chunk),
        out_shape=shape((leaves, r, panels), F32),
        in_specs=[SMEM, SMEM, SMEM, VMEM, VMEM, VMEM, VMEM],
        out_specs=VMEM,
        scratch_shapes=[
            pltpu.VMEM((2 * leaves, r, panels), BF16),
            pltpu.VMEM((leaves + 1, r, panels), F32),
        ],
        compiler_params=params(16),
        cost_estimate=cost(3),
        name="near",
    )(near_target, near_source, near_count, own_charges, first, second, blocks)
    boxes, near, table = lax.optimization_barrier((boxes_next, near, table))

    far_list, far_kinds = leaf_far.T, leaf_far_couple.T
    boxes_next = boxes
    for distance in [4 << i for i in range((per_group // 4).bit_length() - 1)]:
        boxes_next = jnp.concatenate([boxes_next, swap(boxes_next, "dev", distance)])
    far_low, spread = pl.pallas_call(
        far_low_kernel,
        out_shape=(shape((margin, r, k), F32), shape((2 * leaves, 4 * r, 2 * k), BF16)),
        in_specs=[SMEM] * 2 + [VMEM] * 4,
        out_specs=(VMEM, VMEM),
        scratch_shapes=[pltpu.VMEM((2 * leaves, r, 2 * k), BF16)],
        compiler_params=params(16),
        cost_estimate=cost(3),
        name="far_low",
    )(far_list, far_kinds, moments, first, second, table)
    boxes, far_low, spread, table = lax.optimization_barrier(
        (boxes_next, far_low, spread, table)
    )

    groups = jnp.sum(boxes[:, :, k:], axis=0)[None]
    for distance in [1 << i for i in range(lax.axis_size("grp").bit_length() - 1)]:
        groups = jnp.concatenate([groups, swap(groups, "grp", distance)])
    far_high, listed, group_tables = pl.pallas_call(
        far_high_kernel,
        out_shape=(
            shape((leaves - margin, r, k), F32),
            shape((r, k), F32),
            shape((lax.axis_size("grp") - 1, half, 2 * k), F32),
        ),
        in_specs=[SMEM] * 5 + [VMEM] * 3,
        out_specs=(VMEM, VMEM, VMEM),
        compiler_params=params(16),
        cost_estimate=cost(3),
        name="far_high",
    )(far_list, far_kinds, dev_list, dev_couple, grp_couple, spread, table, boxes)

    return pl.pallas_call(
        final_kernel,
        out_shape=shape((leaves, r, panels), F32),
        in_specs=[SMEM, SMEM] + [VMEM] * 9,
        out_specs=VMEM,
        scratch_shapes=[pltpu.VMEM((trans_leaf.shape[0], r, k), F32)],
        compiler_params=params(16),
        name="final",
    )(
        leaf_trans, dev_trans, near, far_low, far_high, listed, group_tables, groups, basis,
        leaf_maps, dev_maps,
    )


def solution(mesh):
    leaf = P(AXES)
    return jax.shard_map(
        local,
        mesh=mesh,
        in_specs=(leaf,) * 12 + (P(),) * 4,
        out_specs=leaf,
        check_vma=False,
    )
```

time: 57.1 us -> 40.4 us (0.71)
  Pallas kernels: 25.7 us -> 17.9 us
  starting transfers between devices: 13.8 us -> 7.35 us
  waiting for transfers between devices: 8.66 us -> 6 us
    ppermute x7 -> x5, starting transfers between devices: 13.1 us -> 3.68 us  [swap(): lax.ppermute(x, axis, [(i, i ^ distance) for i in range(lax.axis_size(axi...]
    pallas_call x4 -> x5, Pallas kernels: 23.7 us -> 15.5 us  [the longest x1 5.94 us: local(): pl.pallas_call(functools.partial(table_kernel, chunk), out_shape=(shape((...]
    ppermute x1, starting transfers between devices: 0.66 us -> 3.67 us  [local(): lax.ppermute(send_second, AXES, partners + [(j, i) for i, j in partners])]
    ppermute x7 -> x5, waiting for transfers between devices: 8.66 us -> 6 us  [swap(): lax.ppermute(x, axis, [(i, i ^ distance) for i in range(lax.axis_size(axi...]
    unnamed x38 -> x30, local copies, waits for them, and re-layouts: 7.35 us -> 7.33 us
  transfers between devices with their start and end apart: 8 -> 6, of which waited for: 2 -> 4; matrix products, arithmetic and copies ran while one was open for 0% -> 0% of each run, Pallas kernels for 37% -> 32%
where the time goes in v2:
time: 40.4 us; the launch traced here: 40.2 us
  Pallas kernels  17.9 us (44%)
  starting transfers between devices  7.35 us (18%)
  local copies, waits for them, and re-layouts  7.33 us (18%)
  waiting for transfers between devices  6 us (15%)
  between operations  1.49 us (4%)
    unnamed x30, local copies, waits for them, and re-layouts  7.33 us
    ppermute x5, waiting for transfers between devices, swap(): lax.ppermute(x, axis, [(i, i ^ distance) for i in range(lax.axis_size(axi...  6 us
    pallas_call x1, Pallas kernels, local(): pl.pallas_call(functools.partial(table_kernel, chunk), out_shape=(shape((...  5.94 us
    ppermute x5, starting transfers between devices, swap(): lax.ppermute(x, axis, [(i, i ^ distance) for i in range(lax.axis_size(axi...  3.68 us
    ppermute x1, starting transfers between devices, local(): lax.ppermute(send_second, AXES, partners + [(j, i) for i, j in partners])  3.67 us
    pallas_call x1, Pallas kernels, local(): pl.pallas_call(functools.partial(near_kernel, chunk), out_shape=shape((le...  2.95 us
    pallas_call x1, Pallas kernels, local(): pl.pallas_call(final_kernel, out_shape=shape((leaves, r, panels), F32), i...  2.59 us
    pallas_call x1, Pallas kernels, local(): pl.pallas_call(moment_kernel, out_shape=(shape((leaves, r, 2 * k), BF16),...  2.39 us
  transfers between devices with their start and end apart: 6, of which 4 were waited for; matrix products, arithmetic and copies ran while one was open for 0% of the time, Pallas kernels for 32%

profile of v2, /device:TPU:0, one launch (start us, length us, event | category | flops | bytes accessed | tf_op | source)
XLA Modules:
  0.0 40.2 jit_solution(12480298293936172088)
XLA Ops:
  0.7 0.0 copy-start
  0.7 2.8 %copy-done = f32[316,64,64]{0,2,1:T(8,128)S(1)} copy-done((f32[316,64,64]{0,2,1:T(8,128)S(1)}, f32[316,64,64]{0,2,1:T(8,128)}, u32[]{:S(2)}) %copy-start) | copy-done | bytes 5177368
  3.4 0.0 copy-start.2
  3.4 1.0 %copy-done.2 = bf16[32,128,64]{1,2,0:T(8,128)(2,1)S(1)} copy-done((bf16[32,128,64]{1,2,0:T(8,128)(2,1)S(1)}, bf16[32,128,64]{1,2,0:T(8,128)(2,1)}, u32[]{:S(2)}) %copy-start.2) | copy-done | bytes 524312
  4.5 0.0 copy-start.3
  4.5 0.9 %copy-done.3 = f32[8,64,64]{2,1,0:T(8,128)S(1)} copy-done((f32[8,64,64]{2,1,0:T(8,128)S(1)}, f32[8,64,64]{2,1,0:T(8,128)}, u32[]{:S(2)}) %copy-start.3) | copy-done | bytes 131096
  5.4 0.0 copy-start.4
  5.4 0.9 %copy-done.4 = f32[8,64,64]{2,1,0:T(8,128)S(1)} copy-done((f32[8,64,64]{2,1,0:T(8,128)S(1)}, f32[8,64,64]{2,1,0:T(8,128)}, u32[]{:S(2)}) %copy-start.4) | copy-done | bytes 131096
  6.4 0.0 copy-start.5
  6.4 0.9 %copy-done.5 = bf16[32,16,128]{2,1,0:T(8,128)(2,1)S(1)} copy-done((bf16[32,16,128]{2,1,0:T(8,128)(2,1)S(1)}, bf16[32,16,128]{2,1,0:T(8,128)(2,1)}, u32[]{:S(2)}) %copy-start.5) | copy-done | bytes 131096
  7.3 0.0 copy-start.9
  7.3 0.7 %copy-done.9 = s32[32]{0:T(128)S(1)} copy-done((s32[32]{0:T(128)S(1)}, s32[32]{0:T(128)}, u32[]{:S(2)}) %copy-start.9) | copy-done | bytes 152
  7.9 0.0 copy-start.1
  7.9 2.4 %moments.1 = (bf16[32,16,128]{2,1,0:T(8,128)(2,1)S(1)}, bf16[17,32,128]{2,1,0:T(8,128)(2,1)S(1)}, bf16[16,32,128]{2,1,0:T(8,128)(2,1)S(1)}, f32[16,128]{1,0:T(8,...) custom-call(s32[32]{0:T(128)S(1)} %copy-done.9, ...), custom_call_target="tpu_custom_call" | custom-call | tf_op jit(solution)/shard_map/moments/pallas_call | solution.py:331
  10.3 3.0 %collective-permute-start = (bf16[17,32,128]{2,1,0:T(8,128)(2,1)S(1)}, bf16[17,32,128]{2,1,0:T(8,128)(2,1)S(1)}, u32[]{:S(2)}, u32[]{:S(2)}) collective-permute-start(bf16[17,32,128]{2,1,0:T(8,128)(2,1)S(1)} %get-tuple-element.34), channel_id=1, source_target_pairs={{0,1},{1,0},{2,3},{3,2},{4,5},{5,4},{6,7},{7,6},{8,9},{9,8},{10,11... | collective-permute-start | bytes 417800 | tf_op jit(solution)/shard_map/ppermute | solution.py:290
  13.4 3.7 %collective-permute-start.1 = (bf16[16,32,128]{2,1,0:T(8,128)(2,1)S(1)}, bf16[16,32,128]{2,1,0:T(8,128)(2,1)S(1)}, u32[]{:S(2)}, u32[]{:S(2)}) collective-permute-start(bf16[16,32,128]{2,1,0:T(8,128)(2,1)S(1)} %get-tuple-element.38), channel_id=1, source_target_pairs={{1,2},{3,4},{5,6},{7,8},{9,10},{11,12},{13,14},{15,16},{17,18},{19... | collective-permute-start | bytes 393224 | tf_op jit(solution)/shard_map/ppermute | solution.py:362
  17.7 0.0 copy-done.1
  17.7 0.0 copy-start.11
  17.7 0.0 copy-start.12
  17.7 5.9 %table.1 = (f32[10112,128]{1,0:T(8,128)S(1)}, bf16[160,128,128]{2,1,0:T(8,128)(2,1)S(1)}) custom-call(s32[1]{0:T(128)S(6)} %copy.17.count, f32[2,32,64,316]{3,2,1,0:T(8,128)S(1)} %get-tuple-element.35.table, bf16[160,128,128]{2,1,0:T(8,128)(2,1)S(1)} %copy-done.1), custom_call_target="tpu_custom_call" | custom-call | bytes 9437184 | tf_op jit(solution)/shard_map/table/pallas_call | solution.py:365
  23.7 0.0 copy-start.6
  23.7 0.0 copy-start.7
  23.7 0.0 collective-permute-done.first
  23.7 0.0 collective-permute-done.1.second
  23.7 0.1 collective-permute-start.2
  23.8 0.0 copy-done.11
  23.8 0.0 copy-done.12
  23.8 0.0 copy-start.8
  23.9 0.0 copy-start.13
  23.9 0.0 copy-start.14
  23.9 2.9 %near.1 = f32[32,16,128]{2,1,0:T(8,128)S(1)} custom-call(s32[160]{0:T(256)S(1)} %copy-done.11, s32[160]{0:T(256)S(1)} %copy-done.12, s32[1]{0:T(128)S(6)} %copy.17.count, bf16[32,16,128]{2,1,0:T(8,128)(2,1)S(1)} %get-tuple-element.40.charges, bf16[17,32,128]{2,1,0:T(8,128)(2,1)S(1)} %collective-permute-done.first, ...), custom_call_target="tpu_custom_call" | custom-call | bytes 9437184 | tf_op jit(solution)/shard_map/near/pallas_call | solution.py:383
  26.8 0.7 %collective-permute-done.2 = f32[2,16,128]{2,1,0:T(8,128)S(1)} collective-permute-done((f32[2,16,128]{2,1,0:T(8,128)S(1)}, f32[2,16,128]{2,1,0:T(8,128)S(1)}, u32[]{:S(2)}, u32[]{:S(2)}) %collective-permute-start.2) | collective-permute-done | bytes 16416 | tf_op jit(solution)/shard_map/ppermute | solution.py:290
  27.6 0.1 collective-permute-start.3
  27.6 0.0 copy-done.6
  27.6 0.0 copy-done.7
  27.6 0.0 copy-start.10
  27.6 2.2 %far_low.1 = (f32[16,16,64]{2,1,0:T(8,128)S(1)}, bf16[64,64,128]{2,1,0:T(8,128)(2,1)S(1)}) custom-call(s32[16,32]{1,0:T(8,128)S(1)} %bitcast.10, s32[16,32]{1,0:T(8,128)S(1)} %bitcast.12, bf16[32,16,128]{2,1,0:T(8,128)(2,1)S(1)} %get-tuple-element.47.moments, bf16[17,32,128]{2,1,0:T(8,128)(2,1)S(1)} %collective-permute-done.first, ...), custom_call_target="tpu_custom_call" | custom-call | bytes 9437184 | tf_op jit(solution)/shard_map/far_low/pallas_call | solution.py:402
  29.8 2.7 %collective-permute-done.3 = f32[4,16,128]{2,1,0:T(8,128)S(1)} collective-permute-done((f32[4,16,128]{2,1,0:T(8,128)S(1)}, f32[4,16,128]{2,1,0:T(8,128)S(1)}, u32[]{:S(2)}, u32[]{:S(2)}) %collective-permute-start.3) | collective-permute-done | bytes 32800 | tf_op jit(solution)/shard_map/ppermute | solution.py:290
  32.5 0.1 slice_reduce_fusion
  32.6 0.1 collective-permute-start.4
  32.7 1.2 %collective-permute-done.4 = f32[1,16,64]{2,1,0:T(8,128)S(1)} collective-permute-done((f32[1,16,64]{2,1,0:T(8,128)S(1)}, f32[1,16,64]{2,1,0:T(8,128)S(1)}, u32[]{:S(2)}, u32[]{:S(2)}) %collective-permute-start.4) | collective-permute-done | bytes 4128 | tf_op jit(solution)/shard_map/ppermute | solution.py:290
  33.8 0.4 %collective-permute-start.5 = (f32[2,16,64]{2,1,0:T(8,128)S(1)}, f32[2,16,64]{2,1,0:T(8,128)S(1)}, u32[]{:S(2)}, u32[]{:S(2)}) collective-permute-start(f32[2,16,64]{2,1,0:T(8,128)S(1)} %pad_maximum_fusion.4), channel_id=1, source_target_pairs={{0,16},{8,24},{16,0},{24,8},{1,17},{9,25},{17,1},{25,9},{2,18},{10... | collective-permute-start | bytes 24584 | tf_op jit(solution)/shard_map/ppermute | solution.py:290
  34.3 0.0 copy-done.8
  34.3 0.0 copy-done.13
  34.3 0.0 copy-done.14
  34.3 1.8 %far_high.1 = (f32[16,16,64]{2,1,0:T(8,128)S(1)}, f32[16,64]{1,0:T(8,128)S(1)}, f32[3,32,128]{2,1,0:T(8,128)S(1)}) custom-call(s32[16,32]{1,0:T(8,128)S(1)} %bitcast.11, s32[16,32]{1,0:T(8,128)S(1)} %bitcast.13, s32[1,4]{1,0:T(1,128)S(1)} %copy-done.13, s32[1,4]{1,0:T(1,128)S(1)} %copy-done.14, s32[4,4]{1,0:T(4,128)S(1)} %copy-done.8, ...), custom_call_target="tpu_custom_call" | custom-call | bytes 9437184 | tf_op jit(solution)/shard_map/far_high/pallas_call | solution.py:419
  36.1 1.5 %collective-permute-done.5 = f32[2,16,64]{2,1,0:T(8,128)S(1)} collective-permute-done((f32[2,16,64]{2,1,0:T(8,128)S(1)}, f32[2,16,64]{2,1,0:T(8,128)S(1)}, u32[]{:S(2)}, u32[]{:S(2)}) %collective-permute-start.5) | collective-permute-done | bytes 8224 | tf_op jit(solution)/shard_map/ppermute | solution.py:290
  37.6 0.0 copy-done.10
  37.6 2.6 %final.1 = f32[32,16,128]{2,1,0:T(8,128)} custom-call(s32[32]{0:T(128)S(1)} %copy-done.10, s32[1]{0:T(128)S(6)} %copy.18.dev_trans_hbm.dev_trans, f32[32,16,128]{2,1,0:T(8,128)S(1)} %near.1, f32[16,16,64]{2,1,0:T(8,128)S(1)} %get-tuple-element.51.far_low, f32[16,16,64]{2,1,0:T(8,128)S(1)} %get-tuple-element.55.far_high, ...), custom_call_target="tpu_custom_call" | custom-call | tf_op jit(solution)/shard_map/final/pallas_call | solution.py:433
  (6 shorter events, 0.0 us)
Async XLA Ops:
  0.7 2.8 %copy-start = (f32[316,64,64]{0,2,1:T(8,128)S(1)}, f32[316,64,64]{0,2,1:T(8,128)}, u32[]{:S(2)}) copy-start(f32[316,64,64]{0,2,1:T(8,128)} %param.31) | copy-start | bytes 15532036
  3.4 1.0 %copy-start.2 = (bf16[32,128,64]{1,2,0:T(8,128)(2,1)S(1)}, bf16[32,128,64]{1,2,0:T(8,128)(2,1)}, u32[]{:S(2)}) copy-start(bf16[32,128,64]{1,2,0:T(8,128)(2,1)} %param.17) | copy-start | bytes 1572868
  4.5 0.9 %copy-start.3 = (f32[8,64,64]{2,1,0:T(8,128)S(1)}, f32[8,64,64]{2,1,0:T(8,128)}, u32[]{:S(2)}) copy-start(f32[8,64,64]{2,1,0:T(8,128)} %trans_leaf_hbm.1) | copy-start | bytes 393220
  5.4 0.9 %copy-start.4 = (f32[8,64,64]{2,1,0:T(8,128)S(1)}, f32[8,64,64]{2,1,0:T(8,128)}, u32[]{:S(2)}) copy-start(f32[8,64,64]{2,1,0:T(8,128)} %trans_dev_hbm.1) | copy-start | bytes 393220
  6.4 0.9 %copy-start.5 = (bf16[32,16,128]{2,1,0:T(8,128)(2,1)S(1)}, bf16[32,16,128]{2,1,0:T(8,128)(2,1)}, u32[]{:S(2)}) copy-start(bf16[32,16,128]{2,1,0:T(8,128)(2,1)} %charges_hbm.1) | copy-start | bytes 393220
  7.3 0.7 %copy-start.9 = (s32[32]{0:T(128)S(1)}, s32[32]{0:T(128)}, u32[]{:S(2)}) copy-start(s32[32]{0:T(128)} %leaf_trans.1) | copy-start | bytes 388
  7.9 9.7 %copy-start.1 = (bf16[160,128,128]{2,1,0:T(8,128)(2,1)S(1)}, bf16[160,128,128]{2,1,0:T(8,128)(2,1)}, u32[]{:S(2)}) copy-start(bf16[160,128,128]{2,1,0:T(8,128)(2,1)} %blocks.1) | copy-start | bytes 15728644
  10.3 13.4 %collective-permute-start = (bf16[17,32,128]{2,1,0:T(8,128)(2,1)S(1)}, bf16[17,32,128]{2,1,0:T(8,128)(2,1)S(1)}, u32[]{:S(2)}, u32[]{:S(2)}) collective-permute-start(bf16[17,32,128]{2,1,0:T(8,128)(2,1)S(1)} %get-tuple-element.34), channel_id=1, source_target_pairs={{0,1},{1,0},{2,3},{3,2},{4,5},{5,4},{6,7},{7,6},{8,9},{9,8},{10,11... | collective-permute-start | bytes 417800 | tf_op jit(solution)/shard_map/ppermute | solution.py:290
  13.4 10.4 %collective-permute-start.1 = (bf16[16,32,128]{2,1,0:T(8,128)(2,1)S(1)}, bf16[16,32,128]{2,1,0:T(8,128)(2,1)S(1)}, u32[]{:S(2)}, u32[]{:S(2)}) collective-permute-start(bf16[16,32,128]{2,1,0:T(8,128)(2,1)S(1)} %get-tuple-element.38), channel_id=1, source_target_pairs={{1,2},{3,4},{5,6},{7,8},{9,10},{11,12},{13,14},{15,16},{17,18},{19... | collective-permute-start | bytes 393224 | tf_op jit(solution)/shard_map/ppermute | solution.py:362
  17.7 6.1 %copy-start.11 = (s32[160]{0:T(256)S(1)}, s32[160]{0:T(256)}, u32[]{:S(2)}) copy-start(s32[160]{0:T(256)} %targets.1) | copy-start | bytes 1924
  17.7 6.1 %copy-start.12 = (s32[160]{0:T(256)S(1)}, s32[160]{0:T(256)}, u32[]{:S(2)}) copy-start(s32[160]{0:T(256)} %sources.1) | copy-start | bytes 1924
  23.7 4.0 %copy-start.6 = (s32[32,16]{0,1:T(8,128)S(1)}, s32[32,16]{0,1:T(8,128)}, u32[]{:S(2)}) copy-start(s32[32,16]{0,1:T(8,128)} %param.22) | copy-start | bytes 6148
  23.7 3.9 %copy-start.7 = (s32[32,16]{0,1:T(8,128)S(1)}, s32[32,16]{0,1:T(8,128)}, u32[]{:S(2)}) copy-start(s32[32,16]{0,1:T(8,128)} %param.23) | copy-start | bytes 6148
  23.7 3.8 %collective-permute-start.2 = (f32[2,16,128]{2,1,0:T(8,128)S(1)}, f32[2,16,128]{2,1,0:T(8,128)S(1)}, u32[]{:S(2)}, u32[]{:S(2)}) collective-permute-start(f32[2,16,128]{2,1,0:T(8,128)S(1)} %pad_maximum_fusion.3), channel_id=1, source_target_pairs={{0,2},{1,3},{2,0},{3,1},{4,6},{5,7},{6,4},{7,5},{8,10},{9,11},{10,... | collective-permute-start | bytes 49160 | tf_op jit(solution)/shard_map/ppermute | solution.py:290
  23.8 10.5 %copy-start.8 = (s32[4,4]{1,0:T(4,128)S(1)}, s32[4,4]{1,0:T(4,128)}, u32[]{:S(2)}) copy-start(s32[4,4]{1,0:T(4,128)} %grp_couple.1) | copy-start | bytes 196
  23.9 10.4 %copy-start.13 = (s32[1,4]{1,0:T(1,128)S(1)}, s32[1,4]{1,0:T(1,128)}, u32[]{:S(2)}) copy-start(s32[1,4]{1,0:T(1,128)} %dev_list.1) | copy-start | bytes 52
  23.9 10.4 %copy-start.14 = (s32[1,4]{1,0:T(1,128)S(1)}, s32[1,4]{1,0:T(1,128)}, u32[]{:S(2)}) copy-start(s32[1,4]{1,0:T(1,128)} %dev_couple.1) | copy-start | bytes 52
  27.6 5.0 %collective-permute-start.3 = (f32[4,16,128]{2,1,0:T(8,128)S(1)}, f32[4,16,128]{2,1,0:T(8,128)S(1)}, u32[]{:S(2)}, u32[]{:S(2)}) collective-permute-start(f32[4,16,128]{2,1,0:T(8,128)S(1)} %pad_maximum_fusion.1), channel_id=1, source_target_pairs={{0,4},{1,5},{2,6},{3,7},{4,0},{5,1},{6,2},{7,3},{8,12},{9,13},{10,... | collective-permute-start | bytes 98312 | tf_op jit(solution)/shard_map/ppermute | solution.py:290
  27.6 10.0 %copy-start.10 = (s32[32]{0:T(128)S(1)}, s32[32]{0:T(128)}, u32[]{:S(2)}) copy-start(s32[32]{0:T(128)} %leaf_trans.1) | copy-start | bytes 388
  32.6 1.2 %collective-permute-start.4 = (f32[1,16,64]{2,1,0:T(8,128)S(1)}, f32[1,16,64]{2,1,0:T(8,128)S(1)}, u32[]{:S(2)}, u32[]{:S(2)}) collective-permute-start(f32[1,16,64]{2,1,0:T(8,128)S(1)} %bitcast.15), channel_id=1, source_target_pairs={{0,8},{8,0},{16,24},{24,16},{1,9},{9,1},{17,25},{25,17},{2,10},{10... | collective-permute-start | bytes 12296 | tf_op jit(solution)/shard_map/ppermute | solution.py:290
  33.8 3.7 %collective-permute-start.5 = (f32[2,16,64]{2,1,0:T(8,128)S(1)}, f32[2,16,64]{2,1,0:T(8,128)S(1)}, u32[]{:S(2)}, u32[]{:S(2)}) collective-permute-start(f32[2,16,64]{2,1,0:T(8,128)S(1)} %pad_maximum_fusion.4), channel_id=1, source_target_pairs={{0,16},{8,24},{16,0},{24,8},{1,17},{9,25},{17,1},{25,9},{2,18},{10... | collective-permute-start | bytes 24584 | tf_op jit(solution)/shard_map/ppermute | solution.py:290

commit v3 on v2

v3 whole, which is shorter than its diff:
```python
import functools

import jax
import jax.numpy as jnp
from jax import lax
from jax.experimental import pallas as pl
from jax.experimental.pallas import tpu as pltpu
from jax.sharding import PartitionSpec as P

F32 = jnp.float32
BF16 = jnp.bfloat16
NT = (((1,), (1,)), ((), ()))
AXES = ("grp", "dev")
VMEM = pl.BlockSpec(memory_space=pltpu.VMEM)
SMEM = pl.BlockSpec(memory_space=pltpu.SMEM)
HBM = pl.BlockSpec(memory_space=pltpu.HBM)
MIB = 2**20


def halves(x):
    half = x.shape[1] // 2
    return jnp.concatenate([x[:, :half], x[:, half:]], axis=0)


def fold(product):
    r, j = product.shape[0] // 2, product.shape[1] // 2
    return product[:r, :j] + product[r:, j:]


def split(x):
    high = x.astype(BF16)
    return high, (x - high.astype(F32)).astype(BF16)


def dot3(a, b, dims=(((1,), (0,)), ((), ()))):
    (a_high, a_low), (b_high, b_low) = split(a), split(b)
    both = lax.dot_general(
        jnp.concatenate([a_high, a_low], axis=0), b_high, dims, preferred_element_type=F32
    )
    rest = lax.dot_general(a_high, b_low, dims, preferred_element_type=F32)
    return both[: a.shape[0]] + both[a.shape[0] :] + rest


def moment_kernel(
    leaf_trans_hbm, dev_trans_hbm, charges_hbm, basis_hbm, trans_leaf_hbm, trans_dev_hbm, table_hbm,
    moments, send_first, send_second, sums, leaf_trans, dev_trans, charges, basis_t,
    trans_leaf, trans_dev, table, classes, sems,
):
    moves = [
        (charges_hbm, charges), (basis_hbm, basis_t), (leaf_trans_hbm, leaf_trans),
        (trans_leaf_hbm, trans_leaf), (dev_trans_hbm, dev_trans), (trans_dev_hbm, trans_dev),
        (table_hbm, table),
    ]
    copies = [
        pltpu.make_async_copy(source, target, sems.at[i])
        for i, (source, target) in enumerate(moves)
    ]
    for copy in copies:
        copy.start()
    leaves, r, _ = charges.shape
    k = basis_t.shape[1]
    margin = leaves // 2
    kinds = trans_leaf.shape[0]
    even = lax.rem(lax.axis_index("dev"), 2) == 0
    left = lax.broadcasted_iota(jnp.int32, (r, 2 * k), 1) < k
    classes[...] = jnp.zeros_like(classes)
    for copy in copies[:3]:
        copy.wait()
    for leaf in range(leaves):
        basis = basis_t[leaf]
        twice = lax.dot_general(
            charges[leaf], jnp.concatenate([basis, basis], axis=0), NT,
            preferred_element_type=F32,
        )
        kind = leaf_trans[leaf]
        classes[kind] = classes[kind] + twice
        high = twice.astype(BF16).astype(F32)
        moments[leaf] = jnp.where(left, high, twice - high).astype(BF16)
    for copy in copies[3:6]:
        copy.wait()
    lhs = [
        jnp.where(left, classes[kind], classes[kind + 1]) for kind in range(0, kinds, 2)
    ]
    box = dot3(jnp.concatenate(lhs, axis=1), trans_leaf[...].reshape(kinds * k, k))
    up = dot3(box, trans_dev[dev_trans[0]])
    both = jnp.concatenate([box, up], axis=1)
    sums[...] = both
    high = both.astype(BF16)
    send_first[margin, :r] = high
    send_first[margin, r:] = (both - high.astype(F32)).astype(BF16)

    def fill(first_from, second_from):
        for leaf in range(margin):
            send_first[leaf, :r] = charges[first_from + leaf]
            send_first[leaf, r:] = moments[first_from + leaf]
            send_second[leaf, :r] = charges[second_from + leaf]
            send_second[leaf, r:] = moments[second_from + leaf]

    @pl.when(even)
    def _():
        fill(margin, 0)

    @pl.when(jnp.logical_not(even))
    def _():
        fill(0, margin)

    copies[6].wait()


def relayout(table, row, out, count):
    kinds = table.shape[3]
    stacked = jnp.concatenate([table[0, row], table[1, row]], axis=0)
    for start in range(0, kinds, 128):
        width = min(128, kinds - start)
        out[pl.ds(start * count + lax.rem(row, count), width, stride=count), :] = stacked[
            :, start : start + width
        ].T


def table_kernel(table, blocks_hbm, out, blocks, sem):
    copy = pltpu.make_async_copy(blocks_hbm, blocks, sem)
    copy.start()
    rows = table.shape[1] // 2

    def step(row, carry):
        relayout(table, row, out, rows)
        return carry

    lax.fori_loop(0, rows, step, 0, unroll=8)
    copy.wait()


def halo_places(leaves):
    margin = leaves // 2
    even = lax.rem(lax.axis_index("dev"), 2) == 0
    return jnp.where(even, margin + leaves, 0), jnp.where(even, 0, margin + leaves)


def first_leaf(leaves):
    return (lax.axis_index("grp") * lax.axis_size("dev") + lax.axis_index("dev")) * leaves


def near_kernel(
    steps, targets, sources, count, charges, first, second, blocks, table, out, table_out,
    window, total,
):
    chunk = blocks.shape[0] // steps
    leaves, r, panels = charges.shape
    margin = leaves // 2
    rows = table.shape[1] // 2
    live = count[0]
    leaf_start = first_leaf(leaves)
    first_at, second_at = halo_places(leaves)
    window[pl.ds(margin, leaves)] = charges[...]
    window[pl.ds(first_at, margin)] = first[:margin, :r]
    window[pl.ds(second_at, margin)] = second[:, :r]
    total[...] = jnp.zeros_like(total)

    def picked(slot):
        return window[sources[slot] - leaf_start + margin]

    def step(index, carry):
        base = index * chunk
        products = []
        for u in range(0, chunk, 2):
            both = lax.dot_general(
                jnp.concatenate([picked(base + u), picked(base + u + 1)], axis=0),
                blocks[pl.ds(base + u, 2)].reshape(2 * panels, panels),
                NT, preferred_element_type=F32,
            )
            products += [both[:r, :panels], both[r:, panels:]]
        for u in range(rows // steps):
            relayout(table, rows + index * (rows // steps) + u, table_out, rows)
        for u in range(chunk):
            slot = base + u
            row = jnp.where(slot < live, targets[slot] - leaf_start, leaves)
            total[row] = total[row] + products[u]
        return carry

    lax.fori_loop(0, steps, step, 0)
    out[...] = total[:leaves]


def couple(tables, kind):
    return jnp.concatenate([table[kind] for table in tables], axis=0)


def far_kernel(
    far, far_couple, dev_list, dev_couple, grp_couple, moments, first, second, table_low,
    table_high, boxes, out, listed_out, group_tables, window, spread,
):
    leaves, r, width = moments.shape
    margin = leaves // 2
    k, half = width // 2, width // 4
    nfar = far.shape[0]
    tables = (table_low, table_high)
    group = lax.axis_index("grp")
    member = lax.axis_index("dev")
    origin = first_leaf(leaves) - margin
    first_at, second_at = halo_places(leaves)
    window[pl.ds(margin, leaves)] = moments[...]
    window[pl.ds(first_at, margin)] = first[:margin, r:]
    window[pl.ds(second_at, margin)] = second[:, r:]
    row = lax.broadcasted_iota(jnp.int32, (width, 4 * width), 0)
    column = lax.broadcasted_iota(jnp.int32, (width, 4 * width), 1)
    copier = (row == (column // width) * half + lax.rem(column, half)).astype(BF16)
    piece = 8
    for start in range(0, 2 * leaves, piece):
        rows = window[start : start + piece].reshape(piece * r, width)
        copied = jnp.dot(rows, copier, preferred_element_type=F32).astype(BF16)
        for section in range(4):
            spread[start : start + piece, section * r : (section + 1) * r] = copied[
                :, section * width : (section + 1) * width
            ].reshape(piece, r, width)
    lane = lax.broadcasted_iota(jnp.int32, (4 * r, width), 1) // half
    for leaf in range(leaves):
        lhs, rhs = [], []
        for quad in range(nfar // 4):
            picked = None
            taken = []
            for q in range(4):
                f = quad * 4 + q
                source = spread[far[f, leaf] - origin]
                picked = source if q == 0 else jnp.where(lane >= q, source, picked)
                taken.append(couple(tables, far_couple[f, leaf]))
            lhs.append(picked)
            rhs.append(jnp.concatenate(split(jnp.concatenate(taken, axis=0)), axis=1))
        product = jnp.dot(
            jnp.concatenate(lhs, axis=1), jnp.concatenate(rhs, axis=0),
            preferred_element_type=F32,
        )
        product = product[: 2 * r] + product[2 * r :]
        out[leaf] = fold(product[:, :width] + product[:, width:])
    lhs, rhs = [], []
    for n in range(dev_list.shape[1]):
        place = jnp.bitwise_xor(dev_list[0, n] - group * lax.axis_size("dev"), member)
        lhs.append(halves(boxes[place][:, :k]))
        rhs.append(couple(tables, dev_couple[0, n]))
    listed_out[...] = fold(dot3(jnp.concatenate(lhs, axis=1), jnp.concatenate(rhs, axis=0)))
    for other in range(1, grp_couple.shape[0]):
        group_tables[(other - 1) * half : other * half] = couple(
            tables, grp_couple[group, jnp.bitwise_xor(group, other)]
        )


def final_kernel(
    steps, leaf_trans, dev_trans, near, far, listed, group_tables, groups, basis_t,
    trans_leaf, trans_dev, out_hbm, out, locals_, sems,
):
    leaves = near.shape[0]
    kinds, k, _ = trans_leaf.shape
    lhs = [halves(groups[other]) for other in range(groups.shape[0])]
    group_local = fold(dot3(jnp.concatenate(lhs, axis=1), group_tables[...]))
    box_local = dot3(group_local, trans_dev[dev_trans[0]], NT) + listed[...]
    by_kind = dot3(box_local, trans_leaf[...].reshape(kinds * k, k), NT)
    for kind in range(kinds):
        locals_[kind] = by_kind[:, kind * k : (kind + 1) * k]
    size = leaves // steps
    copies = []
    for i in range(steps):
        for leaf in range(i * size, (i + 1) * size):
            leaf_local = (locals_[leaf_trans[leaf]] + far[leaf]).astype(BF16)
            out[leaf] = near[leaf] + jnp.dot(
                leaf_local, basis_t[leaf], preferred_element_type=F32
            )
        piece = pl.ds(i * size, size)
        copies.append(pltpu.make_async_copy(out.at[piece], out_hbm.at[piece], sems.at[i]))
        copies[-1].start()
    for copy in copies:
        copy.wait()


def swap(x, axis, distance):
    return lax.ppermute(x, axis, [(i, i ^ distance) for i in range(lax.axis_size(axis))])


def cost(us):
    return pl.CostEstimate(flops=0, bytes_accessed=us * 3 * MIB, transcendentals=0)


def params(mib):
    return pltpu.CompilerParams(vmem_limit_bytes=mib * MIB)


def local(
    charges,
    leaf_basis,
    near_blocks,
    near_target,
    near_source,
    near_count,
    leaf_far,
    leaf_far_couple,
    leaf_trans,
    dev_trans,
    dev_list,
    dev_couple,
    grp_couple,
    trans_leaf,
    trans_dev,
    couple_table,
):
    leaves, r, panels = charges.shape
    k = leaf_basis.shape[2]
    margin = leaves // 2
    slots = near_blocks.shape[0]
    kinds = couple_table.shape[0]
    half = k // 2
    per_group = lax.axis_size("dev")
    devices = per_group * lax.axis_size("grp")
    basis_t = jnp.swapaxes(leaf_basis, 1, 2)
    shape = jax.ShapeDtypeStruct

    (
        moments, send_first, send_second, sums, leaf_kinds, dev_kind, own_charges, basis,
        leaf_maps, dev_maps, raw,
    ) = (
        pl.pallas_call(
            moment_kernel,
            out_shape=(
                shape((leaves, r, 2 * k), BF16),
                shape((margin + 1, 2 * r, panels), BF16),
                shape((margin, 2 * r, panels), BF16),
                shape((r, 2 * k), F32),
                shape(leaf_trans.shape, jnp.int32),
                shape(dev_trans.shape, jnp.int32),
                shape(charges.shape, BF16),
                shape(basis_t.shape, BF16),
                shape(trans_leaf.shape, F32),
                shape(trans_dev.shape, F32),
                shape((2, half, k, kinds), F32),
            ),
            in_specs=[HBM] * 7,
            out_specs=(VMEM,) * 4 + (SMEM,) * 2 + (VMEM,) * 5,
            scratch_shapes=[
                pltpu.VMEM((trans_leaf.shape[0], r, 2 * k), F32),
                pltpu.SemaphoreType.DMA((7,)),
            ],
            compiler_params=params(24),
            name="moments",
        )(
            pltpu.with_memory_space_constraint(leaf_trans, pltpu.HBM),
            dev_trans,
            pltpu.with_memory_space_constraint(charges, pltpu.HBM),
            pltpu.with_memory_space_constraint(basis_t, pltpu.HBM),
            pltpu.with_memory_space_constraint(trans_leaf, pltpu.HBM),
            pltpu.with_memory_space_constraint(trans_dev, pltpu.HBM),
            pltpu.with_memory_space_constraint(jnp.transpose(couple_table, (1, 2, 0)).reshape(2, half, k, kinds), pltpu.HBM),
        )
    )

    first = swap(send_first, "dev", 1)
    partners = [(i, i + 1) for i in range(1, devices - 1, 2)] + [(0, devices - 1)]
    second = lax.ppermute(send_second, AXES, partners + [(j, i) for i, j in partners])

    table_low, blocks = pl.pallas_call(
        table_kernel,
        out_shape=(
            shape((kinds * half // 2, 2 * k), F32),
            shape(near_blocks.shape, BF16),
        ),
        in_specs=[VMEM, HBM],
        out_specs=(VMEM, VMEM),
        scratch_shapes=[pltpu.SemaphoreType.DMA],
        compiler_params=params(24),
        cost_estimate=cost(3),
        name="table",
    )(raw, pltpu.with_memory_space_constraint(near_blocks, pltpu.HBM))

    peer = first[margin, :r].astype(F32) + first[margin, r:].astype(F32)
    pair = jnp.stack([sums, peer])
    pair, table_low, blocks, first, second = lax.optimization_barrier(
        (pair, table_low, blocks, first, second)
    )
    boxes = [pair] + [swap(pair, "dev", distance) for distance in range(2, per_group, 2)]

    steps = 4
    near, table_high = pl.pallas_call(
        functools.partial(near_kernel, steps),
        out_shape=(
            shape((leaves, r, panels), F32),
            shape((kinds * half // 2, 2 * k), F32),
        ),
        in_specs=[SMEM, SMEM, SMEM, VMEM, VMEM, VMEM, VMEM, VMEM],
        out_specs=(VMEM, VMEM),
        scratch_shapes=[
            pltpu.VMEM((2 * leaves, r, panels), BF16),
            pltpu.VMEM((leaves + 1, r, panels), F32),
        ],
        compiler_params=params(16),
        cost_estimate=cost(3),
        name="near",
    )(near_target, near_source, near_count, own_charges, first, second, blocks, raw)
    boxes = jnp.concatenate(boxes)
    boxes, near, table_high = lax.optimization_barrier((boxes, near, table_high))

    group_moment = jnp.sum(boxes[:, :, k:], axis=0)
    groups = [
        swap(group_moment, "grp", distance) for distance in range(1, lax.axis_size("grp"))
    ]
    tables = [x.reshape(kinds, half // 2, 2 * k) for x in (table_low, table_high)]
    far, listed, group_tables = pl.pallas_call(
        far_kernel,
        out_shape=(
            shape((leaves, r, k), F32),
            shape((r, k), F32),
            shape((len(groups) * half, 2 * k), F32),
        ),
        in_specs=[SMEM] * 5 + [VMEM] * 6,
        out_specs=(VMEM, VMEM, VMEM),
        scratch_shapes=[
            pltpu.VMEM((2 * leaves, r, 2 * k), BF16),
            pltpu.VMEM((2 * leaves, 4 * r, 2 * k), BF16),
        ],
        compiler_params=params(16),
        cost_estimate=cost(3),
        name="far",
    )(
        leaf_far.T, leaf_far_couple.T, dev_list, dev_couple, grp_couple, moments, first,
        second, *tables, boxes,
    )

    return pl.pallas_call(
        functools.partial(final_kernel, steps),
        out_shape=shape((leaves, r, panels), F32),
        in_specs=[SMEM, SMEM] + [VMEM] * 8,
        out_specs=HBM,
        scratch_shapes=[
            pltpu.VMEM((leaves, r, panels), F32),
            pltpu.VMEM((trans_leaf.shape[0], r, k), F32),
            pltpu.SemaphoreType.DMA((steps,)),
        ],
        compiler_params=params(16),
        name="final",
    )(
        leaf_kinds, dev_kind, near, far, listed, group_tables, jnp.stack(groups), basis,
        leaf_maps, dev_maps,
    )


def solution(mesh):
    leaf = P(AXES)
    return jax.shard_map(
        local,
        mesh=mesh,
        in_specs=(leaf,) * 12 + (P(),) * 4,
        out_specs=leaf,
        check_vma=False,
    )
```

time: 40.4 us -> 33.6 us (0.83)
  local copies, waits for them, and re-layouts: 7.33 us -> 0.04 us
  starting transfers between devices: 7.35 us -> 13 us
  waiting for transfers between devices: 6 us -> 2.95 us
  Pallas kernels: 17.9 us -> 15.9 us
    unnamed x30 -> x14, local copies, waits for them, and re-layouts: 7.33 us -> 0.04 us
    ppermute x5 -> x7, waiting for transfers between devices: 6 us -> 0.02 us  [swap(): lax.ppermute(x, axis, [(i, i ^ distance) for i in range(lax.axis_size(axi...]
    ppermute x5 -> x7, starting transfers between devices: 3.68 us -> 9.31 us  [swap(): lax.ppermute(x, axis, [(i, i ^ distance) for i in range(lax.axis_size(axi...]
    pallas_call x5 -> x4, Pallas kernels: 15.5 us -> 12 us  [the longest x1 3.44 us: local(): pl.pallas_call(functools.partial(near_kernel, steps), out_shape=(shape((l...]
    ppermute x1, waiting for transfers between devices: 0.01 us -> 2.93 us  [local(): lax.ppermute(send_second, AXES, partners + [(j, i) for i, j in partners])]
    pallas_call x1, Pallas kernels: 2.39 us -> 3.85 us  [local(): pl.pallas_call(moment_kernel, out_shape=(shape((leaves, r, 2 * k), BF16),...]
  transfers between devices with their start and end apart: 6 -> 8, of which waited for: 4 -> 1; matrix products, arithmetic and copies ran while one was open for 0% -> 0% of each run, Pallas kernels for 32% -> 28%
where the time goes in v3:
time: 33.6 us; the launch traced here: 33.5 us
  Pallas kernels  15.9 us (47%)
  starting transfers between devices  13 us (39%)
  waiting for transfers between devices  2.95 us (9%)
  between operations  1.5 us (4%)
    ppermute x7, starting transfers between devices, swap(): lax.ppermute(x, axis, [(i, i ^ distance) for i in range(lax.axis_size(axi...  9.31 us
    pallas_call x1, Pallas kernels, local(): pl.pallas_call(moment_kernel, out_shape=(shape((leaves, r, 2 * k), BF16),...  3.85 us
    ppermute x1, starting transfers between devices, local(): lax.ppermute(send_second, AXES, partners + [(j, i) for i, j in partners])  3.69 us
    pallas_call x1, Pallas kernels, local(): pl.pallas_call(functools.partial(near_kernel, steps), out_shape=(shape((l...  3.44 us
    pallas_call x1, Pallas kernels, local(): pl.pallas_call(far_kernel, out_shape=(shape((leaves, r, k), F32), shape((...  3.26 us
    ppermute x1, waiting for transfers between devices, local(): lax.ppermute(send_second, AXES, partners + [(j, i) for i, j in partners])  2.93 us
    pallas_call x1, Pallas kernels, local(): pl.pallas_call(functools.partial(final_kernel, steps), out_shape=shape((l...  2.81 us
    pallas_call x1, Pallas kernels, local(): pl.pallas_call(table_kernel, out_shape=(shape((kinds * half // 2, 2 * k),...  2.52 us
  transfers between devices with their start and end apart: 8, of which 1 were waited for; matrix products, arithmetic and copies ran while one was open for 0% of the time, Pallas kernels for 28%

profile of v3, /device:TPU:0, one launch (start us, length us, event | category | flops | bytes accessed | tf_op | source)
XLA Modules:
  0.0 33.5 jit_solution(18119723641082137656)
XLA Ops:
  0.7 3.9 %moments.1 = (bf16[32,16,128]{2,1,0:T(8,128)(2,1)S(1)}, bf16[17,32,128]{2,1,0:T(8,128)(2,1)S(1)}, bf16[16,32,128]{2,1,0:T(8,128)(2,1)S(1)}, f32[16,128]{1,0:T(8,...) custom-call(s32[32]{0:T(128)} %leaf_trans_hbm.1, ...), custom_call_target="tpu_custom_call" | custom-call | tf_op jit(solution)/shard_map/moments/pallas_call | solution.py:318
  4.5 3.0 %collective-permute-start = (bf16[17,32,128]{2,1,0:T(8,128)(2,1)S(1)}, bf16[17,32,128]{2,1,0:T(8,128)(2,1)S(1)}, u32[]{:S(2)}, u32[]{:S(2)}) collective-permute-start(bf16[17,32,128]{2,1,0:T(8,128)(2,1)S(1)} %get-tuple-element.34), channel_id=1, source_target_pairs={{0,1},{1,0},{2,3},{3,2},{4,5},{5,4},{6,7},{7,6},{8,9},{9,8},{10,11... | collective-permute-start | bytes 417800 | tf_op jit(solution)/shard_map/ppermute | solution.py:274
  7.5 3.7 %collective-permute-start.1 = (bf16[16,32,128]{2,1,0:T(8,128)(2,1)S(1)}, bf16[16,32,128]{2,1,0:T(8,128)(2,1)S(1)}, u32[]{:S(2)}, u32[]{:S(2)}) collective-permute-start(bf16[16,32,128]{2,1,0:T(8,128)(2,1)S(1)} %get-tuple-element.38), channel_id=1, source_target_pairs={{1,2},{3,4},{5,6},{7,8},{9,10},{11,12},{13,14},{15,16},{17,18},{19... | collective-permute-start | bytes 393224 | tf_op jit(solution)/shard_map/ppermute | solution.py:354
  11.2 0.0 copy-start.3
  11.2 0.0 copy-start.4
  11.2 2.5 %table.1 = (f32[5056,128]{1,0:T(8,128)S(1)}, bf16[160,128,128]{2,1,0:T(8,128)(2,1)S(1)}) custom-call(f32[2,32,64,316]{3,2,1,0:T(8,128)S(1)} %get-tuple-element.35.table, bf16[160,128,128]{2,1,0:T(8,128)(2,1)} %blocks_hbm.1), custom_call_target="tpu_custom_call" | custom-call | bytes 9437184 | tf_op jit(solution)/shard_map/table/pallas_call | solution.py:356
  13.7 0.0 collective-permute-done.first
  13.8 2.9 %collective-permute-done.1.second = bf16[16,32,128]{2,1,0:T(8,128)(2,1)S(1)} collective-permute-done((bf16[16,32,128]{2,1,0:T(8,128)(2,1)S(1)}, bf16[16,32,128]{2,1,0:T(8,128)(2,1)S(1)}, u32[]{:S(2)}, u32[]{:S(2)}) %collective-permute-start.1) | collective-permute-done | bytes 131104 | tf_op jit(solution)/shard_map/ppermute | solution.py:354
  16.7 1.2 %collective-permute-start.4 = (f32[2,16,128]{2,1,0:T(8,128)S(1)}, f32[2,16,128]{2,1,0:T(8,128)S(1)}, u32[]{:S(2)}, u32[]{:S(2)}) collective-permute-start(f32[2,16,128]{2,1,0:T(8,128)S(1)} %pad_maximum_fusion.2), channel_id=1, source_target_pairs={{0,6},{1,7},{2,4},{3,5},{4,2},{5,3},{6,0},{7,1},{8,14},{9,15},{10,... | collective-permute-start | bytes 49160 | tf_op jit(solution)/shard_map/ppermute | solution.py:274
  17.9 0.0 collective-permute-start.3
  17.9 3.2 %collective-permute-start.2 = (f32[2,16,128]{2,1,0:T(8,128)S(1)}, f32[2,16,128]{2,1,0:T(8,128)S(1)}, u32[]{:S(2)}, u32[]{:S(2)}) collective-permute-start(f32[2,16,128]{2,1,0:T(8,128)S(1)} %pad_maximum_fusion.2), channel_id=1, source_target_pairs={{0,2},{1,3},{2,0},{3,1},{4,6},{5,7},{6,4},{7,5},{8,10},{9,11},{10,... | collective-permute-start | bytes 49160 | tf_op jit(solution)/shard_map/ppermute | solution.py:274
  21.7 0.0 copy-done.3
  21.7 0.0 copy-done.4
  21.8 0.0 copy-start
  21.8 0.0 copy-start.1
  21.8 0.0 copy-start.2
  21.8 0.0 copy-start.5
  21.8 0.0 copy-start.6
  21.8 3.4 %near.1 = (f32[32,16,128]{2,1,0:T(8,128)S(1)}, f32[5056,128]{1,0:T(8,128)S(1)}) custom-call(s32[160]{0:T(256)S(1)} %copy-done.3, s32[160]{0:T(256)S(1)} %copy-done.4, s32[1]{0:T(128)S(6)} %copy.17.count, bf16[32,16,128]{2,1,0:T(8,128)(2,1)S(1)} %get-tuple-element.40.charges, bf16[17,32,128]{2,1,0:T(8,128)(2,1)S(1)} %collective-permute-done.first, ...), custom_call_target="tpu_custom_call" | custom-call | bytes 9437184 | tf_op jit(solution)/shard_map/near/pallas_call | solution.py:378
  25.3 0.0 collective-permute-done.4
  25.3 0.0 collective-permute-done.3
  25.3 0.0 collective-permute-done.2
  25.3 0.1 slice_reduce_fusion
  25.4 0.1 collective-permute-start.7
  25.5 0.6 %collective-permute-start.6 = (f32[16,64]{1,0:T(8,128)S(1)}, f32[16,64]{1,0:T(8,128)S(1)}, u32[]{:S(2)}, u32[]{:S(2)}) collective-permute-start(f32[16,64]{1,0:T(8,128)S(1)} %slice_reduce_fusion), channel_id=1, source_target_pairs={{0,16},{8,24},{16,0},{24,8},{1,17},{9,25},{17,1},{25,9},{2,18},{10... | collective-permute-start | bytes 12296 | tf_op jit(solution)/shard_map/ppermute | solution.py:274
  26.1 1.2 %collective-permute-start.5 = (f32[16,64]{1,0:T(8,128)S(1)}, f32[16,64]{1,0:T(8,128)S(1)}, u32[]{:S(2)}, u32[]{:S(2)}) collective-permute-start(f32[16,64]{1,0:T(8,128)S(1)} %slice_reduce_fusion), channel_id=1, source_target_pairs={{0,8},{8,0},{16,24},{24,16},{1,9},{9,1},{17,25},{25,17},{2,10},{10... | collective-permute-start | bytes 12296 | tf_op jit(solution)/shard_map/ppermute | solution.py:274
  27.3 0.0 copy-done
  27.3 0.0 copy-done.1
  27.3 0.0 copy-done.2
  27.3 0.0 copy-done.5
  27.3 0.0 copy-done.6
  27.4 3.3 %far.1 = (f32[32,16,64]{2,1,0:T(8,128)S(1)}, f32[16,64]{1,0:T(8,128)S(1)}, f32[96,128]{1,0:T(8,128)S(1)}) custom-call(s32[16,32]{1,0:T(8,128)S(1)} %bitcast.14, s32[16,32]{1,0:T(8,128)S(1)} %bitcast.15, s32[1,4]{1,0:T(1,128)S(1)} %copy-done.5, s32[1,4]{1,0:T(1,128)S(1)} %copy-done.6, s32[4,4]{1,0:T(4,128)S(1)} %copy-done.2, ...), custom_call_target="tpu_custom_call" | custom-call | bytes 9437184 | tf_op jit(solution)/shard_map/far/pallas_call | solution.py:402
  30.6 0.0 collective-permute-done.7
  30.6 0.0 collective-permute-done.6
  30.6 0.0 collective-permute-done.5
  30.7 2.8 %final.1 = f32[32,16,128]{2,1,0:T(8,128)} custom-call(s32[32]{0:T(128)S(1)} %get-tuple-element.31.leaf_trans, s32[1]{0:T(128)} %get-tuple-element.32.dev_trans, f32[32,16,128]{2,1,0:T(8,128)S(1)} %get-tuple-element.46.near, f32[32,16,64]{2,1,0:T(8,128)S(1)} %get-tuple-element.51.far, f32[16,64]{1,0:T(8,128)S(1)} %get-tuple-element.52.listed, ...), custom_call_target="tpu_custom_call" | custom-call | tf_op jit(solution)/shard_map/final/pallas_call | solution.py:423
  (4 shorter events, 0.0 us)
Async XLA Ops:
  4.5 9.2 %collective-permute-start = (bf16[17,32,128]{2,1,0:T(8,128)(2,1)S(1)}, bf16[17,32,128]{2,1,0:T(8,128)(2,1)S(1)}, u32[]{:S(2)}, u32[]{:S(2)}) collective-permute-start(bf16[17,32,128]{2,1,0:T(8,128)(2,1)S(1)} %get-tuple-element.34), channel_id=1, source_target_pairs={{0,1},{1,0},{2,3},{3,2},{4,5},{5,4},{6,7},{7,6},{8,9},{9,8},{10,11... | collective-permute-start | bytes 417800 | tf_op jit(solution)/shard_map/ppermute | solution.py:274
  7.5 9.2 %collective-permute-start.1 = (bf16[16,32,128]{2,1,0:T(8,128)(2,1)S(1)}, bf16[16,32,128]{2,1,0:T(8,128)(2,1)S(1)}, u32[]{:S(2)}, u32[]{:S(2)}) collective-permute-start(bf16[16,32,128]{2,1,0:T(8,128)(2,1)S(1)} %get-tuple-element.38), channel_id=1, source_target_pairs={{1,2},{3,4},{5,6},{7,8},{9,10},{11,12},{13,14},{15,16},{17,18},{19... | collective-permute-start | bytes 393224 | tf_op jit(solution)/shard_map/ppermute | solution.py:354
  11.2 10.5 %copy-start.3 = (s32[160]{0:T(256)S(1)}, s32[160]{0:T(256)}, u32[]{:S(2)}) copy-start(s32[160]{0:T(256)} %targets.1) | copy-start | bytes 1924
  11.2 10.5 %copy-start.4 = (s32[160]{0:T(256)S(1)}, s32[160]{0:T(256)}, u32[]{:S(2)}) copy-start(s32[160]{0:T(256)} %sources.1) | copy-start | bytes 1924
  16.7 8.6 %collective-permute-start.4 = (f32[2,16,128]{2,1,0:T(8,128)S(1)}, f32[2,16,128]{2,1,0:T(8,128)S(1)}, u32[]{:S(2)}, u32[]{:S(2)}) collective-permute-start(f32[2,16,128]{2,1,0:T(8,128)S(1)} %pad_maximum_fusion.2), channel_id=1, source_target_pairs={{0,6},{1,7},{2,4},{3,5},{4,2},{5,3},{6,0},{7,1},{8,14},{9,15},{10,... | collective-permute-start | bytes 49160 | tf_op jit(solution)/shard_map/ppermute | solution.py:274
  17.9 7.4 %collective-permute-start.3 = (f32[2,16,128]{2,1,0:T(8,128)S(1)}, f32[2,16,128]{2,1,0:T(8,128)S(1)}, u32[]{:S(2)}, u32[]{:S(2)}) collective-permute-start(f32[2,16,128]{2,1,0:T(8,128)S(1)} %pad_maximum_fusion.2), channel_id=1, source_target_pairs={{0,4},{1,5},{2,6},{3,7},{4,0},{5,1},{6,2},{7,3},{8,12},{9,13},{10,... | collective-permute-start | bytes 49160 | tf_op jit(solution)/shard_map/ppermute | solution.py:274
  17.9 7.4 %collective-permute-start.2 = (f32[2,16,128]{2,1,0:T(8,128)S(1)}, f32[2,16,128]{2,1,0:T(8,128)S(1)}, u32[]{:S(2)}, u32[]{:S(2)}) collective-permute-start(f32[2,16,128]{2,1,0:T(8,128)S(1)} %pad_maximum_fusion.2), channel_id=1, source_target_pairs={{0,2},{1,3},{2,0},{3,1},{4,6},{5,7},{6,4},{7,5},{8,10},{9,11},{10,... | collective-permute-start | bytes 49160 | tf_op jit(solution)/shard_map/ppermute | solution.py:274
  21.8 5.6 %copy-start = (s32[32,16]{0,1:T(8,128)S(1)}, s32[32,16]{0,1:T(8,128)}, u32[]{:S(2)}) copy-start(s32[32,16]{0,1:T(8,128)} %param.22) | copy-start | bytes 6148
  21.8 5.6 %copy-start.1 = (s32[32,16]{0,1:T(8,128)S(1)}, s32[32,16]{0,1:T(8,128)}, u32[]{:S(2)}) copy-start(s32[32,16]{0,1:T(8,128)} %param.23) | copy-start | bytes 6148
  21.8 5.6 %copy-start.2 = (s32[4,4]{1,0:T(4,128)S(1)}, s32[4,4]{1,0:T(4,128)}, u32[]{:S(2)}) copy-start(s32[4,4]{1,0:T(4,128)} %grp_couple.1) | copy-start | bytes 196
  21.8 5.5 %copy-start.5 = (s32[1,4]{1,0:T(1,128)S(1)}, s32[1,4]{1,0:T(1,128)}, u32[]{:S(2)}) copy-start(s32[1,4]{1,0:T(1,128)} %dev_list.1) | copy-start | bytes 52
  21.8 5.5 %copy-start.6 = (s32[1,4]{1,0:T(1,128)S(1)}, s32[1,4]{1,0:T(1,128)}, u32[]{:S(2)}) copy-start(s32[1,4]{1,0:T(1,128)} %dev_couple.1) | copy-start | bytes 52
  25.4 5.2 %collective-permute-start.7 = (f32[16,64]{1,0:T(8,128)S(1)}, f32[16,64]{1,0:T(8,128)S(1)}, u32[]{:S(2)}, u32[]{:S(2)}) collective-permute-start(f32[16,64]{1,0:T(8,128)S(1)} %slice_reduce_fusion), channel_id=1, source_target_pairs={{0,24},{8,16},{16,8},{24,0},{1,25},{9,17},{17,9},{25,1},{2,26},{10... | collective-permute-start | bytes 12296 | tf_op jit(solution)/shard_map/ppermute | solution.py:274
  25.5 5.1 %collective-permute-start.6 = (f32[16,64]{1,0:T(8,128)S(1)}, f32[16,64]{1,0:T(8,128)S(1)}, u32[]{:S(2)}, u32[]{:S(2)}) collective-permute-start(f32[16,64]{1,0:T(8,128)S(1)} %slice_reduce_fusion), channel_id=1, source_target_pairs={{0,16},{8,24},{16,0},{24,8},{1,17},{9,25},{17,1},{25,9},{2,18},{10... | collective-permute-start | bytes 12296 | tf_op jit(solution)/shard_map/ppermute | solution.py:274
  26.1 4.5 %collective-permute-start.5 = (f32[16,64]{1,0:T(8,128)S(1)}, f32[16,64]{1,0:T(8,128)S(1)}, u32[]{:S(2)}, u32[]{:S(2)}) collective-permute-start(f32[16,64]{1,0:T(8,128)S(1)} %slice_reduce_fusion), channel_id=1, source_target_pairs={{0,8},{8,0},{16,24},{24,16},{1,9},{9,1},{17,25},{25,17},{2,10},{10... | collective-permute-start | bytes 12296 | tf_op jit(solution)/shard_map/ppermute | solution.py:274

commit v4 on v3

--- a/solution.py
+++ b/solution.py
@@ -42,13 +42,13 @@
 
 
 def moment_kernel(
-    leaf_trans_hbm, dev_trans_hbm, charges_hbm, basis_hbm, trans_leaf_hbm, trans_dev_hbm, table_hbm,
-    moments, send_first, send_second, sums, leaf_trans, dev_trans, charges, basis_t,
+    leaf_trans_hbm, dev_trans, charges_hbm, basis_hbm, trans_leaf_hbm, trans_dev_hbm, table_hbm,
+    moments, send_first, send_second, sums, leaf_trans, dev_trans_out, charges, basis_t,
     trans_leaf, trans_dev, table, classes, sems,
 ):
     moves = [
         (charges_hbm, charges), (basis_hbm, basis_t), (leaf_trans_hbm, leaf_trans),
-        (trans_leaf_hbm, trans_leaf), (dev_trans_hbm, dev_trans), (trans_dev_hbm, trans_dev),
+        (trans_leaf_hbm, trans_leaf), (trans_dev_hbm, trans_dev),
         (table_hbm, table),
     ]
     copies = [
@@ -76,18 +76,16 @@
         classes[kind] = classes[kind] + twice
         high = twice.astype(BF16).astype(F32)
         moments[leaf] = jnp.where(left, high, twice - high).astype(BF16)
-    for copy in copies[3:6]:
+    for copy in copies[3:5]:
         copy.wait()
     lhs = [
         jnp.where(left, classes[kind], classes[kind + 1]) for kind in range(0, kinds, 2)
     ]
     box = dot3(jnp.concatenate(lhs, axis=1), trans_leaf[...].reshape(kinds * k, k))
+    dev_trans_out[0] = dev_trans[0]
     up = dot3(box, trans_dev[dev_trans[0]])
     both = jnp.concatenate([box, up], axis=1)
     sums[...] = both
-    high = both.astype(BF16)
-    send_first[margin, :r] = high
-    send_first[margin, r:] = (both - high.astype(F32)).astype(BF16)
 
     def fill(first_from, second_from):
         for leaf in range(margin):
@@ -104,30 +102,30 @@
     def _():
         fill(0, margin)
 
-    copies[6].wait()
-
-
-def relayout(table, row, out, count):
+    copies[5].wait()
+
+
+def relayout(table, row, out, place, count):
     kinds = table.shape[3]
     stacked = jnp.concatenate([table[0, row], table[1, row]], axis=0)
     for start in range(0, kinds, 128):
         width = min(128, kinds - start)
-        out[pl.ds(start * count + lax.rem(row, count), width, stride=count), :] = stacked[
+        out[pl.ds(start * count + place, width, stride=count), :] = stacked[
             :, start : start + width
         ].T
 
 
-def table_kernel(table, blocks_hbm, out, blocks, sem):
-    copy = pltpu.make_async_copy(blocks_hbm, blocks, sem)
-    copy.start()
-    rows = table.shape[1] // 2
-
-    def step(row, carry):
-        relayout(table, row, out, rows)
+def relayout_rows(table, out, begin, rows):
+    def step(place, carry):
+        relayout(table, begin + place, out, place, rows)
         return carry
 
     lax.fori_loop(0, rows, step, 0, unroll=8)
-    copy.wait()
+
+
+def table_kernel(rows, count, table, out, count_out):
+    count_out[0] = count[0]
+    relayout_rows(table, out, 0, rows)
 
 
 def halo_places(leaves):
@@ -141,13 +139,12 @@
 
 
 def near_kernel(
-    steps, targets, sources, count, charges, first, second, blocks, table, out, table_out,
+    steps, begin, rows, targets, sources, count, charges, first, second, blocks, table, out, table_out,
     window, total,
 ):
     chunk = blocks.shape[0] // steps
     leaves, r, panels = charges.shape
     margin = leaves // 2
-    rows = table.shape[1] // 2
     live = count[0]
     leaf_start = first_leaf(leaves)
     first_at, second_at = halo_places(leaves)
@@ -170,7 +167,8 @@
             )
             products += [both[:r, :panels], both[r:, panels:]]
         for u in range(rows // steps):
-            relayout(table, rows + index * (rows // steps) + u, table_out, rows)
+            place = index * (rows // steps) + u
+            relayout(table, begin + place, table_out, place, rows)
         for u in range(chunk):
             slot = base + u
             row = jnp.where(slot < live, targets[slot] - leaf_start, leaves)
@@ -186,16 +184,15 @@
 
 
 def far_kernel(
-    far, far_couple, dev_list, dev_couple, grp_couple, moments, first, second, table_low,
-    table_high, boxes, out, listed_out, group_tables, window, spread,
+    parts, far, far_couple, dev_couple, grp_couple, moments, first, second, *rest
 ):
+    tables = rest[:parts]
+    out, box_tables, window, spread = rest[parts:]
     leaves, r, width = moments.shape
     margin = leaves // 2
     k, half = width // 2, width // 4
     nfar = far.shape[0]
-    tables = (table_low, table_high)
     group = lax.axis_index("grp")
-    member = lax.axis_index("dev")
     origin = first_leaf(leaves) - margin
     first_at, second_at = halo_places(leaves)
     window[pl.ds(margin, leaves)] = moments[...]
@@ -231,27 +228,32 @@
         )
         product = product[: 2 * r] + product[2 * r :]
         out[leaf] = fold(product[:, :width] + product[:, width:])
-    lhs, rhs = [], []
-    for n in range(dev_list.shape[1]):
-        place = jnp.bitwise_xor(dev_list[0, n] - group * lax.axis_size("dev"), member)
-        lhs.append(halves(boxes[place][:, :k]))
-        rhs.append(couple(tables, dev_couple[0, n]))
-    listed_out[...] = fold(dot3(jnp.concatenate(lhs, axis=1), jnp.concatenate(rhs, axis=0)))
-    for other in range(1, grp_couple.shape[0]):
-        group_tables[(other - 1) * half : other * half] = couple(
-            tables, grp_couple[group, jnp.bitwise_xor(group, other)]
-        )
+    wanted = [
+        grp_couple[group, jnp.bitwise_xor(group, other)]
+        for other in range(1, grp_couple.shape[0])
+    ] + [dev_couple[0, n] for n in range(dev_couple.shape[1])]
+    for i, kind in enumerate(wanted):
+        box_tables[i * half : (i + 1) * half] = couple(tables, kind)
 
 
 def final_kernel(
-    steps, leaf_trans, dev_trans, near, far, listed, group_tables, groups, basis_t,
+    steps, leaf_trans, dev_trans, dev_list, near, far, box_tables, boxes, groups, basis_t,
     trans_leaf, trans_dev, out_hbm, out, locals_, sems,
 ):
     leaves = near.shape[0]
     kinds, k, _ = trans_leaf.shape
-    lhs = [halves(groups[other]) for other in range(groups.shape[0])]
-    group_local = fold(dot3(jnp.concatenate(lhs, axis=1), group_tables[...]))
-    box_local = dot3(group_local, trans_dev[dev_trans[0]], NT) + listed[...]
+    others = groups.shape[0] - 1
+    group = lax.axis_index("grp")
+    member = lax.axis_index("dev")
+    split_at = others * (k // 2)
+    lhs = [halves(groups[other + 1]) for other in range(others)]
+    group_local = fold(dot3(jnp.concatenate(lhs, axis=1), box_tables[:split_at]))
+    lhs = []
+    for n in range(dev_list.shape[1]):
+        place = jnp.bitwise_xor(dev_list[0, n] - group * lax.axis_size("dev"), member)
+        lhs.append(halves(boxes[place]))
+    listed = fold(dot3(jnp.concatenate(lhs, axis=1), box_tables[split_at:]))
+    box_local = dot3(group_local, trans_dev[dev_trans[0]], NT) + listed
     by_kind = dot3(box_local, trans_leaf[...].reshape(kinds * k, k), NT)
     for kind in range(kinds):
         locals_[kind] = by_kind[:, kind * k : (kind + 1) * k]
@@ -319,22 +321,22 @@
             moment_kernel,
             out_shape=(
                 shape((leaves, r, 2 * k), BF16),
-                shape((margin + 1, 2 * r, panels), BF16),
+                shape((margin, 2 * r, panels), BF16),
                 shape((margin, 2 * r, panels), BF16),
                 shape((r, 2 * k), F32),
                 shape(leaf_trans.shape, jnp.int32),
-                shape(dev_trans.shape, jnp.int32),
+                shape((8,), jnp.int32),
                 shape(charges.shape, BF16),
                 shape(basis_t.shape, BF16),
                 shape(trans_leaf.shape, F32),
                 shape(trans_dev.shape, F32),
                 shape((2, half, k, kinds), F32),
             ),
-            in_specs=[HBM] * 7,
+            in_specs=[HBM, SMEM] + [HBM] * 5,
             out_specs=(VMEM,) * 4 + (SMEM,) * 2 + (VMEM,) * 5,
             scratch_shapes=[
                 pltpu.VMEM((trans_leaf.shape[0], r, 2 * k), F32),
-                pltpu.SemaphoreType.DMA((7,)),
+                pltpu.SemaphoreType.DMA((6,)),
             ],
             compiler_params=params(24),
             name="moments",
@@ -349,65 +351,71 @@
         )
     )
 
-    first = swap(send_first, "dev", 1)
+    peer = swap(sums, "dev", 1)
     partners = [(i, i + 1) for i in range(1, devices - 1, 2)] + [(0, devices - 1)]
     second = lax.ppermute(send_second, AXES, partners + [(j, i) for i, j in partners])
-
-    table_low, blocks = pl.pallas_call(
-        table_kernel,
-        out_shape=(
-            shape((kinds * half // 2, 2 * k), F32),
-            shape(near_blocks.shape, BF16),
-        ),
-        in_specs=[VMEM, HBM],
-        out_specs=(VMEM, VMEM),
-        scratch_shapes=[pltpu.SemaphoreType.DMA],
-        compiler_params=params(24),
+    first = swap(send_first, "dev", 1)
+    boxes = jnp.stack([sums[:, :k], peer[:, :k]])
+    groups = (sums + peer)[None, :, k:]
+    boxes, groups, raw = lax.optimization_barrier((boxes, groups, raw))
+
+    groups = jnp.concatenate([groups, swap(groups, "grp", 1)])
+    high_rows = half // 4
+    low_rows = half - high_rows
+    table_low, live = pl.pallas_call(
+        functools.partial(table_kernel, low_rows),
+        out_shape=(shape((kinds * low_rows, 2 * k), F32), shape((8,), jnp.int32)),
+        in_specs=[SMEM, VMEM],
+        out_specs=(VMEM, SMEM),
+        compiler_params=params(16),
         cost_estimate=cost(3),
         name="table",
-    )(raw, pltpu.with_memory_space_constraint(near_blocks, pltpu.HBM))
-
-    peer = first[margin, :r].astype(F32) + first[margin, r:].astype(F32)
-    pair = jnp.stack([sums, peer])
-    pair, table_low, blocks, first, second = lax.optimization_barrier(
-        (pair, table_low, blocks, first, second)
-    )
-    boxes = [pair] + [swap(pair, "dev", distance) for distance in range(2, per_group, 2)]
+    )(near_count, raw)
+    groups, table_low, live, first, second = lax.optimization_barrier(
+        (groups, table_low, live, first, second)
+    )
+    for distance in [2 << i for i in range((lax.axis_size("grp") // 2).bit_length() - 1)]:
+        groups = jnp.concatenate([groups, swap(groups, "grp", distance)])
 
     steps = 4
-    near, table_high = pl.pallas_call(
-        functools.partial(near_kernel, steps),
-        out_shape=(
-            shape((leaves, r, panels), F32),
-            shape((kinds * half // 2, 2 * k), F32),
-        ),
-        in_specs=[SMEM, SMEM, SMEM, VMEM, VMEM, VMEM, VMEM, VMEM],
+
+    def near_part():
+        return pl.pallas_call(
+            functools.partial(near_kernel, steps, low_rows, high_rows),
+            out_shape=(
+                shape((leaves, r, panels), F32),
+                shape((kinds * high_rows, 2 * k), F32),
+            ),
+            in_specs=[SMEM, SMEM, SMEM, VMEM, VMEM, VMEM, VMEM, VMEM],
+            out_specs=(VMEM, VMEM),
+            scratch_shapes=[
+                pltpu.VMEM((2 * leaves, r, panels), BF16),
+                pltpu.VMEM((leaves + 1, r, panels), F32),
+            ],
+            compiler_params=params(16),
+            cost_estimate=cost(3),
+            name="near",
+        )(
+            near_target, near_source, live, own_charges, first, second,
+            near_blocks, raw,
+        )
+
+    near, table_high = near_part()
+    boxes, groups, near, table_high = lax.optimization_barrier((boxes, groups, near, table_high))
+    parts = jnp.concatenate([boxes, groups])
+    got = [swap(parts, "dev", distance) for distance in range(2, per_group, 2)]
+    boxes = jnp.concatenate([boxes] + [part[:2] for part in got])
+    groups = sum([part[2:] for part in got], start=groups)
+
+    tables = [
+        x.reshape(kinds, x.shape[0] // kinds, 2 * k) for x in (table_low, table_high)
+    ]
+    wanted = groups.shape[0] - 1 + dev_couple.shape[1]
+    far, box_tables = pl.pallas_call(
+        functools.partial(far_kernel, len(tables)),
+        out_shape=(shape((leaves, r, k), F32), shape((wanted * half, 2 * k), F32)),
+        in_specs=[SMEM] * 4 + [VMEM] * (3 + len(tables)),
         out_specs=(VMEM, VMEM),
-        scratch_shapes=[
-            pltpu.VMEM((2 * leaves, r, panels), BF16),
-            pltpu.VMEM((leaves + 1, r, panels), F32),
-        ],
-        compiler_params=params(16),
-        cost_estimate=cost(3),
-        name="near",
-    )(near_target, near_source, near_count, own_charges, first, second, blocks, raw)
-    boxes = jnp.concatenate(boxes)
-    boxes, near, table_high = lax.optimization_barrier((boxes, near, table_high))
-
-    group_moment = jnp.sum(boxes[:, :, k:], axis=0)
-    groups = [
-        swap(group_moment, "grp", distance) for distance in range(1, lax.axis_size("grp"))
-    ]
-    tables = [x.reshape(kinds, half // 2, 2 * k) for x in (table_low, table_high)]
-    far, listed, group_tables = pl.pallas_call(
-        far_kernel,
-        out_shape=(
-            shape((leaves, r, k), F32),
-            shape((r, k), F32),
-            shape((len(groups) * half, 2 * k), F32),
-        ),
-        in_specs=[SMEM] * 5 + [VMEM] * 6,
-        out_specs=(VMEM, VMEM, VMEM),
         scratch_shapes=[
             pltpu.VMEM((2 * leaves, r, 2 * k), BF16),
             pltpu.VMEM((2 * leaves, 4 * r, 2 * k), BF16),
@@ -416,14 +424,13 @@
         cost_estimate=cost(3),
         name="far",
     )(
-        leaf_far.T, leaf_far_couple.T, dev_list, dev_couple, grp_couple, moments, first,
-        second, *tables, boxes,
+        leaf_far.T, leaf_far_couple.T, dev_couple, grp_couple, moments, first, second, *tables
     )
 
     return pl.pallas_call(
         functools.partial(final_kernel, steps),
         out_shape=shape((leaves, r, panels), F32),
-        in_specs=[SMEM, SMEM] + [VMEM] * 8,
+        in_specs=[SMEM] * 3 + [VMEM] * 8,
         out_specs=HBM,
         scratch_shapes=[
             pltpu.VMEM((leaves, r, panels), F32),
@@ -433,7 +440,7 @@
         compiler_params=params(16),
         name="final",
     )(
-        leaf_kinds, dev_kind, near, far, listed, group_tables, jnp.stack(groups), basis,
+        leaf_kinds, dev_kind, dev_list, near, far, box_tables, boxes, groups, basis,
         leaf_maps, dev_maps,
     )
 

time: 33.6 us -> 31.9 us (0.949)
  Pallas kernels: 15.9 us -> 14 us
  starting transfers between devices: 13 us -> 14.9 us
  waiting for transfers between devices: 2.95 us -> 1.08 us
    ppermute x1, waiting for transfers between devices: 2.93 us -> 1.07 us  [local(): lax.ppermute(send_second, AXES, partners + [(j, i) for i, j in partners])]
    pallas_call x3, Pallas kernels: 9.22 us -> 7.82 us  [the longest x1 3.38 us: local(): pl.pallas_call(functools.partial(far_kernel, len(tables)), out_shape=(sha...]
    ppermute x1, starting transfers between devices: 3.69 us -> 4.82 us  [local(): lax.ppermute(send_second, AXES, partners + [(j, i) for i, j in partners])]
    ppermute x7, starting transfers between devices: 9.31 us -> 10.1 us  [swap(): lax.ppermute(x, axis, [(i, i ^ distance) for i in range(lax.axis_size(axi...]
    pallas_call x1, Pallas kernels: 2.81 us -> 2.18 us  [local(): pl.pallas_call(functools.partial(final_kernel, steps), out_shape=shape((l...]
  transfers between devices with their start and end apart: 8 -> 8, of which waited for: 1 -> 1; matrix products, arithmetic and copies ran while one was open for 0% -> 0% of each run, Pallas kernels for 28% -> 25%
where the time goes in v4:
time: 31.9 us; the launch traced here: 31.7 us
  starting transfers between devices  14.9 us (47%)
  Pallas kernels  14 us (44%)
  between operations  1.54 us (5%)
  waiting for transfers between devices  1.08 us (3%)
    ppermute x7, starting transfers between devices, swap(): lax.ppermute(x, axis, [(i, i ^ distance) for i in range(lax.axis_size(axi...  10.1 us
    ppermute x1, starting transfers between devices, local(): lax.ppermute(send_second, AXES, partners + [(j, i) for i, j in partners])  4.82 us
    pallas_call x1, Pallas kernels, local(): pl.pallas_call(moment_kernel, out_shape=(shape((leaves, r, 2 * k), BF16),...  3.97 us
    pallas_call x1, Pallas kernels, local(): pl.pallas_call(functools.partial(far_kernel, len(tables)), out_shape=(sha...  3.38 us
    pallas_call x1, Pallas kernels, near_part(): pl.pallas_call(functools.partial(near_kernel, steps, low_rows, high_rows)...  2.87 us
    pallas_call x1, Pallas kernels, local(): pl.pallas_call(functools.partial(final_kernel, steps), out_shape=shape((l...  2.18 us
    pallas_call x1, Pallas kernels, local(): pl.pallas_call(functools.partial(table_kernel, low_rows), out_shape=(shap...  1.56 us
    ppermute x1, waiting for transfers between devices, local(): lax.ppermute(send_second, AXES, partners + [(j, i) for i, j in partners])  1.07 us
  transfers between devices with their start and end apart: 8, of which 1 were waited for; matrix products, arithmetic and copies ran while one was open for 0% of the time, Pallas kernels for 25%

profile of v4, /device:TPU:0, one launch (start us, length us, event | category | flops | bytes accessed | tf_op | source)
XLA Modules:
  0.0 31.7 jit_solution(8226690288128141475)
XLA Ops:
  0.7 0.0 slice-start
  0.7 0.0 slice-start.1
  0.7 0.0 copy-start.3
  0.7 0.0 copy-start.4
  0.7 4.0 %moments.1 = (bf16[32,16,128]{2,1,0:T(8,128)(2,1)S(1)}, bf16[16,32,128]{2,1,0:T(8,128)(2,1)S(1)}, bf16[16,32,128]{2,1,0:T(8,128)(2,1)S(1)}, f32[16,128]{1,0:T(8,...) custom-call(s32[32]{0:T(128)} %leaf_trans_hbm.1, ...), custom_call_target="tpu_custom_call" | custom-call | tf_op jit(solution)/shard_map/moments/pallas_call | solution.py:320
  4.7 3.0 %collective-permute-start = (f32[16,128]{1,0:T(8,128)S(1)}, f32[16,128]{1,0:T(8,128)S(1)}, u32[]{:S(2)}, u32[]{:S(2)}) collective-permute-start(f32[16,128]{1,0:T(8,128)S(1)} %get-tuple-element.36), channel_id=1, source_target_pairs={{0,1},{1,0},{2,3},{3,2},{4,5},{5,4},{6,7},{7,6},{8,9},{9,8},{10,11... | collective-permute-start | bytes 24584 | tf_op jit(solution)/shard_map/ppermute | solution.py:276
  7.7 0.1 collective-permute-start.2
  7.8 4.8 %collective-permute-start.3 = (bf16[16,32,128]{2,1,0:T(8,128)(2,1)S(1)}, bf16[16,32,128]{2,1,0:T(8,128)(2,1)S(1)}, u32[]{:S(2)}, u32[]{:S(2)}) collective-permute-start(bf16[16,32,128]{2,1,0:T(8,128)(2,1)S(1)} %get-tuple-element.44), channel_id=1, source_target_pairs={{1,2},{3,4},{5,6},{7,8},{9,10},{11,12},{13,14},{15,16},{17,18},{19... | collective-permute-start | bytes 393224 | tf_op jit(solution)/shard_map/ppermute | solution.py:356
  12.6 0.0 collective-permute-done
  12.6 0.1 fusion
  12.7 0.3 collective-permute-start.1
  13.6 1.6 %table.1 = (f32[7584,128]{1,0:T(8,128)S(1)}, s32[8]{0:T(128)S(1)}) custom-call(s32[1]{0:T(128)S(6)} %copy.18.count, f32[2,32,64,316]{3,2,1,0:T(8,128)S(1)} %get-tuple-element.40.table), custom_call_target="tpu_custom_call" | custom-call | bytes 9437184 | tf_op jit(solution)/shard_map/table/pallas_call | solution.py:365
  15.2 0.0 collective-permute-done.1
  15.2 0.0 collective-permute-done.2.first
  15.2 1.1 %collective-permute-done.3.second = bf16[16,32,128]{2,1,0:T(8,128)(2,1)S(1)} collective-permute-done((bf16[16,32,128]{2,1,0:T(8,128)(2,1)S(1)}, bf16[16,32,128]{2,1,0:T(8,128)(2,1)S(1)}, u32[]{:S(2)}, u32[]{:S(2)}) %collective-permute-start.3) | collective-permute-done | bytes 131104 | tf_op jit(solution)/shard_map/ppermute | solution.py:356
  16.3 2.3 %collective-permute-start.4 = (f32[2,16,64]{2,1,0:T(8,128)S(1)}, f32[2,16,64]{2,1,0:T(8,128)S(1)}, u32[]{:S(2)}, u32[]{:S(2)}) collective-permute-start(f32[2,16,64]{2,1,0:T(8,128)S(1)} %pad_maximum_fusion.3), channel_id=1, source_target_pairs={{0,16},{8,24},{16,0},{24,8},{1,17},{9,25},{17,1},{25,9},{2,18},{10... | collective-permute-start | bytes 24584 | tf_op jit(solution)/shard_map/ppermute | solution.py:276
  18.6 0.0 slice-done
  18.6 0.0 slice-done.1
  18.6 0.0 copy-done.3
  18.6 0.0 copy-done.4
  18.6 0.0 copy-start
  18.6 0.0 copy-start.1
  18.6 0.0 copy-start.2
  18.6 0.0 copy-start.6
  18.6 2.9 %near.1 = (f32[32,16,128]{2,1,0:T(8,128)S(1)}, f32[2528,128]{1,0:T(8,128)S(1)}) custom-call(s32[160]{0:T(256)S(1)} %copy-done.3, s32[160]{0:T(256)S(1)} %copy-done.4, s32[8]{0:T(128)S(1)} %get-tuple-element.46.count, bf16[32,16,128]{2,1,0:T(8,128)(2,1)S(1)} %get-tuple-element.47.charges, bf16[16,32,128]{2,1,0:T(8,128)(2,1)S(1)} %collective-permute-done.2.first, ...), custom_call_target="tpu_custom_call" | custom-call | bytes 9437184 | tf_op jit(solution)/shard_map/near/pallas_call | solution.py:383
  21.5 0.0 copy-start.5
  21.5 0.0 collective-permute-done.4
  21.6 2.1 %collective-permute-start.7 = (f32[6,16,64]{2,1,0:T(8,128)S(1)}, f32[6,16,64]{2,1,0:T(8,128)S(1)}, u32[]{:S(2)}, u32[]{:S(2)}) collective-permute-start(f32[6,16,64]{2,1,0:T(8,128)S(1)} %constant_dynamic-update-slice_fusion), channel_id=1, source_target_pairs={{0,6},{1,7},{2,4},{3,5},{4,2},{5,3},{6,0},{7,1},{8,14},{9,15},{10,... | collective-permute-start | bytes 73736 | tf_op jit(solution)/shard_map/ppermute | solution.py:276
  23.6 0.0 collective-permute-start.6
  23.7 2.4 %collective-permute-start.5 = (f32[6,16,64]{2,1,0:T(8,128)S(1)}, f32[6,16,64]{2,1,0:T(8,128)S(1)}, u32[]{:S(2)}, u32[]{:S(2)}) collective-permute-start(f32[6,16,64]{2,1,0:T(8,128)S(1)} %constant_dynamic-update-slice_fusion), channel_id=1, source_target_pairs={{0,2},{1,3},{2,0},{3,1},{4,6},{5,7},{6,4},{7,5},{8,10},{9,11},{10,... | collective-permute-start | bytes 73736 | tf_op jit(solution)/shard_map/ppermute | solution.py:276
  26.0 0.0 copy-done
  26.0 0.0 copy-done.1
  26.0 0.0 copy-done.2
  26.0 0.0 copy-done.6
  26.0 3.4 %far.1 = (f32[32,16,64]{2,1,0:T(8,128)S(1)}, f32[224,128]{1,0:T(8,128)S(1)}) custom-call(s32[16,32]{1,0:T(8,128)S(1)} %bitcast.18, s32[16,32]{1,0:T(8,128)S(1)} %bitcast.19, s32[1,4]{1,0:T(1,128)S(1)} %copy-done.6, s32[4,4]{1,0:T(4,128)S(1)} %copy-done.2, bf16[32,16,128]{2,1,0:T(8,128)(2,1)S(1)} %get-tuple-element.53.moments, ...), custom_call_target="tpu_custom_call" | custom-call | bytes 9437184 | tf_op jit(solution)/shard_map/far/pallas_call | solution.py:414
  29.4 0.0 collective-permute-done.7
  29.4 0.0 collective-permute-done.6
  29.5 0.0 collective-permute-done.5
  29.5 0.0 copy-done.5
  29.5 2.2 %final.1 = f32[32,16,128]{2,1,0:T(8,128)} custom-call(s32[32]{0:T(128)S(1)} %get-tuple-element.34.leaf_trans, s32[8]{0:T(128)S(1)} %get-tuple-element.35.dev_trans, s32[1,4]{1,0:T(1,128)S(1)} %copy-done.5, f32[32,16,128]{2,1,0:T(8,128)S(1)} %get-tuple-element.52.near, f32[32,16,64]{2,1,0:T(8,128)S(1)} %get-tuple-element.56.far, ...), custom_call_target="tpu_custom_call" | custom-call | tf_op jit(solution)/shard_map/final/pallas_call | solution.py:430
  (11 shorter events, 0.1 us)
Async XLA Ops:
  0.7 17.9 %slice-start = ((s8[5242880]{0:T(1024)(128)(4,1)}), s8[4194304]{0:T(1024)(128)(4,1)S(1)}, s32[]{:S(2)}) async-start(s8[5242880]{0:T(1024)(128)(4,1)} %bitcast.14), calls=%async_computation | async-start | bytes 8388608
  0.7 17.9 %slice-start.1 = ((s8[5242880]{0:T(1024)(128)(4,1)}), s8[1048576]{0:T(1024)(128)(4,1)S(1)}, s32[]{:S(2)}) async-start(s8[5242880]{0:T(1024)(128)(4,1)} %bitcast.14), calls=%async_computation.1 | async-start | bytes 2097152
  0.7 17.9 %copy-start.3 = (s32[160]{0:T(256)S(1)}, s32[160]{0:T(256)}, u32[]{:S(2)}) copy-start(s32[160]{0:T(256)} %targets.1) | copy-start | bytes 1924
  0.7 17.9 %copy-start.4 = (s32[160]{0:T(256)S(1)}, s32[160]{0:T(256)}, u32[]{:S(2)}) copy-start(s32[160]{0:T(256)} %sources.1) | copy-start | bytes 1924
  4.7 7.9 %collective-permute-start = (f32[16,128]{1,0:T(8,128)S(1)}, f32[16,128]{1,0:T(8,128)S(1)}, u32[]{:S(2)}, u32[]{:S(2)}) collective-permute-start(f32[16,128]{1,0:T(8,128)S(1)} %get-tuple-element.36), channel_id=1, source_target_pairs={{0,1},{1,0},{2,3},{3,2},{4,5},{5,4},{6,7},{7,6},{8,9},{9,8},{10,11... | collective-permute-start | bytes 24584 | tf_op jit(solution)/shard_map/ppermute | solution.py:276
  7.7 7.5 %collective-permute-start.2 = (bf16[16,32,128]{2,1,0:T(8,128)(2,1)S(1)}, bf16[16,32,128]{2,1,0:T(8,128)(2,1)S(1)}, u32[]{:S(2)}, u32[]{:S(2)}) collective-permute-start(bf16[16,32,128]{2,1,0:T(8,128)(2,1)S(1)} %get-tuple-element.43), channel_id=1, source_target_pairs={{0,1},{1,0},{2,3},{3,2},{4,5},{5,4},{6,7},{7,6},{8,9},{9,8},{10,11... | collective-permute-start | bytes 393224 | tf_op jit(solution)/shard_map/ppermute | solution.py:276
  7.8 8.5 %collective-permute-start.3 = (bf16[16,32,128]{2,1,0:T(8,128)(2,1)S(1)}, bf16[16,32,128]{2,1,0:T(8,128)(2,1)S(1)}, u32[]{:S(2)}, u32[]{:S(2)}) collective-permute-start(bf16[16,32,128]{2,1,0:T(8,128)(2,1)S(1)} %get-tuple-element.44), channel_id=1, source_target_pairs={{1,2},{3,4},{5,6},{7,8},{9,10},{11,12},{13,14},{15,16},{17,18},{19... | collective-permute-start | bytes 393224 | tf_op jit(solution)/shard_map/ppermute | solution.py:356
  12.7 2.5 %collective-permute-start.1 = (f32[1,16,64]{2,1,0:T(8,128)S(1)}, f32[1,16,64]{2,1,0:T(8,128)S(1)}, u32[]{:S(2)}, u32[]{:S(2)}) collective-permute-start(f32[1,16,64]{2,1,0:T(8,128)S(1)} %get-tuple-element.39), channel_id=1, source_target_pairs={{0,8},{8,0},{16,24},{24,16},{1,9},{9,1},{17,25},{25,17},{2,10},{10... | collective-permute-start | bytes 12296 | tf_op jit(solution)/shard_map/ppermute | solution.py:276
  16.3 5.3 %collective-permute-start.4 = (f32[2,16,64]{2,1,0:T(8,128)S(1)}, f32[2,16,64]{2,1,0:T(8,128)S(1)}, u32[]{:S(2)}, u32[]{:S(2)}) collective-permute-start(f32[2,16,64]{2,1,0:T(8,128)S(1)} %pad_maximum_fusion.3), channel_id=1, source_target_pairs={{0,16},{8,24},{16,0},{24,8},{1,17},{9,25},{17,1},{25,9},{2,18},{10... | collective-permute-start | bytes 24584 | tf_op jit(solution)/shard_map/ppermute | solution.py:276
  18.6 7.4 %copy-start = (s32[32,16]{0,1:T(8,128)S(1)}, s32[32,16]{0,1:T(8,128)}, u32[]{:S(2)}) copy-start(s32[32,16]{0,1:T(8,128)} %param.22) | copy-start | bytes 6148
  18.6 7.4 %copy-start.1 = (s32[32,16]{0,1:T(8,128)S(1)}, s32[32,16]{0,1:T(8,128)}, u32[]{:S(2)}) copy-start(s32[32,16]{0,1:T(8,128)} %param.23) | copy-start | bytes 6148
  18.6 7.4 %copy-start.2 = (s32[4,4]{1,0:T(4,128)S(1)}, s32[4,4]{1,0:T(4,128)}, u32[]{:S(2)}) copy-start(s32[4,4]{1,0:T(4,128)} %grp_couple.1) | copy-start | bytes 196
  18.6 7.4 %copy-start.6 = (s32[1,4]{1,0:T(1,128)S(1)}, s32[1,4]{1,0:T(1,128)}, u32[]{:S(2)}) copy-start(s32[1,4]{1,0:T(1,128)} %dev_couple.1) | copy-start | bytes 52
  21.5 8.0 %copy-start.5 = (s32[1,4]{1,0:T(1,128)S(1)}, s32[1,4]{1,0:T(1,128)}, u32[]{:S(2)}) copy-start(s32[1,4]{1,0:T(1,128)} %dev_list.1) | copy-start | bytes 52
  21.6 7.9 %collective-permute-start.7 = (f32[6,16,64]{2,1,0:T(8,128)S(1)}, f32[6,16,64]{2,1,0:T(8,128)S(1)}, u32[]{:S(2)}, u32[]{:S(2)}) collective-permute-start(f32[6,16,64]{2,1,0:T(8,128)S(1)} %constant_dynamic-update-slice_fusion), channel_id=1, source_target_pairs={{0,6},{1,7},{2,4},{3,5},{4,2},{5,3},{6,0},{7,1},{8,14},{9,15},{10,... | collective-permute-start | bytes 73736 | tf_op jit(solution)/shard_map/ppermute | solution.py:276
  23.6 5.8 %collective-permute-start.6 = (f32[6,16,64]{2,1,0:T(8,128)S(1)}, f32[6,16,64]{2,1,0:T(8,128)S(1)}, u32[]{:S(2)}, u32[]{:S(2)}) collective-permute-start(f32[6,16,64]{2,1,0:T(8,128)S(1)} %constant_dynamic-update-slice_fusion), channel_id=1, source_target_pairs={{0,4},{1,5},{2,6},{3,7},{4,0},{5,1},{6,2},{7,3},{8,12},{9,13},{10,... | collective-permute-start | bytes 73736 | tf_op jit(solution)/shard_map/ppermute | solution.py:276
  23.7 5.8 %collective-permute-start.5 = (f32[6,16,64]{2,1,0:T(8,128)S(1)}, f32[6,16,64]{2,1,0:T(8,128)S(1)}, u32[]{:S(2)}, u32[]{:S(2)}) collective-permute-start(f32[6,16,64]{2,1,0:T(8,128)S(1)} %constant_dynamic-update-slice_fusion), channel_id=1, source_target_pairs={{0,2},{1,3},{2,0},{3,1},{4,6},{5,7},{6,4},{7,5},{8,10},{9,11},{10,... | collective-permute-start | bytes 73736 | tf_op jit(solution)/shard_map/ppermute | solution.py:276

commit v5 on v4

--- a/solution.py
+++ b/solution.py
@@ -184,7 +184,7 @@
 
 
 def far_kernel(
-    parts, far, far_couple, dev_couple, grp_couple, moments, first, second, *rest
+    parts, offsets, far, far_couple, dev_couple, grp_couple, moments, first, second, *rest
 ):
     tables = rest[:parts]
     out, box_tables, window, spread = rest[parts:]
@@ -229,8 +229,7 @@
         product = product[: 2 * r] + product[2 * r :]
         out[leaf] = fold(product[:, :width] + product[:, width:])
     wanted = [
-        grp_couple[group, jnp.bitwise_xor(group, other)]
-        for other in range(1, grp_couple.shape[0])
+        grp_couple[group, jnp.bitwise_xor(group, other)] for other in offsets[1:]
     ] + [dev_couple[0, n] for n in range(dev_couple.shape[1])]
     for i, kind in enumerate(wanted):
         box_tables[i * half : (i + 1) * half] = couple(tables, kind)
@@ -359,7 +358,10 @@
     groups = (sums + peer)[None, :, k:]
     boxes, groups, raw = lax.optimization_barrier((boxes, groups, raw))
 
-    groups = jnp.concatenate([groups, swap(groups, "grp", 1)])
+    offsets = [0]
+    for distance in [2 << i for i in range((lax.axis_size("grp") // 2).bit_length() - 1)]:
+        groups = jnp.concatenate([groups, swap(groups, "grp", distance)])
+        offsets += [offset ^ distance for offset in offsets]
     high_rows = half // 4
     low_rows = half - high_rows
     table_low, live = pl.pallas_call(
@@ -374,8 +376,8 @@
     groups, table_low, live, first, second = lax.optimization_barrier(
         (groups, table_low, live, first, second)
     )
-    for distance in [2 << i for i in range((lax.axis_size("grp") // 2).bit_length() - 1)]:
-        groups = jnp.concatenate([groups, swap(groups, "grp", distance)])
+    groups = jnp.concatenate([groups, swap(groups, "grp", 1)])
+    offsets += [offset ^ 1 for offset in offsets]
 
     steps = 4
 
@@ -412,7 +414,7 @@
     ]
     wanted = groups.shape[0] - 1 + dev_couple.shape[1]
     far, box_tables = pl.pallas_call(
-        functools.partial(far_kernel, len(tables)),
+        functools.partial(far_kernel, len(tables), tuple(offsets)),
         out_shape=(shape((leaves, r, k), F32), shape((wanted * half, 2 * k), F32)),
         in_specs=[SMEM] * 4 + [VMEM] * (3 + len(tables)),
         out_specs=(VMEM, VMEM),

time: 31.9 us -> 30 us (0.940)
  starting transfers between devices: 14.9 us -> 13 us
    ppermute x7, starting transfers between devices: 10.1 us -> 8.21 us  [swap(): lax.ppermute(x, axis, [(i, i ^ distance) for i in range(lax.axis_size(axi...]
    ppermute x7, waiting for transfers between devices: 0.02 us -> 1.16 us  [swap(): lax.ppermute(x, axis, [(i, i ^ distance) for i in range(lax.axis_size(axi...]
    ppermute x1, waiting for transfers between devices: 1.07 us -> 0.01 us  [local(): lax.ppermute(send_second, AXES, partners + [(j, i) for i, j in partners])]
  transfers between devices with their start and end apart: 8 -> 8, of which waited for: 1 -> 2; matrix products, arithmetic and copies ran while one was open for 0% -> 0% of each run, Pallas kernels for 25% -> 26%
where the time goes in v5:
time: 30 us; the launch traced here: 29.9 us
  Pallas kernels  14 us (47%)
  starting transfers between devices  13 us (43%)
  between operations  1.51 us (5%)
  waiting for transfers between devices  1.16 us (4%)
    ppermute x7, starting transfers between devices, swap(): lax.ppermute(x, axis, [(i, i ^ distance) for i in range(lax.axis_size(axi...  8.21 us
    ppermute x1, starting transfers between devices, local(): lax.ppermute(send_second, AXES, partners + [(j, i) for i, j in partners])  4.82 us
    pallas_call x1, Pallas kernels, local(): pl.pallas_call(moment_kernel, out_shape=(shape((leaves, r, 2 * k), BF16),...  3.97 us
    pallas_call x1, Pallas kernels, local(): pl.pallas_call(functools.partial(far_kernel, len(tables), tuple(offsets))...  3.38 us
    pallas_call x1, Pallas kernels, near_part(): pl.pallas_call(functools.partial(near_kernel, steps, low_rows, high_rows)...  2.9 us
    pallas_call x1, Pallas kernels, local(): pl.pallas_call(functools.partial(final_kernel, steps), out_shape=shape((l...  2.17 us
    pallas_call x1, Pallas kernels, local(): pl.pallas_call(functools.partial(table_kernel, low_rows), out_shape=(shap...  1.56 us
    ppermute x7, waiting for transfers between devices, swap(): lax.ppermute(x, axis, [(i, i ^ distance) for i in range(lax.axis_size(axi...  1.16 us
  transfers between devices with their start and end apart: 8, of which 2 were waited for; matrix products, arithmetic and copies ran while one was open for 0% of the time, Pallas kernels for 26%

profile of v5, /device:TPU:0, one launch (start us, length us, event | category | flops | bytes accessed | tf_op | source)
XLA Modules:
  0.0 29.9 jit_solution(8241611513260382171)
XLA Ops:
  0.7 0.0 slice-start
  0.7 0.0 slice-start.1
  0.7 0.0 copy-start.3
  0.7 0.0 copy-start.4
  0.7 4.0 %moments.1 = (bf16[32,16,128]{2,1,0:T(8,128)(2,1)S(1)}, bf16[16,32,128]{2,1,0:T(8,128)(2,1)S(1)}, bf16[16,32,128]{2,1,0:T(8,128)(2,1)S(1)}, f32[16,128]{1,0:T(8,...) custom-call(s32[32]{0:T(128)} %leaf_trans_hbm.1, ...), custom_call_target="tpu_custom_call" | custom-call | tf_op jit(solution)/shard_map/moments/pallas_call | solution.py:319
  4.7 3.0 %collective-permute-start = (f32[16,128]{1,0:T(8,128)S(1)}, f32[16,128]{1,0:T(8,128)S(1)}, u32[]{:S(2)}, u32[]{:S(2)}) collective-permute-start(f32[16,128]{1,0:T(8,128)S(1)} %get-tuple-element.36), channel_id=1, source_target_pairs={{0,1},{1,0},{2,3},{3,2},{4,5},{5,4},{6,7},{7,6},{8,9},{9,8},{10,11... | collective-permute-start | bytes 24584 | tf_op jit(solution)/shard_map/ppermute | solution.py:275
  7.7 0.1 collective-permute-start.2
  7.8 4.8 %collective-permute-start.3 = (bf16[16,32,128]{2,1,0:T(8,128)(2,1)S(1)}, bf16[16,32,128]{2,1,0:T(8,128)(2,1)S(1)}, u32[]{:S(2)}, u32[]{:S(2)}) collective-permute-start(bf16[16,32,128]{2,1,0:T(8,128)(2,1)S(1)} %get-tuple-element.44), channel_id=1, source_target_pairs={{1,2},{3,4},{5,6},{7,8},{9,10},{11,12},{13,14},{15,16},{17,18},{19... | collective-permute-start | bytes 393224 | tf_op jit(solution)/shard_map/ppermute | solution.py:355
  12.6 0.0 collective-permute-done
  12.6 0.1 fusion
  12.7 0.5 %collective-permute-start.1 = (f32[1,16,64]{2,1,0:T(8,128)S(1)}, f32[1,16,64]{2,1,0:T(8,128)S(1)}, u32[]{:S(2)}, u32[]{:S(2)}) collective-permute-start(f32[1,16,64]{2,1,0:T(8,128)S(1)} %get-tuple-element.39), channel_id=1, source_target_pairs={{0,16},{8,24},{16,0},{24,8},{1,17},{9,25},{17,1},{25,9},{2,18},{10... | collective-permute-start | bytes 12296 | tf_op jit(solution)/shard_map/ppermute | solution.py:275
  13.8 1.6 %table.1 = (f32[7584,128]{1,0:T(8,128)S(1)}, s32[8]{0:T(128)S(1)}) custom-call(s32[1]{0:T(128)S(6)} %copy.18.count, f32[2,32,64,316]{3,2,1,0:T(8,128)S(1)} %get-tuple-element.40.table), custom_call_target="tpu_custom_call" | custom-call | bytes 9437184 | tf_op jit(solution)/shard_map/table/pallas_call | solution.py:367
  15.4 0.9 %collective-permute-done.1 = f32[1,16,64]{2,1,0:T(8,128)S(1)} collective-permute-done((f32[1,16,64]{2,1,0:T(8,128)S(1)}, f32[1,16,64]{2,1,0:T(8,128)S(1)}, u32[]{:S(2)}, u32[]{:S(2)}) %collective-permute-start.1) | collective-permute-done | bytes 4128 | tf_op jit(solution)/shard_map/ppermute | solution.py:275
  16.3 0.0 collective-permute-done.2.first
  16.3 0.0 collective-permute-done.3.second
  16.4 0.2 collective-permute-start.4
  16.5 0.0 slice-done
  16.5 0.0 slice-done.1
  16.5 0.0 copy-done.3
  16.5 0.0 copy-done.4
  16.5 0.0 copy-start
  16.6 0.0 copy-start.1
  16.6 0.0 copy-start.2
  16.6 0.0 copy-start.6
  16.6 2.9 %near.1 = (f32[32,16,128]{2,1,0:T(8,128)S(1)}, f32[2528,128]{1,0:T(8,128)S(1)}) custom-call(s32[160]{0:T(256)S(1)} %copy-done.3, s32[160]{0:T(256)S(1)} %copy-done.4, s32[8]{0:T(128)S(1)} %get-tuple-element.46.count, bf16[32,16,128]{2,1,0:T(8,128)(2,1)S(1)} %get-tuple-element.47.charges, bf16[16,32,128]{2,1,0:T(8,128)(2,1)S(1)} %collective-permute-done.2.first, ...), custom_call_target="tpu_custom_call" | custom-call | bytes 9437184 | tf_op jit(solution)/shard_map/near/pallas_call | solution.py:385
  19.5 0.0 copy-start.5
  19.5 0.0 collective-permute-done.4
  19.6 2.7 %collective-permute-start.7 = (f32[6,16,64]{2,1,0:T(8,128)S(1)}, f32[6,16,64]{2,1,0:T(8,128)S(1)}, u32[]{:S(2)}, u32[]{:S(2)}) collective-permute-start(f32[6,16,64]{2,1,0:T(8,128)S(1)} %constant_dynamic-update-slice_fusion), channel_id=1, source_target_pairs={{0,6},{1,7},{2,4},{3,5},{4,2},{5,3},{6,0},{7,1},{8,14},{9,15},{10,... | collective-permute-start | bytes 73736 | tf_op jit(solution)/shard_map/ppermute | solution.py:275
  22.2 0.0 collective-permute-start.6
  22.2 1.8 %collective-permute-start.5 = (f32[6,16,64]{2,1,0:T(8,128)S(1)}, f32[6,16,64]{2,1,0:T(8,128)S(1)}, u32[]{:S(2)}, u32[]{:S(2)}) collective-permute-start(f32[6,16,64]{2,1,0:T(8,128)S(1)} %constant_dynamic-update-slice_fusion), channel_id=1, source_target_pairs={{0,2},{1,3},{2,0},{3,1},{4,6},{5,7},{6,4},{7,5},{8,10},{9,11},{10,... | collective-permute-start | bytes 73736 | tf_op jit(solution)/shard_map/ppermute | solution.py:275
  24.0 0.0 copy-done
  24.0 0.0 copy-done.1
  24.0 0.0 copy-done.2
  24.0 0.0 copy-done.6
  24.0 3.4 %far.1 = (f32[32,16,64]{2,1,0:T(8,128)S(1)}, f32[224,128]{1,0:T(8,128)S(1)}) custom-call(s32[16,32]{1,0:T(8,128)S(1)} %bitcast.18, s32[16,32]{1,0:T(8,128)S(1)} %bitcast.19, s32[1,4]{1,0:T(1,128)S(1)} %copy-done.6, s32[4,4]{1,0:T(4,128)S(1)} %copy-done.2, bf16[32,16,128]{2,1,0:T(8,128)(2,1)S(1)} %get-tuple-element.53.moments, ...), custom_call_target="tpu_custom_call" | custom-call | bytes 9437184 | tf_op jit(solution)/shard_map/far/pallas_call | solution.py:416
  27.4 0.0 collective-permute-done.7
  27.4 0.2 collective-permute-done.6
  27.6 0.0 collective-permute-done.5
  27.7 0.0 copy-done.5
  27.7 2.2 %final.1 = f32[32,16,128]{2,1,0:T(8,128)} custom-call(s32[32]{0:T(128)S(1)} %get-tuple-element.34.leaf_trans, s32[8]{0:T(128)S(1)} %get-tuple-element.35.dev_trans, s32[1,4]{1,0:T(1,128)S(1)} %copy-done.5, f32[32,16,128]{2,1,0:T(8,128)S(1)} %get-tuple-element.52.near, f32[32,16,64]{2,1,0:T(8,128)S(1)} %get-tuple-element.56.far, ...), custom_call_target="tpu_custom_call" | custom-call | tf_op jit(solution)/shard_map/final/pallas_call | solution.py:432
  (11 shorter events, 0.1 us)
Async XLA Ops:
  0.7 15.9 %slice-start = ((s8[5242880]{0:T(1024)(128)(4,1)}), s8[4194304]{0:T(1024)(128)(4,1)S(1)}, s32[]{:S(2)}) async-start(s8[5242880]{0:T(1024)(128)(4,1)} %bitcast.14), calls=%async_computation | async-start | bytes 8388608
  0.7 15.9 %slice-start.1 = ((s8[5242880]{0:T(1024)(128)(4,1)}), s8[1048576]{0:T(1024)(128)(4,1)S(1)}, s32[]{:S(2)}) async-start(s8[5242880]{0:T(1024)(128)(4,1)} %bitcast.14), calls=%async_computation.1 | async-start | bytes 2097152
  0.7 15.9 %copy-start.3 = (s32[160]{0:T(256)S(1)}, s32[160]{0:T(256)}, u32[]{:S(2)}) copy-start(s32[160]{0:T(256)} %targets.1) | copy-start | bytes 1924
  0.7 15.8 %copy-start.4 = (s32[160]{0:T(256)S(1)}, s32[160]{0:T(256)}, u32[]{:S(2)}) copy-start(s32[160]{0:T(256)} %sources.1) | copy-start | bytes 1924
  4.7 7.9 %collective-permute-start = (f32[16,128]{1,0:T(8,128)S(1)}, f32[16,128]{1,0:T(8,128)S(1)}, u32[]{:S(2)}, u32[]{:S(2)}) collective-permute-start(f32[16,128]{1,0:T(8,128)S(1)} %get-tuple-element.36), channel_id=1, source_target_pairs={{0,1},{1,0},{2,3},{3,2},{4,5},{5,4},{6,7},{7,6},{8,9},{9,8},{10,11... | collective-permute-start | bytes 24584 | tf_op jit(solution)/shard_map/ppermute | solution.py:275
  7.7 8.7 %collective-permute-start.2 = (bf16[16,32,128]{2,1,0:T(8,128)(2,1)S(1)}, bf16[16,32,128]{2,1,0:T(8,128)(2,1)S(1)}, u32[]{:S(2)}, u32[]{:S(2)}) collective-permute-start(bf16[16,32,128]{2,1,0:T(8,128)(2,1)S(1)} %get-tuple-element.43), channel_id=1, source_target_pairs={{0,1},{1,0},{2,3},{3,2},{4,5},{5,4},{6,7},{7,6},{8,9},{9,8},{10,11... | collective-permute-start | bytes 393224 | tf_op jit(solution)/shard_map/ppermute | solution.py:275
  7.8 8.6 %collective-permute-start.3 = (bf16[16,32,128]{2,1,0:T(8,128)(2,1)S(1)}, bf16[16,32,128]{2,1,0:T(8,128)(2,1)S(1)}, u32[]{:S(2)}, u32[]{:S(2)}) collective-permute-start(bf16[16,32,128]{2,1,0:T(8,128)(2,1)S(1)} %get-tuple-element.44), channel_id=1, source_target_pairs={{1,2},{3,4},{5,6},{7,8},{9,10},{11,12},{13,14},{15,16},{17,18},{19... | collective-permute-start | bytes 393224 | tf_op jit(solution)/shard_map/ppermute | solution.py:355
  12.7 3.7 %collective-permute-start.1 = (f32[1,16,64]{2,1,0:T(8,128)S(1)}, f32[1,16,64]{2,1,0:T(8,128)S(1)}, u32[]{:S(2)}, u32[]{:S(2)}) collective-permute-start(f32[1,16,64]{2,1,0:T(8,128)S(1)} %get-tuple-element.39), channel_id=1, source_target_pairs={{0,16},{8,24},{16,0},{24,8},{1,17},{9,25},{17,1},{25,9},{2,18},{10... | collective-permute-start | bytes 12296 | tf_op jit(solution)/shard_map/ppermute | solution.py:275
  16.4 3.2 %collective-permute-start.4 = (f32[2,16,64]{2,1,0:T(8,128)S(1)}, f32[2,16,64]{2,1,0:T(8,128)S(1)}, u32[]{:S(2)}, u32[]{:S(2)}) collective-permute-start(f32[2,16,64]{2,1,0:T(8,128)S(1)} %pad_maximum_fusion.3), channel_id=1, source_target_pairs={{0,8},{8,0},{16,24},{24,16},{1,9},{9,1},{17,25},{25,17},{2,10},{10... | collective-permute-start | bytes 24584 | tf_op jit(solution)/shard_map/ppermute | solution.py:275
  16.5 7.5 %copy-start = (s32[32,16]{0,1:T(8,128)S(1)}, s32[32,16]{0,1:T(8,128)}, u32[]{:S(2)}) copy-start(s32[32,16]{0,1:T(8,128)} %param.22) | copy-start | bytes 6148
  16.6 7.5 %copy-start.1 = (s32[32,16]{0,1:T(8,128)S(1)}, s32[32,16]{0,1:T(8,128)}, u32[]{:S(2)}) copy-start(s32[32,16]{0,1:T(8,128)} %param.23) | copy-start | bytes 6148
  16.6 7.5 %copy-start.2 = (s32[4,4]{1,0:T(4,128)S(1)}, s32[4,4]{1,0:T(4,128)}, u32[]{:S(2)}) copy-start(s32[4,4]{1,0:T(4,128)} %grp_couple.1) | copy-start | bytes 196
  16.6 7.4 %copy-start.6 = (s32[1,4]{1,0:T(1,128)S(1)}, s32[1,4]{1,0:T(1,128)}, u32[]{:S(2)}) copy-start(s32[1,4]{1,0:T(1,128)} %dev_couple.1) | copy-start | bytes 52
  19.5 8.2 %copy-start.5 = (s32[1,4]{1,0:T(1,128)S(1)}, s32[1,4]{1,0:T(1,128)}, u32[]{:S(2)}) copy-start(s32[1,4]{1,0:T(1,128)} %dev_list.1) | copy-start | bytes 52
  19.6 7.9 %collective-permute-start.7 = (f32[6,16,64]{2,1,0:T(8,128)S(1)}, f32[6,16,64]{2,1,0:T(8,128)S(1)}, u32[]{:S(2)}, u32[]{:S(2)}) collective-permute-start(f32[6,16,64]{2,1,0:T(8,128)S(1)} %constant_dynamic-update-slice_fusion), channel_id=1, source_target_pairs={{0,6},{1,7},{2,4},{3,5},{4,2},{5,3},{6,0},{7,1},{8,14},{9,15},{10,... | collective-permute-start | bytes 73736 | tf_op jit(solution)/shard_map/ppermute | solution.py:275
  22.2 5.4 %collective-permute-start.6 = (f32[6,16,64]{2,1,0:T(8,128)S(1)}, f32[6,16,64]{2,1,0:T(8,128)S(1)}, u32[]{:S(2)}, u32[]{:S(2)}) collective-permute-start(f32[6,16,64]{2,1,0:T(8,128)S(1)} %constant_dynamic-update-slice_fusion), channel_id=1, source_target_pairs={{0,4},{1,5},{2,6},{3,7},{4,0},{5,1},{6,2},{7,3},{8,12},{9,13},{10,... | collective-permute-start | bytes 73736 | tf_op jit(solution)/shard_map/ppermute | solution.py:275
  22.2 5.4 %collective-permute-start.5 = (f32[6,16,64]{2,1,0:T(8,128)S(1)}, f32[6,16,64]{2,1,0:T(8,128)S(1)}, u32[]{:S(2)}, u32[]{:S(2)}) collective-permute-start(f32[6,16,64]{2,1,0:T(8,128)S(1)} %constant_dynamic-update-slice_fusion), channel_id=1, source_target_pairs={{0,2},{1,3},{2,0},{3,1},{4,6},{5,7},{6,4},{7,5},{8,10},{9,11},{10,... | collective-permute-start | bytes 73736 | tf_op jit(solution)/shard_map/ppermute | solution.py:275

commit v6 on v5

--- a/solution.py
+++ b/solution.py
@@ -15,6 +15,8 @@
 SMEM = pl.BlockSpec(memory_space=pltpu.SMEM)
 HBM = pl.BlockSpec(memory_space=pltpu.HBM)
 MIB = 2**20
+TABLE_ROWS = 4
+PIECES = 4
 
 
 def halves(x):
@@ -46,10 +48,18 @@
     moments, send_first, send_second, sums, leaf_trans, dev_trans_out, charges, basis_t,
     trans_leaf, trans_dev, table, classes, sems,
 ):
-    moves = [
-        (charges_hbm, charges), (basis_hbm, basis_t), (leaf_trans_hbm, leaf_trans),
-        (trans_leaf_hbm, trans_leaf), (trans_dev_hbm, trans_dev),
-        (table_hbm, table),
+    leaves, r, _ = charges.shape
+    k = basis_t.shape[1]
+    margin = leaves // 2
+    kinds = trans_leaf.shape[0]
+    size = leaves // PIECES
+    pieces = [pl.ds(i * size, size) for i in range(PIECES)]
+    moves = [(leaf_trans_hbm, leaf_trans), (charges_hbm, charges)]
+    moves += [(basis_hbm.at[piece], basis_t.at[piece]) for piece in pieces]
+    moves += [(trans_leaf_hbm, trans_leaf), (trans_dev_hbm, trans_dev)]
+    moves += [
+        (table_hbm.at[:, pl.ds(i, TABLE_ROWS)], table.at[:, pl.ds(i, TABLE_ROWS)])
+        for i in range(0, table.shape[1], TABLE_ROWS)
     ]
     copies = [
         pltpu.make_async_copy(source, target, sems.at[i])
@@ -57,27 +67,28 @@
     ]
     for copy in copies:
         copy.start()
-    leaves, r, _ = charges.shape
-    k = basis_t.shape[1]
-    margin = leaves // 2
-    kinds = trans_leaf.shape[0]
     even = lax.rem(lax.axis_index("dev"), 2) == 0
     left = lax.broadcasted_iota(jnp.int32, (r, 2 * k), 1) < k
-    classes[...] = jnp.zeros_like(classes)
-    for copy in copies[:3]:
-        copy.wait()
-    for leaf in range(leaves):
-        basis = basis_t[leaf]
-        twice = lax.dot_general(
-            charges[leaf], jnp.concatenate([basis, basis], axis=0), NT,
-            preferred_element_type=F32,
-        )
-        kind = leaf_trans[leaf]
-        classes[kind] = classes[kind] + twice
-        high = twice.astype(BF16).astype(F32)
-        moments[leaf] = jnp.where(left, high, twice - high).astype(BF16)
-    for copy in copies[3:5]:
-        copy.wait()
+    for lane in range(PIECES):
+        classes[lane][...] = jnp.zeros_like(classes[lane])
+    copies[0].wait()
+    copies[1].wait()
+    for piece in range(PIECES):
+        copies[2 + piece].wait()
+        for leaf in range(piece * size, (piece + 1) * size):
+            basis = basis_t[leaf]
+            twice = lax.dot_general(
+                charges[leaf], jnp.concatenate([basis, basis], axis=0), NT,
+                preferred_element_type=F32,
+            )
+            kind = leaf_trans[leaf]
+            lane = classes[leaf % PIECES]
+            lane[kind] = lane[kind] + twice
+            high = twice.astype(BF16).astype(F32)
+            moments[leaf] = jnp.where(left, high, twice - high).astype(BF16)
+    copies[2 + PIECES].wait()
+    copies[3 + PIECES].wait()
+    classes = sum([lane[...] for lane in classes[1:]], start=classes[0][...])
     lhs = [
         jnp.where(left, classes[kind], classes[kind + 1]) for kind in range(0, kinds, 2)
     ]
@@ -102,7 +113,8 @@
     def _():
         fill(0, margin)
 
-    copies[5].wait()
+    for copy in copies[4 + PIECES :]:
+        copy.wait()
 
 
 def relayout(table, row, out, place, count):
@@ -115,17 +127,31 @@
         ].T
 
 
-def relayout_rows(table, out, begin, rows):
-    def step(place, carry):
-        relayout(table, begin + place, out, place, rows)
+def relayout_rows(table, out, begin, count, rows):
+    def step(row, carry):
+        relayout(table, row, out, begin + row, rows)
         return carry
 
-    lax.fori_loop(0, rows, step, 0, unroll=8)
-
-
-def table_kernel(rows, count, table, out, count_out):
-    count_out[0] = count[0]
-    relayout_rows(table, out, 0, rows)
+    lax.fori_loop(0, count, step, 0, unroll=8)
+
+
+def table_kernel(table, high_hbm, out, high, sems):
+    low_rows, high_rows = table.shape[1], high.shape[1]
+    copies = [
+        pltpu.make_async_copy(
+            high_hbm.at[:, pl.ds(low_rows + i, TABLE_ROWS)],
+            high.at[:, pl.ds(i, TABLE_ROWS)],
+            sems.at[i // TABLE_ROWS],
+        )
+        for i in range(0, high_rows, TABLE_ROWS)
+    ]
+    for copy in copies:
+        copy.start()
+    rows = out.shape[0] // table.shape[3]
+    relayout_rows(table, out, 0, low_rows, rows)
+    for copy in copies:
+        copy.wait()
+    relayout_rows(high, out, low_rows, rows - low_rows, rows)
 
 
 def halo_places(leaves):
@@ -145,7 +171,7 @@
     chunk = blocks.shape[0] // steps
     leaves, r, panels = charges.shape
     margin = leaves // 2
-    live = count[0]
+    live = count[...]
     leaf_start = first_leaf(leaves)
     first_at, second_at = halo_places(leaves)
     window[pl.ds(margin, leaves)] = charges[...]
@@ -159,41 +185,46 @@
     def step(index, carry):
         base = index * chunk
         products = []
-        for u in range(0, chunk, 2):
+        empty = jnp.zeros((r, panels), BF16)
+        for u in [base + i for i in range(0, chunk, 4)]:
+            one, two, three, four = (picked(u + i) for i in range(4))
+            lhs = jnp.concatenate([one, empty, three, empty], axis=0)
+            rhs = jnp.concatenate([empty, two, empty, four], axis=0)
             both = lax.dot_general(
-                jnp.concatenate([picked(base + u), picked(base + u + 1)], axis=0),
-                blocks[pl.ds(base + u, 2)].reshape(2 * panels, panels),
+                jnp.concatenate([lhs, rhs], axis=1),
+                jnp.concatenate(
+                    [
+                        jnp.concatenate([blocks[u], blocks[u + 2]], axis=0),
+                        jnp.concatenate([blocks[u + 1], blocks[u + 3]], axis=0),
+                    ],
+                    axis=1,
+                ),
                 NT, preferred_element_type=F32,
             )
-            products += [both[:r, :panels], both[r:, panels:]]
+            products += [both[:r, :panels], both[r : 2 * r, :panels]]
+            products += [both[2 * r : 3 * r, panels:], both[3 * r :, panels:]]
         for u in range(rows // steps):
             place = index * (rows // steps) + u
             relayout(table, begin + place, table_out, place, rows)
         for u in range(chunk):
             slot = base + u
-            row = jnp.where(slot < live, targets[slot] - leaf_start, leaves)
-            total[row] = total[row] + products[u]
+            row = targets[slot] - leaf_start
+            total[row] = total[row] + jnp.where(live > slot, products[u], 0.0)
         return carry
 
     lax.fori_loop(0, steps, step, 0)
-    out[...] = total[:leaves]
+    out[...] = total[...]
 
 
 def couple(tables, kind):
     return jnp.concatenate([table[kind] for table in tables], axis=0)
 
 
-def far_kernel(
-    parts, offsets, far, far_couple, dev_couple, grp_couple, moments, first, second, *rest
-):
-    tables = rest[:parts]
-    out, box_tables, window, spread = rest[parts:]
+def spread_kernel(count, moments, first, second, spread, count_out, window):
+    count_out[...] = jnp.full(count_out.shape, count[0], jnp.int32)
     leaves, r, width = moments.shape
     margin = leaves // 2
-    k, half = width // 2, width // 4
-    nfar = far.shape[0]
-    group = lax.axis_index("grp")
-    origin = first_leaf(leaves) - margin
+    half = width // 4
     first_at, second_at = halo_places(leaves)
     window[pl.ds(margin, leaves)] = moments[...]
     window[pl.ds(first_at, margin)] = first[:margin, r:]
@@ -209,6 +240,16 @@
             spread[start : start + piece, section * r : (section + 1) * r] = copied[
                 :, section * width : (section + 1) * width
             ].reshape(piece, r, width)
+
+
+def far_kernel(parts, offsets, far, far_couple, dev_couple, grp_couple, spread, *rest):
+    tables = rest[:parts]
+    out, box_tables = rest[parts:]
+    leaves, r, k = out.shape
+    width, half = 2 * k, k // 2
+    nfar = far.shape[0]
+    group = lax.axis_index("grp")
+    origin = first_leaf(leaves) - leaves // 2
     lane = lax.broadcasted_iota(jnp.int32, (4 * r, width), 1) // half
     for leaf in range(leaves):
         lhs, rhs = [], []
@@ -275,6 +316,15 @@
     return lax.ppermute(x, axis, [(i, i ^ distance) for i in range(lax.axis_size(axis))])
 
 
+def side_by_side(first, second, move):
+    parts = jnp.concatenate([first, second])
+    total, _, k = parts.shape
+    half = (total + 1) // 2
+    parts = jnp.pad(parts, ((0, 2 * half - total), (0, 0), (0, 0)))
+    got = move(jnp.concatenate([parts[:half], parts[half:]], axis=2))
+    return jnp.concatenate([got[:, :, :k], got[:, :, k:]])[:total]
+
+
 def cost(us):
     return pl.CostEstimate(flops=0, bytes_accessed=us * 3 * MIB, transcendentals=0)
 
@@ -312,6 +362,9 @@
     basis_t = jnp.swapaxes(leaf_basis, 1, 2)
     shape = jax.ShapeDtypeStruct
 
+    couplings = pltpu.with_memory_space_constraint(
+        jnp.transpose(couple_table, (1, 2, 0)).reshape(2, half, k, kinds), pltpu.HBM
+    )
     (
         moments, send_first, send_second, sums, leaf_kinds, dev_kind, own_charges, basis,
         leaf_maps, dev_maps, raw,
@@ -329,13 +382,13 @@
                 shape(basis_t.shape, BF16),
                 shape(trans_leaf.shape, F32),
                 shape(trans_dev.shape, F32),
-                shape((2, half, k, kinds), F32),
+                shape((2, half // 2, k, kinds), F32),
             ),
             in_specs=[HBM, SMEM] + [HBM] * 5,
             out_specs=(VMEM,) * 4 + (SMEM,) * 2 + (VMEM,) * 5,
             scratch_shapes=[
-                pltpu.VMEM((trans_leaf.shape[0], r, 2 * k), F32),
-                pltpu.SemaphoreType.DMA((6,)),
+                [pltpu.VMEM((trans_leaf.shape[0], r, 2 * k), F32) for _ in range(PIECES)],
+                pltpu.SemaphoreType.DMA((4 + PIECES + half // 2 // TABLE_ROWS,)),
             ],
             compiler_params=params(24),
             name="moments",
@@ -346,53 +399,68 @@
             pltpu.with_memory_space_constraint(basis_t, pltpu.HBM),
             pltpu.with_memory_space_constraint(trans_leaf, pltpu.HBM),
             pltpu.with_memory_space_constraint(trans_dev, pltpu.HBM),
-            pltpu.with_memory_space_constraint(jnp.transpose(couple_table, (1, 2, 0)).reshape(2, half, k, kinds), pltpu.HBM),
+            couplings,
         )
     )
 
+    first = swap(send_first, "dev", 1)
     peer = swap(sums, "dev", 1)
     partners = [(i, i + 1) for i in range(1, devices - 1, 2)] + [(0, devices - 1)]
     second = lax.ppermute(send_second, AXES, partners + [(j, i) for i, j in partners])
-    first = swap(send_first, "dev", 1)
     boxes = jnp.stack([sums[:, :k], peer[:, :k]])
     groups = (sums + peer)[None, :, k:]
     boxes, groups, raw = lax.optimization_barrier((boxes, groups, raw))
-
     offsets = [0]
     for distance in [2 << i for i in range((lax.axis_size("grp") // 2).bit_length() - 1)]:
         groups = jnp.concatenate([groups, swap(groups, "grp", distance)])
         offsets += [offset ^ distance for offset in offsets]
     high_rows = half // 4
     low_rows = half - high_rows
-    table_low, live = pl.pallas_call(
-        functools.partial(table_kernel, low_rows),
-        out_shape=(shape((kinds * low_rows, 2 * k), F32), shape((8,), jnp.int32)),
-        in_specs=[SMEM, VMEM],
-        out_specs=(VMEM, SMEM),
+    table_low, raw = pl.pallas_call(
+        table_kernel,
+        out_shape=(
+            shape((kinds * low_rows, 2 * k), F32),
+            shape((2, half // 2, k, kinds), F32),
+        ),
+        in_specs=[VMEM, HBM],
+        out_specs=(VMEM, VMEM),
+        scratch_shapes=[pltpu.SemaphoreType.DMA((half // 2 // TABLE_ROWS,))],
         compiler_params=params(16),
         cost_estimate=cost(3),
         name="table",
-    )(near_count, raw)
-    groups, table_low, live, first, second = lax.optimization_barrier(
-        (groups, table_low, live, first, second)
+    )(raw, couplings)
+    groups, table_low, first, second = lax.optimization_barrier(
+        (groups, table_low, first, second)
     )
     groups = jnp.concatenate([groups, swap(groups, "grp", 1)])
     offsets += [offset ^ 1 for offset in offsets]
-
-    steps = 4
+    spread, live = pl.pallas_call(
+        spread_kernel,
+        out_shape=(shape((2 * leaves, 4 * r, 2 * k), BF16), shape((r, panels), jnp.int32)),
+        in_specs=[SMEM] + [VMEM] * 3,
+        out_specs=(VMEM, VMEM),
+        scratch_shapes=[pltpu.VMEM((2 * leaves, r, 2 * k), BF16)],
+        compiler_params=params(16),
+        cost_estimate=cost(1),
+        name="spread",
+    )(near_count, moments, first, second)
+    groups, spread, live, first, second = lax.optimization_barrier(
+        (groups, spread, live, first, second)
+    )
+    steps = 2
 
     def near_part():
         return pl.pallas_call(
-            functools.partial(near_kernel, steps, low_rows, high_rows),
+            functools.partial(near_kernel, steps, low_rows - half // 2, high_rows),
             out_shape=(
                 shape((leaves, r, panels), F32),
                 shape((kinds * high_rows, 2 * k), F32),
             ),
-            in_specs=[SMEM, SMEM, SMEM, VMEM, VMEM, VMEM, VMEM, VMEM],
+            in_specs=[SMEM] * 2 + [VMEM] * 6,
             out_specs=(VMEM, VMEM),
             scratch_shapes=[
                 pltpu.VMEM((2 * leaves, r, panels), BF16),
-                pltpu.VMEM((leaves + 1, r, panels), F32),
+                pltpu.VMEM((leaves, r, panels), F32),
             ],
             compiler_params=params(16),
             cost_estimate=cost(3),
@@ -402,12 +470,17 @@
             near_blocks, raw,
         )
 
-    near, table_high = near_part()
-    boxes, groups, near, table_high = lax.optimization_barrier((boxes, groups, near, table_high))
-    parts = jnp.concatenate([boxes, groups])
-    got = [swap(parts, "dev", distance) for distance in range(2, per_group, 2)]
-    boxes = jnp.concatenate([boxes] + [part[:2] for part in got])
-    groups = sum([part[2:] for part in got], start=groups)
+    near = None
+    for distance in [2 << i for i in range((per_group // 2).bit_length() - 1)]:
+        count = boxes.shape[0]
+        got = side_by_side(boxes, groups, functools.partial(swap, axis="dev", distance=distance))
+        boxes = jnp.concatenate([boxes, got[:count]])
+        groups = groups + got[count:]
+        if near is None:
+            near, table_high = near_part()
+            boxes, groups, near, table_high = lax.optimization_barrier(
+                (boxes, groups, near, table_high)
+            )
 
     tables = [
         x.reshape(kinds, x.shape[0] // kinds, 2 * k) for x in (table_low, table_high)
@@ -416,28 +489,24 @@
     far, box_tables = pl.pallas_call(
         functools.partial(far_kernel, len(tables), tuple(offsets)),
         out_shape=(shape((leaves, r, k), F32), shape((wanted * half, 2 * k), F32)),
-        in_specs=[SMEM] * 4 + [VMEM] * (3 + len(tables)),
+        in_specs=[SMEM] * 4 + [VMEM] * (1 + len(tables)),
         out_specs=(VMEM, VMEM),
-        scratch_shapes=[
-            pltpu.VMEM((2 * leaves, r, 2 * k), BF16),
-            pltpu.VMEM((2 * leaves, 4 * r, 2 * k), BF16),
-        ],
         compiler_params=params(16),
         cost_estimate=cost(3),
         name="far",
     )(
-        leaf_far.T, leaf_far_couple.T, dev_couple, grp_couple, moments, first, second, *tables
+        leaf_far.T, leaf_far_couple.T, dev_couple, grp_couple, spread, *tables
     )
 
     return pl.pallas_call(
-        functools.partial(final_kernel, steps),
+        functools.partial(final_kernel, 8),
         out_shape=shape((leaves, r, panels), F32),
         in_specs=[SMEM] * 3 + [VMEM] * 8,
         out_specs=HBM,
         scratch_shapes=[
             pltpu.VMEM((leaves, r, panels), F32),
             pltpu.VMEM((trans_leaf.shape[0], r, k), F32),
-            pltpu.SemaphoreType.DMA((steps,)),
+            pltpu.SemaphoreType.DMA((8,)),
         ],
         compiler_params=params(16),
         name="final",

time: 30 us -> 28.6 us (0.953)
  starting transfers between devices: 13 us -> 10.6 us
  waiting for transfers between devices: 1.16 us -> 2.08 us
    ppermute x7 -> x6, starting transfers between devices: 8.21 us -> 5.8 us  [swap(): lax.ppermute(x, axis, [(i, i ^ distance) for i in range(lax.axis_size(axi...]
    pallas_call x3 -> x4, Pallas kernels: 6.63 us -> 7.79 us  [the longest x1 2.65 us: local(): pl.pallas_call(table_kernel, out_shape=(shape((kinds * low_rows, 2 * k),...]
    ppermute x7 -> x6, waiting for transfers between devices: 1.16 us -> 2.08 us  [swap(): lax.ppermute(x, axis, [(i, i ^ distance) for i in range(lax.axis_size(axi...]
    pallas_call x1, Pallas kernels: 3.97 us -> 3.08 us  [local(): pl.pallas_call(moment_kernel, out_shape=(shape((leaves, r, 2 * k), BF16),...]
    pallas_call x1, Pallas kernels: 3.38 us -> 2.92 us  [local(): pl.pallas_call(functools.partial(far_kernel, len(tables), tuple(offsets))...]
  transfers between devices with their start and end apart: 8 -> 7, of which waited for: 2 -> 3; matrix products, arithmetic and copies ran while one was open for 0% -> 0% of each run, Pallas kernels for 26% -> 30%
where the time goes in v6:
time: 28.6 us; the launch traced here: 28.4 us
  Pallas kernels  13.8 us (48%)
  starting transfers between devices  10.6 us (37%)
  waiting for transfers between devices  2.08 us (7%)
  between operations  1.48 us (5%)
  other arithmetic  0.34 us (1%)
    ppermute x6, starting transfers between devices, swap(): lax.ppermute(x, axis, [(i, i ^ distance) for i in range(lax.axis_size(axi...  5.8 us
    ppermute x1, starting transfers between devices, local(): lax.ppermute(send_second, AXES, partners + [(j, i) for i, j in partners])  4.82 us
    pallas_call x1, Pallas kernels, local(): pl.pallas_call(moment_kernel, out_shape=(shape((leaves, r, 2 * k), BF16),...  3.08 us
    pallas_call x1, Pallas kernels, local(): pl.pallas_call(functools.partial(far_kernel, len(tables), tuple(offsets))...  2.92 us
    pallas_call x1, Pallas kernels, local(): pl.pallas_call(table_kernel, out_shape=(shape((kinds * low_rows, 2 * k),...  2.65 us
    pallas_call x1, Pallas kernels, near_part(): pl.pallas_call(functools.partial(near_kernel, steps, low_rows - half // 2...  2.52 us
    pallas_call x1, Pallas kernels, local(): pl.pallas_call(functools.partial(final_kernel, 8), out_shape=shape((leave...  2.19 us
    ppermute x6, waiting for transfers between devices, swap(): lax.ppermute(x, axis, [(i, i ^ distance) for i in range(lax.axis_size(axi...  2.08 us
  transfers between devices with their start and end apart: 7, of which 3 were waited for; matrix products, arithmetic and copies ran while one was open for 0% of the time, Pallas kernels for 30%

profile of v6, /device:TPU:0, one launch (start us, length us, event | category | flops | bytes accessed | tf_op | source)
XLA Modules:
  0.0 28.4 jit_solution(2416063650665074362)
XLA Ops:
  0.7 3.1 %moments.1 = (bf16[32,16,128]{2,1,0:T(8,128)(2,1)S(1)}, bf16[16,32,128]{2,1,0:T(8,128)(2,1)S(1)}, bf16[16,32,128]{2,1,0:T(8,128)(2,1)S(1)}, f32[16,128]{1,0:T(8,...) custom-call(s32[32]{0:T(128)} %leaf_trans_hbm.1, ...), custom_call_target="tpu_custom_call" | custom-call | tf_op jit(solution)/shard_map/moments/pallas_call | solution.py:372
  3.7 3.0 %collective-permute-start = (f32[16,128]{1,0:T(8,128)S(1)}, f32[16,128]{1,0:T(8,128)S(1)}, u32[]{:S(2)}, u32[]{:S(2)}) collective-permute-start(f32[16,128]{1,0:T(8,128)S(1)} %get-tuple-element.42), channel_id=1, source_target_pairs={{0,1},{1,0},{2,3},{3,2},{4,5},{5,4},{6,7},{7,6},{8,9},{9,8},{10,11... | collective-permute-start | bytes 24584 | tf_op jit(solution)/shard_map/ppermute | solution.py:316
  6.8 0.1 collective-permute-start.2
  6.8 4.8 %collective-permute-start.3 = (bf16[16,32,128]{2,1,0:T(8,128)(2,1)S(1)}, bf16[16,32,128]{2,1,0:T(8,128)(2,1)S(1)}, u32[]{:S(2)}, u32[]{:S(2)}) collective-permute-start(bf16[16,32,128]{2,1,0:T(8,128)(2,1)S(1)} %get-tuple-element.49), channel_id=1, source_target_pairs={{1,2},{3,4},{5,6},{7,8},{9,10},{11,12},{13,14},{15,16},{17,18},{19... | collective-permute-start | bytes 393224 | tf_op jit(solution)/shard_map/ppermute | solution.py:409
  11.7 0.0 collective-permute-done
  11.7 0.1 fusion.2
  11.7 0.0 slice-start
  11.7 0.0 slice-start.1
  11.8 0.0 copy-start.3
  11.8 0.0 copy-start.4
  11.8 0.6 %collective-permute-start.1 = (f32[1,16,64]{2,1,0:T(8,128)S(1)}, f32[1,16,64]{2,1,0:T(8,128)S(1)}, u32[]{:S(2)}, u32[]{:S(2)}) collective-permute-start(f32[1,16,64]{2,1,0:T(8,128)S(1)} %get-tuple-element.45), channel_id=1, source_target_pairs={{0,16},{8,24},{16,0},{24,8},{1,17},{9,25},{17,1},{25,9},{2,18},{10... | collective-permute-start | bytes 12296 | tf_op jit(solution)/shard_map/ppermute | solution.py:316
  12.4 2.6 %table.1 = (f32[7584,128]{1,0:T(8,128)S(1)}, f32[2,16,64,316]{3,2,1,0:T(8,128)S(1)}) custom-call(f32[2,16,64,316]{3,2,1,0:T(8,128)S(1)} %get-tuple-element.46.table, f32[2,32,64,316]{3,2,1,0:T(8,128)} %bitcast.21), custom_call_target="tpu_custom_call" | custom-call | bytes 9437184 | tf_op jit(solution)/shard_map/table/pallas_call | solution.py:419
  15.0 0.5 %collective-permute-done.1 = f32[1,16,64]{2,1,0:T(8,128)S(1)} collective-permute-done((f32[1,16,64]{2,1,0:T(8,128)S(1)}, f32[1,16,64]{2,1,0:T(8,128)S(1)}, u32[]{:S(2)}, u32[]{:S(2)}) %collective-permute-start.1) | collective-permute-done | bytes 4128 | tf_op jit(solution)/shard_map/ppermute | solution.py:316
  15.5 0.0 collective-permute-done.2.first
  15.5 0.0 collective-permute-done.3.second
  15.5 0.6 %collective-permute-start.4 = (f32[2,16,64]{2,1,0:T(8,128)S(1)}, f32[2,16,64]{2,1,0:T(8,128)S(1)}, u32[]{:S(2)}, u32[]{:S(2)}) collective-permute-start(f32[2,16,64]{2,1,0:T(8,128)S(1)} %pad_maximum_fusion.7), channel_id=1, source_target_pairs={{0,8},{8,0},{16,24},{24,16},{1,9},{9,1},{17,25},{25,17},{2,10},{10... | collective-permute-start | bytes 24584 | tf_op jit(solution)/shard_map/ppermute | solution.py:316
  16.8 0.4 %spread.1 = (bf16[64,64,128]{2,1,0:T(8,128)(2,1)S(1)}, s32[16,128]{1,0:T(8,128)S(1)}) custom-call(s32[1]{0:T(128)S(6)} %copy.17.count, bf16[32,16,128]{2,1,0:T(8,128)(2,1)S(1)} %get-tuple-element.51.moments, bf16[16,32,128]{2,1,0:T(8,128)(2,1)S(1)} %collective-permute-done.2.first, bf16[16,32,128]{2,1,0:T(8,128)(2,1)S(1)} %collective-permute-done.3.second), custom_call_target="tpu_custom_call" | custom-call | bytes 3145728 | tf_op jit(solution)/shard_map/spread/pallas_call | solution.py:437
  17.2 0.0 collective-permute-done.4
  17.2 0.1 fusion.1
  17.3 0.1 collective-permute-start.5
  17.4 0.0 slice-done
  17.4 0.0 slice-done.1
  17.4 0.0 copy-done.3
  17.4 0.0 copy-done.4
  17.4 0.0 copy-start
  17.4 0.0 copy-start.1
  17.4 0.0 copy-start.2
  17.5 0.0 copy-start.5
  17.5 2.5 %near.1 = (f32[32,16,128]{2,1,0:T(8,128)S(1)}, f32[2528,128]{1,0:T(8,128)S(1)}) custom-call(s32[160]{0:T(256)S(1)} %copy-done.3, s32[160]{0:T(256)S(1)} %copy-done.4, s32[16,128]{1,0:T(8,128)S(1)} %get-tuple-element.57.count, bf16[32,16,128]{2,1,0:T(8,128)(2,1)S(1)} %get-tuple-element.58.charges, bf16[16,32,128]{2,1,0:T(8,128)(2,1)S(1)} %collective-permute-done.2.first, ...), custom_call_target="tpu_custom_call" | custom-call | bytes 9437184 | tf_op jit(solution)/shard_map/near/pallas_call | solution.py:453
  20.0 0.0 copy-start.6
  20.0 1.1 %collective-permute-done.5 = f32[3,16,128]{2,1,0:T(8,128)S(1)} collective-permute-done((f32[3,16,128]{2,1,0:T(8,128)S(1)}, f32[3,16,128]{2,1,0:T(8,128)S(1)}, u32[]{:S(2)}, u32[]{:S(2)}) %collective-permute-start.5) | collective-permute-done | bytes 24608 | tf_op jit(solution)/shard_map/ppermute | solution.py:316
  21.2 0.1 fusion.3
  21.2 0.1 pad_maximum_fusion.4
  21.3 1.5 %collective-permute-start.6 = (f32[4,16,128]{2,1,0:T(8,128)S(1)}, f32[4,16,128]{2,1,0:T(8,128)S(1)}, u32[]{:S(2)}, u32[]{:S(2)}) collective-permute-start(f32[4,16,128]{2,1,0:T(8,128)S(1)} %pad_maximum_fusion.4), channel_id=1, source_target_pairs={{0,4},{1,5},{2,6},{3,7},{4,0},{5,1},{6,2},{7,3},{8,12},{9,13},{10,... | collective-permute-start | bytes 98312 | tf_op jit(solution)/shard_map/ppermute | solution.py:316
  22.8 0.0 copy-done
  22.8 0.0 copy-done.1
  22.8 0.0 copy-done.2
  22.8 0.0 copy-done.5
  22.8 2.9 %far.1 = (f32[32,16,64]{2,1,0:T(8,128)S(1)}, f32[224,128]{1,0:T(8,128)S(1)}) custom-call(s32[16,32]{1,0:T(8,128)S(1)} %bitcast.18, s32[16,32]{1,0:T(8,128)S(1)} %bitcast.19, s32[1,4]{1,0:T(1,128)S(1)} %copy-done.5, s32[4,4]{1,0:T(4,128)S(1)} %copy-done.2, bf16[64,64,128]{2,1,0:T(8,128)(2,1)S(1)} %get-tuple-element.65.spread, f32[316,24,128]{2,1,0:T(8,128)S(1)} %bitcast.16, ...), custom_call_target="tpu_custom_call" | custom-call | bytes 9437184 | tf_op jit(solution)/shard_map/far/pallas_call | solution.py:489
  25.7 0.4 %collective-permute-done.6 = f32[4,16,128]{2,1,0:T(8,128)S(1)} collective-permute-done((f32[4,16,128]{2,1,0:T(8,128)S(1)}, f32[4,16,128]{2,1,0:T(8,128)S(1)}, u32[]{:S(2)}, u32[]{:S(2)}) %collective-permute-start.6) | collective-permute-done | bytes 32800 | tf_op jit(solution)/shard_map/ppermute | solution.py:316
  26.2 0.1 slice_add_fusion
  26.2 0.0 copy-done.6
  26.3 2.2 %final.1 = f32[32,16,128]{2,1,0:T(8,128)} custom-call(s32[32]{0:T(128)S(1)} %get-tuple-element.40.leaf_trans, s32[8]{0:T(128)S(1)} %get-tuple-element.41.dev_trans, s32[1,4]{1,0:T(1,128)S(1)} %copy-done.6, f32[32,16,128]{2,1,0:T(8,128)S(1)} %get-tuple-element.64.near, f32[32,16,64]{2,1,0:T(8,128)S(1)} %get-tuple-element.68.far, ...), custom_call_target="tpu_custom_call" | custom-call | tf_op jit(solution)/shard_map/final/pallas_call | solution.py:501
  (8 shorter events, 0.0 us)
Async XLA Ops:
  3.7 7.9 %collective-permute-start = (f32[16,128]{1,0:T(8,128)S(1)}, f32[16,128]{1,0:T(8,128)S(1)}, u32[]{:S(2)}, u32[]{:S(2)}) collective-permute-start(f32[16,128]{1,0:T(8,128)S(1)} %get-tuple-element.42), channel_id=1, source_target_pairs={{0,1},{1,0},{2,3},{3,2},{4,5},{5,4},{6,7},{7,6},{8,9},{9,8},{10,11... | collective-permute-start | bytes 24584 | tf_op jit(solution)/shard_map/ppermute | solution.py:316
  6.8 8.7 %collective-permute-start.2 = (bf16[16,32,128]{2,1,0:T(8,128)(2,1)S(1)}, bf16[16,32,128]{2,1,0:T(8,128)(2,1)S(1)}, u32[]{:S(2)}, u32[]{:S(2)}) collective-permute-start(bf16[16,32,128]{2,1,0:T(8,128)(2,1)S(1)} %get-tuple-element.48), channel_id=1, source_target_pairs={{0,1},{1,0},{2,3},{3,2},{4,5},{5,4},{6,7},{7,6},{8,9},{9,8},{10,11... | collective-permute-start | bytes 393224 | tf_op jit(solution)/shard_map/ppermute | solution.py:316
  6.8 8.7 %collective-permute-start.3 = (bf16[16,32,128]{2,1,0:T(8,128)(2,1)S(1)}, bf16[16,32,128]{2,1,0:T(8,128)(2,1)S(1)}, u32[]{:S(2)}, u32[]{:S(2)}) collective-permute-start(bf16[16,32,128]{2,1,0:T(8,128)(2,1)S(1)} %get-tuple-element.49), channel_id=1, source_target_pairs={{1,2},{3,4},{5,6},{7,8},{9,10},{11,12},{13,14},{15,16},{17,18},{19... | collective-permute-start | bytes 393224 | tf_op jit(solution)/shard_map/ppermute | solution.py:409
  11.7 5.7 %slice-start = ((s8[5242880]{0:T(1024)(128)(4,1)}), s8[4194304]{0:T(1024)(128)(4,1)S(1)}, s32[]{:S(2)}) async-start(s8[5242880]{0:T(1024)(128)(4,1)} %bitcast.14), calls=%async_computation | async-start | bytes 8388608
  11.7 5.7 %slice-start.1 = ((s8[5242880]{0:T(1024)(128)(4,1)}), s8[1048576]{0:T(1024)(128)(4,1)S(1)}, s32[]{:S(2)}) async-start(s8[5242880]{0:T(1024)(128)(4,1)} %bitcast.14), calls=%async_computation.1 | async-start | bytes 2097152
  11.8 5.6 %copy-start.3 = (s32[160]{0:T(256)S(1)}, s32[160]{0:T(256)}, u32[]{:S(2)}) copy-start(s32[160]{0:T(256)} %targets.1) | copy-start | bytes 1924
  11.8 5.6 %copy-start.4 = (s32[160]{0:T(256)S(1)}, s32[160]{0:T(256)}, u32[]{:S(2)}) copy-start(s32[160]{0:T(256)} %sources.1) | copy-start | bytes 1924
  11.8 3.7 %collective-permute-start.1 = (f32[1,16,64]{2,1,0:T(8,128)S(1)}, f32[1,16,64]{2,1,0:T(8,128)S(1)}, u32[]{:S(2)}, u32[]{:S(2)}) collective-permute-start(f32[1,16,64]{2,1,0:T(8,128)S(1)} %get-tuple-element.45), channel_id=1, source_target_pairs={{0,16},{8,24},{16,0},{24,8},{1,17},{9,25},{17,1},{25,9},{2,18},{10... | collective-permute-start | bytes 12296 | tf_op jit(solution)/shard_map/ppermute | solution.py:316
  15.5 1.7 %collective-permute-start.4 = (f32[2,16,64]{2,1,0:T(8,128)S(1)}, f32[2,16,64]{2,1,0:T(8,128)S(1)}, u32[]{:S(2)}, u32[]{:S(2)}) collective-permute-start(f32[2,16,64]{2,1,0:T(8,128)S(1)} %pad_maximum_fusion.7), channel_id=1, source_target_pairs={{0,8},{8,0},{16,24},{24,16},{1,9},{9,1},{17,25},{25,17},{2,10},{10... | collective-permute-start | bytes 24584 | tf_op jit(solution)/shard_map/ppermute | solution.py:316
  17.3 3.8 %collective-permute-start.5 = (f32[3,16,128]{2,1,0:T(8,128)S(1)}, f32[3,16,128]{2,1,0:T(8,128)S(1)}, u32[]{:S(2)}, u32[]{:S(2)}) collective-permute-start(f32[3,16,128]{2,1,0:T(8,128)S(1)} %fusion.1), channel_id=1, source_target_pairs={{0,2},{1,3},{2,0},{3,1},{4,6},{5,7},{6,4},{7,5},{8,10},{9,11},{10,... | collective-permute-start | bytes 73736 | tf_op jit(solution)/shard_map/ppermute | solution.py:316
  17.4 5.4 %copy-start = (s32[32,16]{0,1:T(8,128)S(1)}, s32[32,16]{0,1:T(8,128)}, u32[]{:S(2)}) copy-start(s32[32,16]{0,1:T(8,128)} %param.22) | copy-start | bytes 6148
  17.4 5.4 %copy-start.1 = (s32[32,16]{0,1:T(8,128)S(1)}, s32[32,16]{0,1:T(8,128)}, u32[]{:S(2)}) copy-start(s32[32,16]{0,1:T(8,128)} %param.23) | copy-start | bytes 6148
  17.4 5.4 %copy-start.2 = (s32[4,4]{1,0:T(4,128)S(1)}, s32[4,4]{1,0:T(4,128)}, u32[]{:S(2)}) copy-start(s32[4,4]{1,0:T(4,128)} %grp_couple.1) | copy-start | bytes 196
  17.5 5.3 %copy-start.5 = (s32[1,4]{1,0:T(1,128)S(1)}, s32[1,4]{1,0:T(1,128)}, u32[]{:S(2)}) copy-start(s32[1,4]{1,0:T(1,128)} %dev_couple.1) | copy-start | bytes 52
  20.0 6.3 %copy-start.6 = (s32[1,4]{1,0:T(1,128)S(1)}, s32[1,4]{1,0:T(1,128)}, u32[]{:S(2)}) copy-start(s32[1,4]{1,0:T(1,128)} %dev_list.1) | copy-start | bytes 52
  21.3 4.8 %collective-permute-start.6 = (f32[4,16,128]{2,1,0:T(8,128)S(1)}, f32[4,16,128]{2,1,0:T(8,128)S(1)}, u32[]{:S(2)}, u32[]{:S(2)}) collective-permute-start(f32[4,16,128]{2,1,0:T(8,128)S(1)} %pad_maximum_fusion.4), channel_id=1, source_target_pairs={{0,4},{1,5},{2,6},{3,7},{4,0},{5,1},{6,2},{7,3},{8,12},{9,13},{10,... | collective-permute-start | bytes 98312 | tf_op jit(solution)/shard_map/ppermute | solution.py:316

commit v7 on v6

--- a/solution.py
+++ b/solution.py
@@ -15,7 +15,7 @@
 SMEM = pl.BlockSpec(memory_space=pltpu.SMEM)
 HBM = pl.BlockSpec(memory_space=pltpu.HBM)
 MIB = 2**20
-TABLE_ROWS = 4
+TABLE_ROWS = 8
 PIECES = 4
 
 
@@ -53,9 +53,7 @@
     margin = leaves // 2
     kinds = trans_leaf.shape[0]
     size = leaves // PIECES
-    pieces = [pl.ds(i * size, size) for i in range(PIECES)]
-    moves = [(leaf_trans_hbm, leaf_trans), (charges_hbm, charges)]
-    moves += [(basis_hbm.at[piece], basis_t.at[piece]) for piece in pieces]
+    moves = [(basis_hbm, basis_t), (charges_hbm, charges), (leaf_trans_hbm, leaf_trans)]
     moves += [(trans_leaf_hbm, trans_leaf), (trans_dev_hbm, trans_dev)]
     moves += [
         (table_hbm.at[:, pl.ds(i, TABLE_ROWS)], table.at[:, pl.ds(i, TABLE_ROWS)])
@@ -71,10 +69,9 @@
     left = lax.broadcasted_iota(jnp.int32, (r, 2 * k), 1) < k
     for lane in range(PIECES):
         classes[lane][...] = jnp.zeros_like(classes[lane])
-    copies[0].wait()
-    copies[1].wait()
+    for copy in copies[:3]:
+        copy.wait()
     for piece in range(PIECES):
-        copies[2 + piece].wait()
         for leaf in range(piece * size, (piece + 1) * size):
             basis = basis_t[leaf]
             twice = lax.dot_general(
@@ -86,8 +83,8 @@
             lane[kind] = lane[kind] + twice
             high = twice.astype(BF16).astype(F32)
             moments[leaf] = jnp.where(left, high, twice - high).astype(BF16)
-    copies[2 + PIECES].wait()
-    copies[3 + PIECES].wait()
+    copies[3].wait()
+    copies[4].wait()
     classes = sum([lane[...] for lane in classes[1:]], start=classes[0][...])
     lhs = [
         jnp.where(left, classes[kind], classes[kind + 1]) for kind in range(0, kinds, 2)
@@ -113,7 +110,7 @@
     def _():
         fill(0, margin)
 
-    for copy in copies[4 + PIECES :]:
+    for copy in copies[5:]:
         copy.wait()
 
 
@@ -242,11 +239,13 @@
             ].reshape(piece, r, width)
 
 
-def far_kernel(parts, offsets, far, far_couple, dev_couple, grp_couple, spread, *rest):
+def far_kernel(
+    parts, offsets, far, far_couple, dev_couple, grp_couple, spread, trans_leaf, *rest
+):
     tables = rest[:parts]
-    out, box_tables = rest[parts:]
-    leaves, r, k = out.shape
-    width, half = 2 * k, k // 2
+    out, box_tables, leaf_maps = rest[parts:]
+    pairs, r, width = out.shape
+    leaves, k, half = 2 * pairs, width // 2, width // 4
     nfar = far.shape[0]
     group = lax.axis_index("grp")
     origin = first_leaf(leaves) - leaves // 2
@@ -268,7 +267,18 @@
             preferred_element_type=F32,
         )
         product = product[: 2 * r] + product[2 * r :]
-        out[leaf] = fold(product[:, :width] + product[:, width:])
+        product = product[:, :width] + product[:, width:]
+        own, other = (product[:r], product[r:]) if leaf % 2 == 0 else (product[r:], product[:r])
+        folded = own + pltpu.roll(other, k, 1)
+        if leaf % 2 == 0:
+            even_leaf = folded
+        else:
+            out[leaf // 2] = jnp.where(lane[:r] < 2, even_leaf, folded)
+    for kind in range(0, trans_leaf.shape[0], 2):
+        two = trans_leaf[kind : kind + 2].reshape(width, k).T
+        high, low = split(two)
+        leaf_maps[0, :, kind * k : (kind + 2) * k] = high
+        leaf_maps[1, :, kind * k : (kind + 2) * k] = low
     wanted = [
         grp_couple[group, jnp.bitwise_xor(group, other)] for other in offsets[1:]
     ] + [dev_couple[0, n] for n in range(dev_couple.shape[1])]
@@ -278,10 +288,11 @@
 
 def final_kernel(
     steps, leaf_trans, dev_trans, dev_list, near, far, box_tables, boxes, groups, basis_t,
-    trans_leaf, trans_dev, out_hbm, out, locals_, sems,
+    leaf_maps, trans_dev, out_hbm, out, locals_, sems,
 ):
-    leaves = near.shape[0]
-    kinds, k, _ = trans_leaf.shape
+    leaves, r, panels = near.shape
+    k = leaf_maps.shape[1]
+    kinds = leaf_maps.shape[2] // k
     others = groups.shape[0] - 1
     group = lax.axis_index("grp")
     member = lax.axis_index("dev")
@@ -294,17 +305,36 @@
         lhs.append(halves(boxes[place]))
     listed = fold(dot3(jnp.concatenate(lhs, axis=1), box_tables[split_at:]))
     box_local = dot3(group_local, trans_dev[dev_trans[0]], NT) + listed
-    by_kind = dot3(box_local, trans_leaf[...].reshape(kinds * k, k), NT)
-    for kind in range(kinds):
-        locals_[kind] = by_kind[:, kind * k : (kind + 1) * k]
+    high, low = split(box_local)
+    by_kind = jnp.dot(
+        jnp.concatenate([high, low], axis=0), leaf_maps[0], preferred_element_type=F32
+    )
+    by_kind = by_kind[:r] + by_kind[r:]
+    by_kind += jnp.dot(high, leaf_maps[1], preferred_element_type=F32)
+    left = lax.broadcasted_iota(jnp.int32, (r, 2 * k), 1) < k
+    for kind in range(0, kinds, 2):
+        two = by_kind[:, kind * k : (kind + 2) * k]
+        turned = pltpu.roll(two, k, 1)
+        locals_[kind] = jnp.where(left, two, turned)
+        locals_[kind + 1] = jnp.where(left, turned, two)
     size = leaves // steps
     copies = []
     for i in range(steps):
-        for leaf in range(i * size, (i + 1) * size):
-            leaf_local = (locals_[leaf_trans[leaf]] + far[leaf]).astype(BF16)
-            out[leaf] = near[leaf] + jnp.dot(
-                leaf_local, basis_t[leaf], preferred_element_type=F32
+        for leaf in range(i * size, (i + 1) * size, 4):
+            lhs = []
+            for u in range(4):
+                whole = locals_[leaf_trans[leaf + u]] + far[(leaf + u) // 2]
+                lhs.append(jnp.where(left if u % 2 == 0 else jnp.logical_not(left), whole, 0.0))
+            rhs = [
+                basis_t[leaf + u : leaf + u + 2].reshape(2 * k, panels) for u in range(0, 4, 2)
+            ]
+            product = jnp.dot(
+                jnp.concatenate(lhs, axis=0).astype(BF16), jnp.concatenate(rhs, axis=1),
+                preferred_element_type=F32,
             )
+            for u in range(4):
+                columns = slice(u // 2 * panels, (u // 2 + 1) * panels)
+                out[leaf + u] = near[leaf + u] + product[u * r : (u + 1) * r, columns]
         piece = pl.ds(i * size, size)
         copies.append(pltpu.make_async_copy(out.at[piece], out_hbm.at[piece], sems.at[i]))
         copies[-1].start()
@@ -388,7 +418,7 @@
             out_specs=(VMEM,) * 4 + (SMEM,) * 2 + (VMEM,) * 5,
             scratch_shapes=[
                 [pltpu.VMEM((trans_leaf.shape[0], r, 2 * k), F32) for _ in range(PIECES)],
-                pltpu.SemaphoreType.DMA((4 + PIECES + half // 2 // TABLE_ROWS,)),
+                pltpu.SemaphoreType.DMA((5 + half // 2 // TABLE_ROWS,)),
             ],
             compiler_params=params(24),
             name="moments",
@@ -486,16 +516,20 @@
         x.reshape(kinds, x.shape[0] // kinds, 2 * k) for x in (table_low, table_high)
     ]
     wanted = groups.shape[0] - 1 + dev_couple.shape[1]
-    far, box_tables = pl.pallas_call(
+    far, box_tables, leaf_maps = pl.pallas_call(
         functools.partial(far_kernel, len(tables), tuple(offsets)),
-        out_shape=(shape((leaves, r, k), F32), shape((wanted * half, 2 * k), F32)),
-        in_specs=[SMEM] * 4 + [VMEM] * (1 + len(tables)),
-        out_specs=(VMEM, VMEM),
+        out_shape=(
+            shape((leaves // 2, r, 2 * k), F32),
+            shape((wanted * half, 2 * k), F32),
+            shape((2, k, trans_leaf.shape[0] * k), BF16),
+        ),
+        in_specs=[SMEM] * 4 + [VMEM] * (2 + len(tables)),
+        out_specs=(VMEM, VMEM, VMEM),
         compiler_params=params(16),
         cost_estimate=cost(3),
         name="far",
     )(
-        leaf_far.T, leaf_far_couple.T, dev_couple, grp_couple, spread, *tables
+        leaf_far.T, leaf_far_couple.T, dev_couple, grp_couple, spread, leaf_maps, *tables
     )
 
     return pl.pallas_call(
@@ -505,7 +539,7 @@
         out_specs=HBM,
         scratch_shapes=[
             pltpu.VMEM((leaves, r, panels), F32),
-            pltpu.VMEM((trans_leaf.shape[0], r, k), F32),
+            pltpu.VMEM((trans_leaf.shape[0], r, 2 * k), F32),
             pltpu.SemaphoreType.DMA((8,)),
         ],
         compiler_params=params(16),

time: 28.6 us -> 28.4 us (level)
  no operation moved by 1% of the time
where the time goes in v7:
time: 28.4 us; the launch traced here: 28.2 us
  Pallas kernels  13.7 us (48%)
  starting transfers between devices  10.6 us (37%)
  waiting for transfers between devices  2.01 us (7%)
  between operations  1.48 us (5%)
  other arithmetic  0.34 us (1%)
    ppermute x6, starting transfers between devices, swap(): lax.ppermute(x, axis, [(i, i ^ distance) for i in range(lax.axis_size(axi...  5.81 us
    ppermute x1, starting transfers between devices, local(): lax.ppermute(send_second, AXES, partners + [(j, i) for i, j in partners])  4.82 us
    pallas_call x1, Pallas kernels, local(): pl.pallas_call(functools.partial(far_kernel, len(tables), tuple(offsets))...  2.96 us
    pallas_call x1, Pallas kernels, local(): pl.pallas_call(moment_kernel, out_shape=(shape((leaves, r, 2 * k), BF16),...  2.92 us
    pallas_call x1, Pallas kernels, local(): pl.pallas_call(table_kernel, out_shape=(shape((kinds * low_rows, 2 * k),...  2.67 us
    pallas_call x1, Pallas kernels, near_part(): pl.pallas_call(functools.partial(near_kernel, steps, low_rows - half // 2...  2.52 us
    pallas_call x1, Pallas kernels, local(): pl.pallas_call(functools.partial(final_kernel, 8), out_shape=shape((leave...  2.15 us
    ppermute x6, waiting for transfers between devices, swap(): lax.ppermute(x, axis, [(i, i ^ distance) for i in range(lax.axis_size(axi...  2.01 us
  transfers between devices with their start and end apart: 7, of which 3 were waited for; matrix products, arithmetic and copies ran while one was open for 0% of the time, Pallas kernels for 30%

profile of v7, /device:TPU:0, one launch (start us, length us, event | category | flops | bytes accessed | tf_op | source)
XLA Modules:
  0.0 28.2 jit_solution(8449769988603638614)
XLA Ops:
  0.7 2.9 %moments.1 = (bf16[32,16,128]{2,1,0:T(8,128)(2,1)S(1)}, bf16[16,32,128]{2,1,0:T(8,128)(2,1)S(1)}, bf16[16,32,128]{2,1,0:T(8,128)(2,1)S(1)}, f32[16,128]{1,0:T(8,...) custom-call(s32[32]{0:T(128)} %leaf_trans_hbm.1, ...), custom_call_target="tpu_custom_call" | custom-call | tf_op jit(solution)/shard_map/moments/pallas_call | solution.py:402
  3.6 3.0 %collective-permute-start = (f32[16,128]{1,0:T(8,128)S(1)}, f32[16,128]{1,0:T(8,128)S(1)}, u32[]{:S(2)}, u32[]{:S(2)}) collective-permute-start(f32[16,128]{1,0:T(8,128)S(1)} %get-tuple-element.43), channel_id=1, source_target_pairs={{0,1},{1,0},{2,3},{3,2},{4,5},{5,4},{6,7},{7,6},{8,9},{9,8},{10,11... | collective-permute-start | bytes 24584 | tf_op jit(solution)/shard_map/ppermute | solution.py:346
  6.6 0.1 collective-permute-start.2
  6.7 4.8 %collective-permute-start.3 = (bf16[16,32,128]{2,1,0:T(8,128)(2,1)S(1)}, bf16[16,32,128]{2,1,0:T(8,128)(2,1)S(1)}, u32[]{:S(2)}, u32[]{:S(2)}) collective-permute-start(bf16[16,32,128]{2,1,0:T(8,128)(2,1)S(1)} %get-tuple-element.50), channel_id=1, source_target_pairs={{1,2},{3,4},{5,6},{7,8},{9,10},{11,12},{13,14},{15,16},{17,18},{19... | collective-permute-start | bytes 393224 | tf_op jit(solution)/shard_map/ppermute | solution.py:439
  11.5 0.0 collective-permute-done
  11.5 0.1 fusion.2
  11.6 0.0 slice-start
  11.6 0.0 slice-start.1
  11.6 0.0 copy-start.3
  11.6 0.0 copy-start.4
  11.6 0.6 %collective-permute-start.1 = (f32[1,16,64]{2,1,0:T(8,128)S(1)}, f32[1,16,64]{2,1,0:T(8,128)S(1)}, u32[]{:S(2)}, u32[]{:S(2)}) collective-permute-start(f32[1,16,64]{2,1,0:T(8,128)S(1)} %get-tuple-element.46), channel_id=1, source_target_pairs={{0,16},{8,24},{16,0},{24,8},{1,17},{9,25},{17,1},{25,9},{2,18},{10... | collective-permute-start | bytes 12296 | tf_op jit(solution)/shard_map/ppermute | solution.py:346
  12.2 2.7 %table.1 = (f32[7584,128]{1,0:T(8,128)S(1)}, f32[2,16,64,316]{3,2,1,0:T(8,128)S(1)}) custom-call(f32[2,16,64,316]{3,2,1,0:T(8,128)S(1)} %get-tuple-element.47.table, f32[2,32,64,316]{3,2,1,0:T(8,128)} %bitcast.21), custom_call_target="tpu_custom_call" | custom-call | bytes 9437184 | tf_op jit(solution)/shard_map/table/pallas_call | solution.py:449
  14.8 0.5 %collective-permute-done.1 = f32[1,16,64]{2,1,0:T(8,128)S(1)} collective-permute-done((f32[1,16,64]{2,1,0:T(8,128)S(1)}, f32[1,16,64]{2,1,0:T(8,128)S(1)}, u32[]{:S(2)}, u32[]{:S(2)}) %collective-permute-start.1) | collective-permute-done | bytes 4128 | tf_op jit(solution)/shard_map/ppermute | solution.py:346
  15.3 0.0 collective-permute-done.2.first
  15.3 0.0 collective-permute-done.3.second
  15.3 0.6 %collective-permute-start.4 = (f32[2,16,64]{2,1,0:T(8,128)S(1)}, f32[2,16,64]{2,1,0:T(8,128)S(1)}, u32[]{:S(2)}, u32[]{:S(2)}) collective-permute-start(f32[2,16,64]{2,1,0:T(8,128)S(1)} %pad_maximum_fusion.7), channel_id=1, source_target_pairs={{0,8},{8,0},{16,24},{24,16},{1,9},{9,1},{17,25},{25,17},{2,10},{10... | collective-permute-start | bytes 24584 | tf_op jit(solution)/shard_map/ppermute | solution.py:346
  16.6 0.4 %spread.1 = (bf16[64,64,128]{2,1,0:T(8,128)(2,1)S(1)}, s32[16,128]{1,0:T(8,128)S(1)}) custom-call(s32[1]{0:T(128)S(6)} %copy.17.count, bf16[32,16,128]{2,1,0:T(8,128)(2,1)S(1)} %get-tuple-element.52.moments, bf16[16,32,128]{2,1,0:T(8,128)(2,1)S(1)} %collective-permute-done.2.first, bf16[16,32,128]{2,1,0:T(8,128)(2,1)S(1)} %collective-permute-done.3.second), custom_call_target="tpu_custom_call" | custom-call | bytes 3145728 | tf_op jit(solution)/shard_map/spread/pallas_call | solution.py:467
  17.0 0.0 collective-permute-done.4
  17.1 0.1 fusion.1
  17.2 0.1 collective-permute-start.5
  17.2 0.0 slice-done
  17.2 0.0 slice-done.1
  17.2 0.0 copy-done.3
  17.2 0.0 copy-done.4
  17.2 0.0 copy-start
  17.3 0.0 copy-start.1
  17.3 0.0 copy-start.2
  17.3 0.0 copy-start.5
  17.3 2.5 %near.1 = (f32[32,16,128]{2,1,0:T(8,128)S(1)}, f32[2528,128]{1,0:T(8,128)S(1)}) custom-call(s32[160]{0:T(256)S(1)} %copy-done.3, s32[160]{0:T(256)S(1)} %copy-done.4, s32[16,128]{1,0:T(8,128)S(1)} %get-tuple-element.58.count, bf16[32,16,128]{2,1,0:T(8,128)(2,1)S(1)} %get-tuple-element.59.charges, bf16[16,32,128]{2,1,0:T(8,128)(2,1)S(1)} %collective-permute-done.2.first, ...), custom_call_target="tpu_custom_call" | custom-call | bytes 9437184 | tf_op jit(solution)/shard_map/near/pallas_call | solution.py:483
  19.8 0.0 copy-start.6
  19.8 1.2 %collective-permute-done.5 = f32[3,16,128]{2,1,0:T(8,128)S(1)} collective-permute-done((f32[3,16,128]{2,1,0:T(8,128)S(1)}, f32[3,16,128]{2,1,0:T(8,128)S(1)}, u32[]{:S(2)}, u32[]{:S(2)}) %collective-permute-start.5) | collective-permute-done | bytes 24608 | tf_op jit(solution)/shard_map/ppermute | solution.py:346
  21.0 0.1 fusion.3
  21.1 0.1 pad_maximum_fusion.4
  21.2 1.5 %collective-permute-start.6 = (f32[4,16,128]{2,1,0:T(8,128)S(1)}, f32[4,16,128]{2,1,0:T(8,128)S(1)}, u32[]{:S(2)}, u32[]{:S(2)}) collective-permute-start(f32[4,16,128]{2,1,0:T(8,128)S(1)} %pad_maximum_fusion.4), channel_id=1, source_target_pairs={{0,4},{1,5},{2,6},{3,7},{4,0},{5,1},{6,2},{7,3},{8,12},{9,13},{10,... | collective-permute-start | bytes 98312 | tf_op jit(solution)/shard_map/ppermute | solution.py:346
  22.6 0.0 copy-done
  22.6 0.0 copy-done.1
  22.6 0.0 copy-done.2
  22.6 0.0 copy-done.5
  22.6 3.0 %far.1 = (f32[16,16,128]{2,1,0:T(8,128)S(1)}, f32[224,128]{1,0:T(8,128)S(1)}, bf16[2,64,512]{2,1,0:T(8,128)(2,1)S(1)}) custom-call(s32[16,32]{1,0:T(8,128)S(1)} %bitcast.18, s32[16,32]{1,0:T(8,128)S(1)} %bitcast.19, s32[1,4]{1,0:T(1,128)S(1)} %copy-done.5, s32[4,4]{1,0:T(4,128)S(1)} %copy-done.2, bf16[64,64,128]{2,1,0:T(8,128)(2,1)S(1)} %get-tuple-element.66.spread, ...), custom_call_target="tpu_custom_call" | custom-call | bytes 9437184 | tf_op jit(solution)/shard_map/far/pallas_call | solution.py:519
  25.6 0.4 %collective-permute-done.6 = f32[4,16,128]{2,1,0:T(8,128)S(1)} collective-permute-done((f32[4,16,128]{2,1,0:T(8,128)S(1)}, f32[4,16,128]{2,1,0:T(8,128)S(1)}, u32[]{:S(2)}, u32[]{:S(2)}) %collective-permute-start.6) | collective-permute-done | bytes 32800 | tf_op jit(solution)/shard_map/ppermute | solution.py:346
  26.0 0.1 slice_add_fusion
  26.1 0.0 copy-done.6
  26.1 2.2 %final.1 = f32[32,16,128]{2,1,0:T(8,128)} custom-call(s32[32]{0:T(128)S(1)} %get-tuple-element.41.leaf_trans, s32[8]{0:T(128)S(1)} %get-tuple-element.42.dev_trans, s32[1,4]{1,0:T(1,128)S(1)} %copy-done.6, f32[32,16,128]{2,1,0:T(8,128)S(1)} %get-tuple-element.65.near, f32[16,16,128]{2,1,0:T(8,128)S(1)} %get-tuple-element.70.far, ...), custom_call_target="tpu_custom_call" | custom-call | tf_op jit(solution)/shard_map/final/pallas_call | solution.py:535
  (8 shorter events, 0.0 us)
Async XLA Ops:
  3.6 7.9 %collective-permute-start = (f32[16,128]{1,0:T(8,128)S(1)}, f32[16,128]{1,0:T(8,128)S(1)}, u32[]{:S(2)}, u32[]{:S(2)}) collective-permute-start(f32[16,128]{1,0:T(8,128)S(1)} %get-tuple-element.43), channel_id=1, source_target_pairs={{0,1},{1,0},{2,3},{3,2},{4,5},{5,4},{6,7},{7,6},{8,9},{9,8},{10,11... | collective-permute-start | bytes 24584 | tf_op jit(solution)/shard_map/ppermute | solution.py:346
  6.6 8.7 %collective-permute-start.2 = (bf16[16,32,128]{2,1,0:T(8,128)(2,1)S(1)}, bf16[16,32,128]{2,1,0:T(8,128)(2,1)S(1)}, u32[]{:S(2)}, u32[]{:S(2)}) collective-permute-start(bf16[16,32,128]{2,1,0:T(8,128)(2,1)S(1)} %get-tuple-element.49), channel_id=1, source_target_pairs={{0,1},{1,0},{2,3},{3,2},{4,5},{5,4},{6,7},{7,6},{8,9},{9,8},{10,11... | collective-permute-start | bytes 393224 | tf_op jit(solution)/shard_map/ppermute | solution.py:346
  6.7 8.7 %collective-permute-start.3 = (bf16[16,32,128]{2,1,0:T(8,128)(2,1)S(1)}, bf16[16,32,128]{2,1,0:T(8,128)(2,1)S(1)}, u32[]{:S(2)}, u32[]{:S(2)}) collective-permute-start(bf16[16,32,128]{2,1,0:T(8,128)(2,1)S(1)} %get-tuple-element.50), channel_id=1, source_target_pairs={{1,2},{3,4},{5,6},{7,8},{9,10},{11,12},{13,14},{15,16},{17,18},{19... | collective-permute-start | bytes 393224 | tf_op jit(solution)/shard_map/ppermute | solution.py:439
  11.6 5.7 %slice-start = ((s8[5242880]{0:T(1024)(128)(4,1)}), s8[4194304]{0:T(1024)(128)(4,1)S(1)}, s32[]{:S(2)}) async-start(s8[5242880]{0:T(1024)(128)(4,1)} %bitcast.14), calls=%async_computation | async-start | bytes 8388608
  11.6 5.7 %slice-start.1 = ((s8[5242880]{0:T(1024)(128)(4,1)}), s8[1048576]{0:T(1024)(128)(4,1)S(1)}, s32[]{:S(2)}) async-start(s8[5242880]{0:T(1024)(128)(4,1)} %bitcast.14), calls=%async_computation.1 | async-start | bytes 2097152
  11.6 5.7 %copy-start.3 = (s32[160]{0:T(256)S(1)}, s32[160]{0:T(256)}, u32[]{:S(2)}) copy-start(s32[160]{0:T(256)} %targets.1) | copy-start | bytes 1924
  11.6 5.6 %copy-start.4 = (s32[160]{0:T(256)S(1)}, s32[160]{0:T(256)}, u32[]{:S(2)}) copy-start(s32[160]{0:T(256)} %sources.1) | copy-start | bytes 1924
  11.6 3.7 %collective-permute-start.1 = (f32[1,16,64]{2,1,0:T(8,128)S(1)}, f32[1,16,64]{2,1,0:T(8,128)S(1)}, u32[]{:S(2)}, u32[]{:S(2)}) collective-permute-start(f32[1,16,64]{2,1,0:T(8,128)S(1)} %get-tuple-element.46), channel_id=1, source_target_pairs={{0,16},{8,24},{16,0},{24,8},{1,17},{9,25},{17,1},{25,9},{2,18},{10... | collective-permute-start | bytes 12296 | tf_op jit(solution)/shard_map/ppermute | solution.py:346
  15.3 1.7 %collective-permute-start.4 = (f32[2,16,64]{2,1,0:T(8,128)S(1)}, f32[2,16,64]{2,1,0:T(8,128)S(1)}, u32[]{:S(2)}, u32[]{:S(2)}) collective-permute-start(f32[2,16,64]{2,1,0:T(8,128)S(1)} %pad_maximum_fusion.7), channel_id=1, source_target_pairs={{0,8},{8,0},{16,24},{24,16},{1,9},{9,1},{17,25},{25,17},{2,10},{10... | collective-permute-start | bytes 24584 | tf_op jit(solution)/shard_map/ppermute | solution.py:346
  17.2 3.8 %collective-permute-start.5 = (f32[3,16,128]{2,1,0:T(8,128)S(1)}, f32[3,16,128]{2,1,0:T(8,128)S(1)}, u32[]{:S(2)}, u32[]{:S(2)}) collective-permute-start(f32[3,16,128]{2,1,0:T(8,128)S(1)} %fusion.1), channel_id=1, source_target_pairs={{0,2},{1,3},{2,0},{3,1},{4,6},{5,7},{6,4},{7,5},{8,10},{9,11},{10,... | collective-permute-start | bytes 73736 | tf_op jit(solution)/shard_map/ppermute | solution.py:346
  17.2 5.4 %copy-start = (s32[32,16]{0,1:T(8,128)S(1)}, s32[32,16]{0,1:T(8,128)}, u32[]{:S(2)}) copy-start(s32[32,16]{0,1:T(8,128)} %param.22) | copy-start | bytes 6148
  17.3 5.4 %copy-start.1 = (s32[32,16]{0,1:T(8,128)S(1)}, s32[32,16]{0,1:T(8,128)}, u32[]{:S(2)}) copy-start(s32[32,16]{0,1:T(8,128)} %param.23) | copy-start | bytes 6148
  17.3 5.4 %copy-start.2 = (s32[4,4]{1,0:T(4,128)S(1)}, s32[4,4]{1,0:T(4,128)}, u32[]{:S(2)}) copy-start(s32[4,4]{1,0:T(4,128)} %grp_couple.1) | copy-start | bytes 196
  17.3 5.4 %copy-start.5 = (s32[1,4]{1,0:T(1,128)S(1)}, s32[1,4]{1,0:T(1,128)}, u32[]{:S(2)}) copy-start(s32[1,4]{1,0:T(1,128)} %dev_couple.1) | copy-start | bytes 52
  19.8 6.3 %copy-start.6 = (s32[1,4]{1,0:T(1,128)S(1)}, s32[1,4]{1,0:T(1,128)}, u32[]{:S(2)}) copy-start(s32[1,4]{1,0:T(1,128)} %dev_list.1) | copy-start | bytes 52
  21.2 4.8 %collective-permute-start.6 = (f32[4,16,128]{2,1,0:T(8,128)S(1)}, f32[4,16,128]{2,1,0:T(8,128)S(1)}, u32[]{:S(2)}, u32[]{:S(2)}) collective-permute-start(f32[4,16,128]{2,1,0:T(8,128)S(1)} %pad_maximum_fusion.4), channel_id=1, source_target_pairs={{0,4},{1,5},{2,6},{3,7},{4,0},{5,1},{6,2},{7,3},{8,12},{9,13},{10,... | collective-permute-start | bytes 98312 | tf_op jit(solution)/shard_map/ppermute | solution.py:346

commit v8 on v7

--- a/solution.py
+++ b/solution.py
@@ -71,15 +71,20 @@
         classes[lane][...] = jnp.zeros_like(classes[lane])
     for copy in copies[:3]:
         copy.wait()
-    for piece in range(PIECES):
-        for leaf in range(piece * size, (piece + 1) * size):
-            basis = basis_t[leaf]
-            twice = lax.dot_general(
-                charges[leaf], jnp.concatenate([basis, basis], axis=0), NT,
-                preferred_element_type=F32,
-            )
+    panels = charges.shape[2]
+    for start in range(0, leaves, PIECES):
+        product = lax.dot_general(
+            charges[start : start + PIECES].reshape(PIECES * r, panels),
+            basis_t[start : start + PIECES].reshape(PIECES * k, panels), NT,
+            preferred_element_type=F32,
+        )
+        for u in range(PIECES):
+            leaf = start + u
+            pair = product[u * r : (u + 1) * r, u // 2 * 2 * k : (u // 2 + 1) * 2 * k]
+            turned = pltpu.roll(pair, k, 1)
+            twice = jnp.where(left, pair, turned) if u % 2 == 0 else jnp.where(left, turned, pair)
             kind = leaf_trans[leaf]
-            lane = classes[leaf % PIECES]
+            lane = classes[u]
             lane[kind] = lane[kind] + twice
             high = twice.astype(BF16).astype(F32)
             moments[leaf] = jnp.where(left, high, twice - high).astype(BF16)
@@ -146,9 +151,11 @@
         copy.start()
     rows = out.shape[0] // table.shape[3]
     relayout_rows(table, out, 0, low_rows, rows)
-    for copy in copies:
+    for i, copy in enumerate(copies):
         copy.wait()
-    relayout_rows(high, out, low_rows, rows - low_rows, rows)
+        begin = i * TABLE_ROWS
+        if low_rows + begin < rows:
+            relayout_rows(high.at[:, begin : begin + TABLE_ROWS], out, low_rows + begin, TABLE_ROWS, rows)
 
 
 def halo_places(leaves):
@@ -412,13 +419,13 @@
                 shape(basis_t.shape, BF16),
                 shape(trans_leaf.shape, F32),
                 shape(trans_dev.shape, F32),
-                shape((2, half // 2, k, kinds), F32),
+                shape((2, half // 4, k, kinds), F32),
             ),
             in_specs=[HBM, SMEM] + [HBM] * 5,
             out_specs=(VMEM,) * 4 + (SMEM,) * 2 + (VMEM,) * 5,
             scratch_shapes=[
                 [pltpu.VMEM((trans_leaf.shape[0], r, 2 * k), F32) for _ in range(PIECES)],
-                pltpu.SemaphoreType.DMA((5 + half // 2 // TABLE_ROWS,)),
+                pltpu.SemaphoreType.DMA((5 + half // 4 // TABLE_ROWS,)),
             ],
             compiler_params=params(24),
             name="moments",
@@ -450,11 +457,11 @@
         table_kernel,
         out_shape=(
             shape((kinds * low_rows, 2 * k), F32),
-            shape((2, half // 2, k, kinds), F32),
+            shape((2, half - half // 4, k, kinds), F32),
         ),
         in_specs=[VMEM, HBM],
         out_specs=(VMEM, VMEM),
-        scratch_shapes=[pltpu.SemaphoreType.DMA((half // 2 // TABLE_ROWS,))],
+        scratch_shapes=[pltpu.SemaphoreType.DMA(((half - half // 4) // TABLE_ROWS,))],
         compiler_params=params(16),
         cost_estimate=cost(3),
         name="table",
@@ -481,7 +488,7 @@
 
     def near_part():
         return pl.pallas_call(
-            functools.partial(near_kernel, steps, low_rows - half // 2, high_rows),
+            functools.partial(near_kernel, steps, low_rows - half // 4, high_rows),
             out_shape=(
                 shape((leaves, r, panels), F32),
                 shape((kinds * high_rows, 2 * k), F32),

time: 28.4 us -> 27.9 us (0.982)
  Pallas kernels: 13.7 us -> 13.1 us
  starting transfers between devices: 10.6 us -> 10.9 us
    ppermute x6, starting transfers between devices: 5.81 us -> 6.11 us  [swap(): lax.ppermute(x, axis, [(i, i ^ distance) for i in range(lax.axis_size(axi...]
    pallas_call x1, Pallas kernels: 2.92 us -> 2.62 us  [local(): pl.pallas_call(moment_kernel, out_shape=(shape((leaves, r, 2 * k), BF16),...]
where the time goes in v8:
time: 27.9 us; the launch traced here: 27.7 us
  Pallas kernels  13.1 us (47%)
  starting transfers between devices  10.9 us (39%)
  waiting for transfers between devices  1.73 us (6%)
  between operations  1.49 us (5%)
  other arithmetic  0.34 us (1%)
    ppermute x6, starting transfers between devices, swap(): lax.ppermute(x, axis, [(i, i ^ distance) for i in range(lax.axis_size(axi...  6.11 us
    ppermute x1, starting transfers between devices, local(): lax.ppermute(send_second, AXES, partners + [(j, i) for i, j in partners])  4.83 us
    pallas_call x1, Pallas kernels, local(): pl.pallas_call(functools.partial(far_kernel, len(tables), tuple(offsets))...  2.96 us
    pallas_call x1, Pallas kernels, local(): pl.pallas_call(moment_kernel, out_shape=(shape((leaves, r, 2 * k), BF16),...  2.62 us
    pallas_call x1, Pallas kernels, near_part(): pl.pallas_call(functools.partial(near_kernel, steps, low_rows - half // 4...  2.52 us
    pallas_call x1, Pallas kernels, local(): pl.pallas_call(table_kernel, out_shape=(shape((kinds * low_rows, 2 * k),...  2.41 us
    pallas_call x1, Pallas kernels, local(): pl.pallas_call(functools.partial(final_kernel, 8), out_shape=shape((leave...  2.15 us
    ppermute x6, waiting for transfers between devices, swap(): lax.ppermute(x, axis, [(i, i ^ distance) for i in range(lax.axis_size(axi...  1.73 us
  transfers between devices with their start and end apart: 7, of which 3 were waited for; matrix products, arithmetic and copies ran while one was open for 0% of the time, Pallas kernels for 30%

profile of v8, /device:TPU:0, one launch (start us, length us, event | category | flops | bytes accessed | tf_op | source)
XLA Modules:
  0.0 27.7 jit_solution(17857983584699289320)
XLA Ops:
  0.7 0.0 slice-start
  0.7 2.6 %moments.1 = (bf16[32,16,128]{2,1,0:T(8,128)(2,1)S(1)}, bf16[16,32,128]{2,1,0:T(8,128)(2,1)S(1)}, bf16[16,32,128]{2,1,0:T(8,128)(2,1)S(1)}, f32[16,128]{1,0:T(8,...) custom-call(s32[32]{0:T(128)} %leaf_trans_hbm.1, ...), custom_call_target="tpu_custom_call" | custom-call | tf_op jit(solution)/shard_map/moments/pallas_call | solution.py:409
  3.3 0.0 copy-start.3
  3.3 0.0 copy-start.4
  3.3 3.0 %collective-permute-start = (f32[16,128]{1,0:T(8,128)S(1)}, f32[16,128]{1,0:T(8,128)S(1)}, u32[]{:S(2)}, u32[]{:S(2)}) collective-permute-start(f32[16,128]{1,0:T(8,128)S(1)} %get-tuple-element.43), channel_id=1, source_target_pairs={{0,1},{1,0},{2,3},{3,2},{4,5},{5,4},{6,7},{7,6},{8,9},{9,8},{10,11... | collective-permute-start | bytes 24584 | tf_op jit(solution)/shard_map/ppermute | solution.py:353
  6.3 0.1 collective-permute-start.2
  6.4 4.8 %collective-permute-start.3 = (bf16[16,32,128]{2,1,0:T(8,128)(2,1)S(1)}, bf16[16,32,128]{2,1,0:T(8,128)(2,1)S(1)}, u32[]{:S(2)}, u32[]{:S(2)}) collective-permute-start(bf16[16,32,128]{2,1,0:T(8,128)(2,1)S(1)} %get-tuple-element.50), channel_id=1, source_target_pairs={{1,2},{3,4},{5,6},{7,8},{9,10},{11,12},{13,14},{15,16},{17,18},{19... | collective-permute-start | bytes 393224 | tf_op jit(solution)/shard_map/ppermute | solution.py:446
  11.2 0.0 collective-permute-done
  11.3 0.1 fusion.2
  11.3 0.0 slice-start.1
  11.3 0.6 %collective-permute-start.1 = (f32[1,16,64]{2,1,0:T(8,128)S(1)}, f32[1,16,64]{2,1,0:T(8,128)S(1)}, u32[]{:S(2)}, u32[]{:S(2)}) collective-permute-start(f32[1,16,64]{2,1,0:T(8,128)S(1)} %get-tuple-element.46), channel_id=1, source_target_pairs={{0,16},{8,24},{16,0},{24,8},{1,17},{9,25},{17,1},{25,9},{2,18},{10... | collective-permute-start | bytes 12296 | tf_op jit(solution)/shard_map/ppermute | solution.py:353
  11.9 2.4 %table.1 = (f32[7584,128]{1,0:T(8,128)S(1)}, f32[2,24,64,316]{3,2,1,0:T(8,128)S(1)}) custom-call(f32[2,8,64,316]{3,2,1,0:T(8,128)S(1)} %get-tuple-element.47.table, f32[2,32,64,316]{3,2,1,0:T(8,128)} %bitcast.21), custom_call_target="tpu_custom_call" | custom-call | bytes 9437184 | tf_op jit(solution)/shard_map/table/pallas_call | solution.py:456
  14.3 0.7 %collective-permute-done.1 = f32[1,16,64]{2,1,0:T(8,128)S(1)} collective-permute-done((f32[1,16,64]{2,1,0:T(8,128)S(1)}, f32[1,16,64]{2,1,0:T(8,128)S(1)}, u32[]{:S(2)}, u32[]{:S(2)}) %collective-permute-start.1) | collective-permute-done | bytes 4128 | tf_op jit(solution)/shard_map/ppermute | solution.py:353
  15.0 0.0 collective-permute-done.2.first
  15.0 0.0 collective-permute-done.3.second
  15.1 0.4 %collective-permute-start.4 = (f32[2,16,64]{2,1,0:T(8,128)S(1)}, f32[2,16,64]{2,1,0:T(8,128)S(1)}, u32[]{:S(2)}, u32[]{:S(2)}) collective-permute-start(f32[2,16,64]{2,1,0:T(8,128)S(1)} %pad_maximum_fusion.7), channel_id=1, source_target_pairs={{0,8},{8,0},{16,24},{24,16},{1,9},{9,1},{17,25},{25,17},{2,10},{10... | collective-permute-start | bytes 24584 | tf_op jit(solution)/shard_map/ppermute | solution.py:353
  16.1 0.4 %spread.1 = (bf16[64,64,128]{2,1,0:T(8,128)(2,1)S(1)}, s32[16,128]{1,0:T(8,128)S(1)}) custom-call(s32[1]{0:T(128)S(6)} %copy.17.count, bf16[32,16,128]{2,1,0:T(8,128)(2,1)S(1)} %get-tuple-element.52.moments, bf16[16,32,128]{2,1,0:T(8,128)(2,1)S(1)} %collective-permute-done.2.first, bf16[16,32,128]{2,1,0:T(8,128)(2,1)S(1)} %collective-permute-done.3.second), custom_call_target="tpu_custom_call" | custom-call | bytes 3145728 | tf_op jit(solution)/shard_map/spread/pallas_call | solution.py:474
  16.5 0.0 collective-permute-done.4
  16.6 0.1 fusion.1
  16.6 0.3 %collective-permute-start.5 = (f32[3,16,128]{2,1,0:T(8,128)S(1)}, f32[3,16,128]{2,1,0:T(8,128)S(1)}, u32[]{:S(2)}, u32[]{:S(2)}) collective-permute-start(f32[3,16,128]{2,1,0:T(8,128)S(1)} %fusion.1), channel_id=1, source_target_pairs={{0,2},{1,3},{2,0},{3,1},{4,6},{5,7},{6,4},{7,5},{8,10},{9,11},{10,... | collective-permute-start | bytes 73736 | tf_op jit(solution)/shard_map/ppermute | solution.py:353
  17.0 0.0 slice-done
  17.0 0.0 copy-done.3
  17.0 0.0 copy-done.4
  17.0 0.0 slice-done.1
  17.0 0.0 copy-start
  17.0 0.0 copy-start.1
  17.0 0.0 copy-start.2
  17.0 0.0 copy-start.5
  17.0 2.5 %near.1 = (f32[32,16,128]{2,1,0:T(8,128)S(1)}, f32[2528,128]{1,0:T(8,128)S(1)}) custom-call(s32[160]{0:T(256)S(1)} %copy-done.3, s32[160]{0:T(256)S(1)} %copy-done.4, s32[16,128]{1,0:T(8,128)S(1)} %get-tuple-element.58.count, bf16[32,16,128]{2,1,0:T(8,128)(2,1)S(1)} %get-tuple-element.59.charges, bf16[16,32,128]{2,1,0:T(8,128)(2,1)S(1)} %collective-permute-done.2.first, ...), custom_call_target="tpu_custom_call" | custom-call | bytes 9437184 | tf_op jit(solution)/shard_map/near/pallas_call | solution.py:490
  19.6 0.0 copy-start.6
  19.6 0.9 %collective-permute-done.5 = f32[3,16,128]{2,1,0:T(8,128)S(1)} collective-permute-done((f32[3,16,128]{2,1,0:T(8,128)S(1)}, f32[3,16,128]{2,1,0:T(8,128)S(1)}, u32[]{:S(2)}, u32[]{:S(2)}) %collective-permute-start.5) | collective-permute-done | bytes 24608 | tf_op jit(solution)/shard_map/ppermute | solution.py:353
  20.5 0.1 fusion.3
  20.6 0.1 pad_maximum_fusion.4
  20.6 1.7 %collective-permute-start.6 = (f32[4,16,128]{2,1,0:T(8,128)S(1)}, f32[4,16,128]{2,1,0:T(8,128)S(1)}, u32[]{:S(2)}, u32[]{:S(2)}) collective-permute-start(f32[4,16,128]{2,1,0:T(8,128)S(1)} %pad_maximum_fusion.4), channel_id=1, source_target_pairs={{0,4},{1,5},{2,6},{3,7},{4,0},{5,1},{6,2},{7,3},{8,12},{9,13},{10,... | collective-permute-start | bytes 98312 | tf_op jit(solution)/shard_map/ppermute | solution.py:353
  22.4 0.0 copy-done
  22.4 0.0 copy-done.1
  22.4 0.0 copy-done.2
  22.4 0.0 copy-done.5
  22.4 3.0 %far.1 = (f32[16,16,128]{2,1,0:T(8,128)S(1)}, f32[224,128]{1,0:T(8,128)S(1)}, bf16[2,64,512]{2,1,0:T(8,128)(2,1)S(1)}) custom-call(s32[16,32]{1,0:T(8,128)S(1)} %bitcast.18, s32[16,32]{1,0:T(8,128)S(1)} %bitcast.19, s32[1,4]{1,0:T(1,128)S(1)} %copy-done.5, s32[4,4]{1,0:T(4,128)S(1)} %copy-done.2, bf16[64,64,128]{2,1,0:T(8,128)(2,1)S(1)} %get-tuple-element.66.spread, ...), custom_call_target="tpu_custom_call" | custom-call | bytes 9437184 | tf_op jit(solution)/shard_map/far/pallas_call | solution.py:526
  25.4 0.1 collective-permute-done.6
  25.5 0.1 slice_add_fusion
  25.6 0.0 copy-done.6
  25.6 2.2 %final.1 = f32[32,16,128]{2,1,0:T(8,128)} custom-call(s32[32]{0:T(128)S(1)} %get-tuple-element.41.leaf_trans, s32[8]{0:T(128)S(1)} %get-tuple-element.42.dev_trans, s32[1,4]{1,0:T(1,128)S(1)} %copy-done.6, f32[32,16,128]{2,1,0:T(8,128)S(1)} %get-tuple-element.65.near, f32[16,16,128]{2,1,0:T(8,128)S(1)} %get-tuple-element.70.far, ...), custom_call_target="tpu_custom_call" | custom-call | tf_op jit(solution)/shard_map/final/pallas_call | solution.py:542
  (8 shorter events, 0.0 us)
Async XLA Ops:
  0.7 16.3 %slice-start = ((s8[5242880]{0:T(1024)(128)(4,1)}), s8[4194304]{0:T(1024)(128)(4,1)S(1)}, s32[]{:S(2)}) async-start(s8[5242880]{0:T(1024)(128)(4,1)} %bitcast.14), calls=%async_computation | async-start | bytes 8388608
  3.3 13.7 %copy-start.3 = (s32[160]{0:T(256)S(1)}, s32[160]{0:T(256)}, u32[]{:S(2)}) copy-start(s32[160]{0:T(256)} %targets.1) | copy-start | bytes 1924
  3.3 13.7 %copy-start.4 = (s32[160]{0:T(256)S(1)}, s32[160]{0:T(256)}, u32[]{:S(2)}) copy-start(s32[160]{0:T(256)} %sources.1) | copy-start | bytes 1924
  3.3 7.9 %collective-permute-start = (f32[16,128]{1,0:T(8,128)S(1)}, f32[16,128]{1,0:T(8,128)S(1)}, u32[]{:S(2)}, u32[]{:S(2)}) collective-permute-start(f32[16,128]{1,0:T(8,128)S(1)} %get-tuple-element.43), channel_id=1, source_target_pairs={{0,1},{1,0},{2,3},{3,2},{4,5},{5,4},{6,7},{7,6},{8,9},{9,8},{10,11... | collective-permute-start | bytes 24584 | tf_op jit(solution)/shard_map/ppermute | solution.py:353
  6.3 8.7 %collective-permute-start.2 = (bf16[16,32,128]{2,1,0:T(8,128)(2,1)S(1)}, bf16[16,32,128]{2,1,0:T(8,128)(2,1)S(1)}, u32[]{:S(2)}, u32[]{:S(2)}) collective-permute-start(bf16[16,32,128]{2,1,0:T(8,128)(2,1)S(1)} %get-tuple-element.49), channel_id=1, source_target_pairs={{0,1},{1,0},{2,3},{3,2},{4,5},{5,4},{6,7},{7,6},{8,9},{9,8},{10,11... | collective-permute-start | bytes 393224 | tf_op jit(solution)/shard_map/ppermute | solution.py:353
  6.4 8.6 %collective-permute-start.3 = (bf16[16,32,128]{2,1,0:T(8,128)(2,1)S(1)}, bf16[16,32,128]{2,1,0:T(8,128)(2,1)S(1)}, u32[]{:S(2)}, u32[]{:S(2)}) collective-permute-start(bf16[16,32,128]{2,1,0:T(8,128)(2,1)S(1)} %get-tuple-element.50), channel_id=1, source_target_pairs={{1,2},{3,4},{5,6},{7,8},{9,10},{11,12},{13,14},{15,16},{17,18},{19... | collective-permute-start | bytes 393224 | tf_op jit(solution)/shard_map/ppermute | solution.py:446
  11.3 5.7 %slice-start.1 = ((s8[5242880]{0:T(1024)(128)(4,1)}), s8[1048576]{0:T(1024)(128)(4,1)S(1)}, s32[]{:S(2)}) async-start(s8[5242880]{0:T(1024)(128)(4,1)} %bitcast.14), calls=%async_computation.1 | async-start | bytes 2097152
  11.3 3.7 %collective-permute-start.1 = (f32[1,16,64]{2,1,0:T(8,128)S(1)}, f32[1,16,64]{2,1,0:T(8,128)S(1)}, u32[]{:S(2)}, u32[]{:S(2)}) collective-permute-start(f32[1,16,64]{2,1,0:T(8,128)S(1)} %get-tuple-element.46), channel_id=1, source_target_pairs={{0,16},{8,24},{16,0},{24,8},{1,17},{9,25},{17,1},{25,9},{2,18},{10... | collective-permute-start | bytes 12296 | tf_op jit(solution)/shard_map/ppermute | solution.py:353
  15.1 1.5 %collective-permute-start.4 = (f32[2,16,64]{2,1,0:T(8,128)S(1)}, f32[2,16,64]{2,1,0:T(8,128)S(1)}, u32[]{:S(2)}, u32[]{:S(2)}) collective-permute-start(f32[2,16,64]{2,1,0:T(8,128)S(1)} %pad_maximum_fusion.7), channel_id=1, source_target_pairs={{0,8},{8,0},{16,24},{24,16},{1,9},{9,1},{17,25},{25,17},{2,10},{10... | collective-permute-start | bytes 24584 | tf_op jit(solution)/shard_map/ppermute | solution.py:353
  16.6 3.8 %collective-permute-start.5 = (f32[3,16,128]{2,1,0:T(8,128)S(1)}, f32[3,16,128]{2,1,0:T(8,128)S(1)}, u32[]{:S(2)}, u32[]{:S(2)}) collective-permute-start(f32[3,16,128]{2,1,0:T(8,128)S(1)} %fusion.1), channel_id=1, source_target_pairs={{0,2},{1,3},{2,0},{3,1},{4,6},{5,7},{6,4},{7,5},{8,10},{9,11},{10,... | collective-permute-start | bytes 73736 | tf_op jit(solution)/shard_map/ppermute | solution.py:353
  17.0 5.4 %copy-start = (s32[32,16]{0,1:T(8,128)S(1)}, s32[32,16]{0,1:T(8,128)}, u32[]{:S(2)}) copy-start(s32[32,16]{0,1:T(8,128)} %param.22) | copy-start | bytes 6148
  17.0 5.4 %copy-start.1 = (s32[32,16]{0,1:T(8,128)S(1)}, s32[32,16]{0,1:T(8,128)}, u32[]{:S(2)}) copy-start(s32[32,16]{0,1:T(8,128)} %param.23) | copy-start | bytes 6148
  17.0 5.4 %copy-start.2 = (s32[4,4]{1,0:T(4,128)S(1)}, s32[4,4]{1,0:T(4,128)}, u32[]{:S(2)}) copy-start(s32[4,4]{1,0:T(4,128)} %grp_couple.1) | copy-start | bytes 196
  17.0 5.4 %copy-start.5 = (s32[1,4]{1,0:T(1,128)S(1)}, s32[1,4]{1,0:T(1,128)}, u32[]{:S(2)}) copy-start(s32[1,4]{1,0:T(1,128)} %dev_couple.1) | copy-start | bytes 52
  19.6 6.0 %copy-start.6 = (s32[1,4]{1,0:T(1,128)S(1)}, s32[1,4]{1,0:T(1,128)}, u32[]{:S(2)}) copy-start(s32[1,4]{1,0:T(1,128)} %dev_list.1) | copy-start | bytes 52
  20.6 4.8 %collective-permute-start.6 = (f32[4,16,128]{2,1,0:T(8,128)S(1)}, f32[4,16,128]{2,1,0:T(8,128)S(1)}, u32[]{:S(2)}, u32[]{:S(2)}) collective-permute-start(f32[4,16,128]{2,1,0:T(8,128)S(1)} %pad_maximum_fusion.4), channel_id=1, source_target_pairs={{0,4},{1,5},{2,6},{3,7},{4,0},{5,1},{6,2},{7,3},{8,12},{9,13},{10,... | collective-permute-start | bytes 98312 | tf_op jit(solution)/shard_map/ppermute | solution.py:353

commit v9 on v8

--- a/solution.py
+++ b/solution.py
@@ -15,7 +15,7 @@
 SMEM = pl.BlockSpec(memory_space=pltpu.SMEM)
 HBM = pl.BlockSpec(memory_space=pltpu.HBM)
 MIB = 2**20
-TABLE_ROWS = 8
+TABLE_ROWS = 4
 PIECES = 4
 
 
@@ -419,13 +419,13 @@
                 shape(basis_t.shape, BF16),
                 shape(trans_leaf.shape, F32),
                 shape(trans_dev.shape, F32),
-                shape((2, half // 4, k, kinds), F32),
+                shape((2, half // 8, k, kinds), F32),
             ),
             in_specs=[HBM, SMEM] + [HBM] * 5,
             out_specs=(VMEM,) * 4 + (SMEM,) * 2 + (VMEM,) * 5,
             scratch_shapes=[
                 [pltpu.VMEM((trans_leaf.shape[0], r, 2 * k), F32) for _ in range(PIECES)],
-                pltpu.SemaphoreType.DMA((5 + half // 4 // TABLE_ROWS,)),
+                pltpu.SemaphoreType.DMA((5 + half // 8 // TABLE_ROWS,)),
             ],
             compiler_params=params(24),
             name="moments",
@@ -457,11 +457,11 @@
         table_kernel,
         out_shape=(
             shape((kinds * low_rows, 2 * k), F32),
-            shape((2, half - half // 4, k, kinds), F32),
+            shape((2, half - half // 8, k, kinds), F32),
         ),
         in_specs=[VMEM, HBM],
         out_specs=(VMEM, VMEM),
-        scratch_shapes=[pltpu.SemaphoreType.DMA(((half - half // 4) // TABLE_ROWS,))],
+        scratch_shapes=[pltpu.SemaphoreType.DMA(((half - half // 8) // TABLE_ROWS,))],
         compiler_params=params(16),
         cost_estimate=cost(3),
         name="table",
@@ -488,7 +488,7 @@
 
     def near_part():
         return pl.pallas_call(
-            functools.partial(near_kernel, steps, low_rows - half // 4, high_rows),
+            functools.partial(near_kernel, steps, low_rows - half // 8, high_rows),
             out_shape=(
                 shape((leaves, r, panels), F32),
                 shape((kinds * high_rows, 2 * k), F32),

time: 27.9 us -> 29 us (1.039)
  Pallas kernels: 13.1 us -> 14.2 us
  starting transfers between devices: 10.9 us -> 10.2 us
  waiting for transfers between devices: 1.73 us -> 2.42 us
    pallas_call x1, Pallas kernels: 2.41 us -> 3.54 us  [local(): pl.pallas_call(table_kernel, out_shape=(shape((kinds * low_rows, 2 * k),...]
    ppermute x6, starting transfers between devices: 6.11 us -> 5.37 us  [swap(): lax.ppermute(x, axis, [(i, i ^ distance) for i in range(lax.axis_size(axi...]
    ppermute x6, waiting for transfers between devices: 1.73 us -> 2.42 us  [swap(): lax.ppermute(x, axis, [(i, i ^ distance) for i in range(lax.axis_size(axi...]
  transfers between devices with their start and end apart: 7 -> 7, of which waited for: 3 -> 2; matrix products, arithmetic and copies ran while one was open for 0% -> 0% of each run, Pallas kernels for 30% -> 33%
where the time goes in v9:
time: 29 us; the launch traced here: 28.9 us
  Pallas kernels  14.2 us (49%)
  starting transfers between devices  10.2 us (35%)
  waiting for transfers between devices  2.42 us (8%)
  between operations  1.54 us (5%)
  other arithmetic  0.34 us (1%)
    ppermute x6, starting transfers between devices, swap(): lax.ppermute(x, axis, [(i, i ^ distance) for i in range(lax.axis_size(axi...  5.37 us
    ppermute x1, starting transfers between devices, local(): lax.ppermute(send_second, AXES, partners + [(j, i) for i, j in partners])  4.83 us
    pallas_call x1, Pallas kernels, local(): pl.pallas_call(table_kernel, out_shape=(shape((kinds * low_rows, 2 * k),...  3.54 us
    pallas_call x1, Pallas kernels, local(): pl.pallas_call(functools.partial(far_kernel, len(tables), tuple(offsets))...  2.96 us
    pallas_call x1, Pallas kernels, local(): pl.pallas_call(moment_kernel, out_shape=(shape((leaves, r, 2 * k), BF16),...  2.62 us
    pallas_call x1, Pallas kernels, near_part(): pl.pallas_call(functools.partial(near_kernel, steps, low_rows - half // 8...  2.52 us
    ppermute x6, waiting for transfers between devices, swap(): lax.ppermute(x, axis, [(i, i ^ distance) for i in range(lax.axis_size(axi...  2.42 us
    pallas_call x1, Pallas kernels, local(): pl.pallas_call(functools.partial(final_kernel, 8), out_shape=shape((leave...  2.15 us
  transfers between devices with their start and end apart: 7, of which 2 were waited for; matrix products, arithmetic and copies ran while one was open for 0% of the time, Pallas kernels for 33%

profile of v9, /device:TPU:0, one launch (start us, length us, event | category | flops | bytes accessed | tf_op | source)
XLA Modules:
  0.0 28.9 jit_solution(6384962741326049235)
XLA Ops:
  0.7 0.0 slice-start
  0.7 2.6 %moments.1 = (bf16[32,16,128]{2,1,0:T(8,128)(2,1)S(1)}, bf16[16,32,128]{2,1,0:T(8,128)(2,1)S(1)}, bf16[16,32,128]{2,1,0:T(8,128)(2,1)S(1)}, f32[16,128]{1,0:T(8,...) custom-call(s32[32]{0:T(128)} %leaf_trans_hbm.1, ...), custom_call_target="tpu_custom_call" | custom-call | tf_op jit(solution)/shard_map/moments/pallas_call | solution.py:409
  3.3 0.0 copy-start.3
  3.3 0.0 copy-start.4
  3.3 3.0 %collective-permute-start = (f32[16,128]{1,0:T(8,128)S(1)}, f32[16,128]{1,0:T(8,128)S(1)}, u32[]{:S(2)}, u32[]{:S(2)}) collective-permute-start(f32[16,128]{1,0:T(8,128)S(1)} %get-tuple-element.43), channel_id=1, source_target_pairs={{0,1},{1,0},{2,3},{3,2},{4,5},{5,4},{6,7},{7,6},{8,9},{9,8},{10,11... | collective-permute-start | bytes 24584 | tf_op jit(solution)/shard_map/ppermute | solution.py:353
  6.3 0.1 collective-permute-start.2
  6.4 4.8 %collective-permute-start.3 = (bf16[16,32,128]{2,1,0:T(8,128)(2,1)S(1)}, bf16[16,32,128]{2,1,0:T(8,128)(2,1)S(1)}, u32[]{:S(2)}, u32[]{:S(2)}) collective-permute-start(bf16[16,32,128]{2,1,0:T(8,128)(2,1)S(1)} %get-tuple-element.50), channel_id=1, source_target_pairs={{1,2},{3,4},{5,6},{7,8},{9,10},{11,12},{13,14},{15,16},{17,18},{19... | collective-permute-start | bytes 393224 | tf_op jit(solution)/shard_map/ppermute | solution.py:446
  11.2 0.0 collective-permute-done
  11.3 0.1 fusion.2
  11.3 0.0 slice-start.1
  11.3 0.6 %collective-permute-start.1 = (f32[1,16,64]{2,1,0:T(8,128)S(1)}, f32[1,16,64]{2,1,0:T(8,128)S(1)}, u32[]{:S(2)}, u32[]{:S(2)}) collective-permute-start(f32[1,16,64]{2,1,0:T(8,128)S(1)} %get-tuple-element.46), channel_id=1, source_target_pairs={{0,16},{8,24},{16,0},{24,8},{1,17},{9,25},{17,1},{25,9},{2,18},{10... | collective-permute-start | bytes 12296 | tf_op jit(solution)/shard_map/ppermute | solution.py:353
  11.9 3.5 %table.1 = (f32[7584,128]{1,0:T(8,128)S(1)}, f32[2,28,64,316]{3,2,1,0:T(8,128)S(1)}) custom-call(f32[2,4,64,316]{3,2,1,0:T(8,128)S(1)} %get-tuple-element.47.table, f32[2,32,64,316]{3,2,1,0:T(8,128)} %bitcast.21), custom_call_target="tpu_custom_call" | custom-call | bytes 9437184 | tf_op jit(solution)/shard_map/table/pallas_call | solution.py:456
  15.4 0.0 collective-permute-done.1
  15.5 0.0 collective-permute-done.2.first
  15.5 0.0 collective-permute-done.3.second
  15.5 1.1 %collective-permute-start.4 = (f32[2,16,64]{2,1,0:T(8,128)S(1)}, f32[2,16,64]{2,1,0:T(8,128)S(1)}, u32[]{:S(2)}, u32[]{:S(2)}) collective-permute-start(f32[2,16,64]{2,1,0:T(8,128)S(1)} %pad_maximum_fusion.7), channel_id=1, source_target_pairs={{0,8},{8,0},{16,24},{24,16},{1,9},{9,1},{17,25},{25,17},{2,10},{10... | collective-permute-start | bytes 24584 | tf_op jit(solution)/shard_map/ppermute | solution.py:353
  17.2 0.4 %spread.1 = (bf16[64,64,128]{2,1,0:T(8,128)(2,1)S(1)}, s32[16,128]{1,0:T(8,128)S(1)}) custom-call(s32[1]{0:T(128)S(6)} %copy.17.count, bf16[32,16,128]{2,1,0:T(8,128)(2,1)S(1)} %get-tuple-element.52.moments, bf16[16,32,128]{2,1,0:T(8,128)(2,1)S(1)} %collective-permute-done.2.first, bf16[16,32,128]{2,1,0:T(8,128)(2,1)S(1)} %collective-permute-done.3.second), custom_call_target="tpu_custom_call" | custom-call | bytes 3145728 | tf_op jit(solution)/shard_map/spread/pallas_call | solution.py:474
  17.6 0.0 collective-permute-done.4
  17.7 0.1 fusion.1
  17.8 0.0 collective-permute-start.5
  17.8 0.0 slice-done
  17.8 0.0 copy-done.3
  17.8 0.0 copy-done.4
  17.8 0.0 slice-done.1
  17.8 0.0 copy-start
  17.8 0.0 copy-start.1
  17.9 0.0 copy-start.2
  17.9 0.0 copy-start.5
  17.9 2.5 %near.1 = (f32[32,16,128]{2,1,0:T(8,128)S(1)}, f32[2528,128]{1,0:T(8,128)S(1)}) custom-call(s32[160]{0:T(256)S(1)} %copy-done.3, s32[160]{0:T(256)S(1)} %copy-done.4, s32[16,128]{1,0:T(8,128)S(1)} %get-tuple-element.58.count, bf16[32,16,128]{2,1,0:T(8,128)(2,1)S(1)} %get-tuple-element.59.charges, bf16[16,32,128]{2,1,0:T(8,128)(2,1)S(1)} %collective-permute-done.2.first, ...), custom_call_target="tpu_custom_call" | custom-call | bytes 9437184 | tf_op jit(solution)/shard_map/near/pallas_call | solution.py:490
  20.4 0.0 copy-start.6
  20.4 1.2 %collective-permute-done.5 = f32[3,16,128]{2,1,0:T(8,128)S(1)} collective-permute-done((f32[3,16,128]{2,1,0:T(8,128)S(1)}, f32[3,16,128]{2,1,0:T(8,128)S(1)}, u32[]{:S(2)}, u32[]{:S(2)}) %collective-permute-start.5) | collective-permute-done | bytes 24608 | tf_op jit(solution)/shard_map/ppermute | solution.py:353
  21.6 0.1 fusion.3
  21.7 0.1 pad_maximum_fusion.4
  21.8 0.6 %collective-permute-start.6 = (f32[4,16,128]{2,1,0:T(8,128)S(1)}, f32[4,16,128]{2,1,0:T(8,128)S(1)}, u32[]{:S(2)}, u32[]{:S(2)}) collective-permute-start(f32[4,16,128]{2,1,0:T(8,128)S(1)} %pad_maximum_fusion.4), channel_id=1, source_target_pairs={{0,4},{1,5},{2,6},{3,7},{4,0},{5,1},{6,2},{7,3},{8,12},{9,13},{10,... | collective-permute-start | bytes 98312 | tf_op jit(solution)/shard_map/ppermute | solution.py:353
  22.4 0.0 copy-done
  22.4 0.0 copy-done.1
  22.4 0.0 copy-done.2
  22.4 0.0 copy-done.5
  22.4 3.0 %far.1 = (f32[16,16,128]{2,1,0:T(8,128)S(1)}, f32[224,128]{1,0:T(8,128)S(1)}, bf16[2,64,512]{2,1,0:T(8,128)(2,1)S(1)}) custom-call(s32[16,32]{1,0:T(8,128)S(1)} %bitcast.18, s32[16,32]{1,0:T(8,128)S(1)} %bitcast.19, s32[1,4]{1,0:T(1,128)S(1)} %copy-done.5, s32[4,4]{1,0:T(4,128)S(1)} %copy-done.2, bf16[64,64,128]{2,1,0:T(8,128)(2,1)S(1)} %get-tuple-element.66.spread, ...), custom_call_target="tpu_custom_call" | custom-call | bytes 9437184 | tf_op jit(solution)/shard_map/far/pallas_call | solution.py:526
  25.4 1.2 %collective-permute-done.6 = f32[4,16,128]{2,1,0:T(8,128)S(1)} collective-permute-done((f32[4,16,128]{2,1,0:T(8,128)S(1)}, f32[4,16,128]{2,1,0:T(8,128)S(1)}, u32[]{:S(2)}, u32[]{:S(2)}) %collective-permute-start.6) | collective-permute-done | bytes 32800 | tf_op jit(solution)/shard_map/ppermute | solution.py:353
  26.6 0.1 slice_add_fusion
  26.7 0.0 copy-done.6
  26.7 2.2 %final.1 = f32[32,16,128]{2,1,0:T(8,128)} custom-call(s32[32]{0:T(128)S(1)} %get-tuple-element.41.leaf_trans, s32[8]{0:T(128)S(1)} %get-tuple-element.42.dev_trans, s32[1,4]{1,0:T(1,128)S(1)} %copy-done.6, f32[32,16,128]{2,1,0:T(8,128)S(1)} %get-tuple-element.65.near, f32[16,16,128]{2,1,0:T(8,128)S(1)} %get-tuple-element.70.far, ...), custom_call_target="tpu_custom_call" | custom-call | tf_op jit(solution)/shard_map/final/pallas_call | solution.py:542
  (8 shorter events, 0.0 us)
Async XLA Ops:
  0.7 17.1 %slice-start = ((s8[5242880]{0:T(1024)(128)(4,1)}), s8[4194304]{0:T(1024)(128)(4,1)S(1)}, s32[]{:S(2)}) async-start(s8[5242880]{0:T(1024)(128)(4,1)} %bitcast.14), calls=%async_computation | async-start | bytes 8388608
  3.3 14.5 %copy-start.3 = (s32[160]{0:T(256)S(1)}, s32[160]{0:T(256)}, u32[]{:S(2)}) copy-start(s32[160]{0:T(256)} %targets.1) | copy-start | bytes 1924
  3.3 14.5 %copy-start.4 = (s32[160]{0:T(256)S(1)}, s32[160]{0:T(256)}, u32[]{:S(2)}) copy-start(s32[160]{0:T(256)} %sources.1) | copy-start | bytes 1924
  3.3 7.9 %collective-permute-start = (f32[16,128]{1,0:T(8,128)S(1)}, f32[16,128]{1,0:T(8,128)S(1)}, u32[]{:S(2)}, u32[]{:S(2)}) collective-permute-start(f32[16,128]{1,0:T(8,128)S(1)} %get-tuple-element.43), channel_id=1, source_target_pairs={{0,1},{1,0},{2,3},{3,2},{4,5},{5,4},{6,7},{7,6},{8,9},{9,8},{10,11... | collective-permute-start | bytes 24584 | tf_op jit(solution)/shard_map/ppermute | solution.py:353
  6.3 9.1 %collective-permute-start.2 = (bf16[16,32,128]{2,1,0:T(8,128)(2,1)S(1)}, bf16[16,32,128]{2,1,0:T(8,128)(2,1)S(1)}, u32[]{:S(2)}, u32[]{:S(2)}) collective-permute-start(bf16[16,32,128]{2,1,0:T(8,128)(2,1)S(1)} %get-tuple-element.49), channel_id=1, source_target_pairs={{0,1},{1,0},{2,3},{3,2},{4,5},{5,4},{6,7},{7,6},{8,9},{9,8},{10,11... | collective-permute-start | bytes 393224 | tf_op jit(solution)/shard_map/ppermute | solution.py:353
  6.4 9.1 %collective-permute-start.3 = (bf16[16,32,128]{2,1,0:T(8,128)(2,1)S(1)}, bf16[16,32,128]{2,1,0:T(8,128)(2,1)S(1)}, u32[]{:S(2)}, u32[]{:S(2)}) collective-permute-start(bf16[16,32,128]{2,1,0:T(8,128)(2,1)S(1)} %get-tuple-element.50), channel_id=1, source_target_pairs={{1,2},{3,4},{5,6},{7,8},{9,10},{11,12},{13,14},{15,16},{17,18},{19... | collective-permute-start | bytes 393224 | tf_op jit(solution)/shard_map/ppermute | solution.py:446
  11.3 6.5 %slice-start.1 = ((s8[5242880]{0:T(1024)(128)(4,1)}), s8[1048576]{0:T(1024)(128)(4,1)S(1)}, s32[]{:S(2)}) async-start(s8[5242880]{0:T(1024)(128)(4,1)} %bitcast.14), calls=%async_computation.1 | async-start | bytes 2097152
  11.3 4.1 %collective-permute-start.1 = (f32[1,16,64]{2,1,0:T(8,128)S(1)}, f32[1,16,64]{2,1,0:T(8,128)S(1)}, u32[]{:S(2)}, u32[]{:S(2)}) collective-permute-start(f32[1,16,64]{2,1,0:T(8,128)S(1)} %get-tuple-element.46), channel_id=1, source_target_pairs={{0,16},{8,24},{16,0},{24,8},{1,17},{9,25},{17,1},{25,9},{2,18},{10... | collective-permute-start | bytes 12296 | tf_op jit(solution)/shard_map/ppermute | solution.py:353
  15.5 2.2 %collective-permute-start.4 = (f32[2,16,64]{2,1,0:T(8,128)S(1)}, f32[2,16,64]{2,1,0:T(8,128)S(1)}, u32[]{:S(2)}, u32[]{:S(2)}) collective-permute-start(f32[2,16,64]{2,1,0:T(8,128)S(1)} %pad_maximum_fusion.7), channel_id=1, source_target_pairs={{0,8},{8,0},{16,24},{24,16},{1,9},{9,1},{17,25},{25,17},{2,10},{10... | collective-permute-start | bytes 24584 | tf_op jit(solution)/shard_map/ppermute | solution.py:353
  17.8 3.8 %collective-permute-start.5 = (f32[3,16,128]{2,1,0:T(8,128)S(1)}, f32[3,16,128]{2,1,0:T(8,128)S(1)}, u32[]{:S(2)}, u32[]{:S(2)}) collective-permute-start(f32[3,16,128]{2,1,0:T(8,128)S(1)} %fusion.1), channel_id=1, source_target_pairs={{0,2},{1,3},{2,0},{3,1},{4,6},{5,7},{6,4},{7,5},{8,10},{9,11},{10,... | collective-permute-start | bytes 73736 | tf_op jit(solution)/shard_map/ppermute | solution.py:353
  17.8 4.6 %copy-start = (s32[32,16]{0,1:T(8,128)S(1)}, s32[32,16]{0,1:T(8,128)}, u32[]{:S(2)}) copy-start(s32[32,16]{0,1:T(8,128)} %param.22) | copy-start | bytes 6148
  17.8 4.6 %copy-start.1 = (s32[32,16]{0,1:T(8,128)S(1)}, s32[32,16]{0,1:T(8,128)}, u32[]{:S(2)}) copy-start(s32[32,16]{0,1:T(8,128)} %param.23) | copy-start | bytes 6148
  17.9 4.5 %copy-start.2 = (s32[4,4]{1,0:T(4,128)S(1)}, s32[4,4]{1,0:T(4,128)}, u32[]{:S(2)}) copy-start(s32[4,4]{1,0:T(4,128)} %grp_couple.1) | copy-start | bytes 196
  17.9 4.5 %copy-start.5 = (s32[1,4]{1,0:T(1,128)S(1)}, s32[1,4]{1,0:T(1,128)}, u32[]{:S(2)}) copy-start(s32[1,4]{1,0:T(1,128)} %dev_couple.1) | copy-start | bytes 52
  20.4 6.3 %copy-start.6 = (s32[1,4]{1,0:T(1,128)S(1)}, s32[1,4]{1,0:T(1,128)}, u32[]{:S(2)}) copy-start(s32[1,4]{1,0:T(1,128)} %dev_list.1) | copy-start | bytes 52
  21.8 4.8 %collective-permute-start.6 = (f32[4,16,128]{2,1,0:T(8,128)S(1)}, f32[4,16,128]{2,1,0:T(8,128)S(1)}, u32[]{:S(2)}, u32[]{:S(2)}) collective-permute-start(f32[4,16,128]{2,1,0:T(8,128)S(1)} %pad_maximum_fusion.4), channel_id=1, source_target_pairs={{0,4},{1,5},{2,6},{3,7},{4,0},{5,1},{6,2},{7,3},{8,12},{9,13},{10,... | collective-permute-start | bytes 98312 | tf_op jit(solution)/shard_map/ppermute | solution.py:353
